TPU v7x, 128 devices: a whole 4x4x4 slice. The times are simulated.
128 devices in a mesh: ta: 8 (over x, core), ha: 16 (over y, z).
Axes of the slice: x: 4, y: 4, z: 4, core: 2. Of those that a mesh axis runs over, the one named last changes fastest.
Arguments:
- activations: bfloat16 [16, 32, 160, 512], P('ta', 'ha'), may hold values from -96 to 96
- gain: float32 [512], replicated, may hold values from 0.1 to 1.9
- shift: float32 [512], replicated, may hold values from -3 to 3
- weight: bfloat16 [3, 3, 3, 512, 512], replicated, may hold values from -0.0546875 to 0.0546875
- cotangent: bfloat16 [16, 32, 160, 512], P('ta', 'ha'), may hold values from -8 to 8
Outputs:
- output: bfloat16 [16, 32, 160, 512], P('ta', 'ha')
- input_grad: bfloat16 [16, 32, 160, 512], P('ta', 'ha')
All inputs are finite; a program needn't handle non-finite values.
Results may differ from a plain program's by a relative error of at most 0.0049.
Values may be sent and summed in bfloat16 or wider, within the bound.
No kernel may reach another device: no remote copies, remote signals or barrier semaphores. Data moves between devices by JAX's collectives and lax.ppermute only.
A program may use at most 128 MiB of HBM per device.

v0:
```python
import jax
import jax.numpy as jnp
from jax import lax
from jax.sharding import PartitionSpec as P

GROUPS = 32


def shifted(value, axis, steps):
    count = lax.axis_size(axis)
    first, last = (max(0, -steps), min(count, count - steps))
    return lax.ppermute(value, axis, [(source, source + steps) for source in range(first, last)])


def extended_2(value, sides, width):
    for axis, dim in sides:
        peers, length = (lax.axis_size(axis), value.shape[dim])
        up = [(i, (i + 1) % peers) for i in range(peers - 1)]
        down = [(j, i) for i, j in up]
        last = lax.slice_in_dim(value, length - width, length, axis=dim)
        first = lax.slice_in_dim(value, 0, width, axis=dim)
        before = lax.ppermute(last, axis, up)
        after = lax.ppermute(first, axis, down)
        value = jnp.concatenate([before, value, after], axis=dim)
    return value


def group_sum(values, groups):
    per_channel = jnp.sum(values.reshape(-1, values.shape[-1]), axis=0)
    return jnp.sum(per_channel.reshape(groups, -1), axis=1)


def on_device(activations, gain, shift, weight, cotangent):
    frames, rows, cols, chans = activations.shape
    per_group = chans // GROUPS
    count = lax.axis_size("ta") * frames * lax.axis_size("ha") * rows * cols * per_group
    xf = activations.astype(jnp.float32)
    mean = lax.psum(group_sum(xf, GROUPS), ("ta", "ha")) / count
    centered = xf - jnp.repeat(mean, per_group)
    var = lax.psum(group_sum(centered * centered, GROUPS), ("ta", "ha")) / count
    mean_c = jnp.repeat(mean, per_group)
    rstd_c = jnp.repeat(lax.rsqrt(var + 1e-06), per_group)
    first_frames = lax.axis_index("ta") == 0
    normal_part = (activations.astype(jnp.float32) - mean_c) * rstd_c
    extend_block = jax.nn.silu(normal_part * gain + shift).astype(jnp.bfloat16)
    prior = shifted(extend_block, "ta", 1)
    repeated = jnp.broadcast_to(extend_block[:1], prior.shape)
    prior = jnp.where(first_frames, repeated, prior)
    longer = jnp.concatenate([prior, extend_block], axis=0)
    extended = extended_2(longer, (("ha", 1),), 1)
    widened = jnp.pad(extended, ((0, 0), (0, 0), (1, 1), (0, 0)))
    total = jnp.zeros((frames, rows, cols, chans), jnp.float32)
    for a in range(3):
        for b in range(3):
            block = widened[a : a + frames, b : b + rows]
            stacked = jnp.concatenate([block[:, :, c : c + cols] for c in range(3)], axis=-1)
            kernel = weight[a, b].reshape(3 * chans, chans)
            total = total + jnp.einsum(
                "thwk,ko->thwo", stacked, kernel, preferred_element_type=jnp.float32
            )
    output = total.astype(jnp.bfloat16)
    padded_grad = jnp.zeros((frames + 2, rows + 2, cols + 2, chans), jnp.float32)
    for a in range(3):
        for b in range(3):
            terms = jnp.einsum(
                "thwo,dio->thwdi", cotangent, weight[a, b], preferred_element_type=jnp.float32
            )
            for c in range(3):
                padded_grad = padded_grad.at[a : a + frames, b : b + rows, c : c + cols].add(
                    terms[:, :, :, c]
                )
    grad_ext = padded_grad[:, :, 1:-1]
    incoming = shifted(grad_ext[:2], "ta", -1)
    own_frames = grad_ext[2:] + incoming
    local_first = jnp.where(first_frames, grad_ext[0] + grad_ext[1], 0.0)
    own_frames = own_frames.at[0].add(local_first)
    from_later = shifted(own_frames[:, :1], "ha", -1)
    from_earlier = shifted(own_frames[:, -1:], "ha", 1)
    acts_grad = own_frames[:, 1:-1]
    acts_grad = acts_grad.at[:, -1:].add(from_later)
    acts_grad = acts_grad.at[:, :1].add(from_earlier)
    normed = (xf - mean_c) * rstd_c
    pre = normed * gain + shift
    sig = jax.nn.sigmoid(pre)
    pre_grad = acts_grad * sig * (1.0 + pre * (1.0 - sig))
    shift_sum, gain_sum = lax.psum(
        (
            jnp.sum(pre_grad.reshape(-1, chans), axis=0),
            jnp.sum((pre_grad * normed).reshape(-1, chans), axis=0),
        ),
        ("ta", "ha"),
    )
    first = jnp.repeat(jnp.sum((gain * shift_sum).reshape(GROUPS, -1), axis=1) / count, per_group)
    second = jnp.repeat(jnp.sum((gain * gain_sum).reshape(GROUPS, -1), axis=1) / count, per_group)
    input_grad = (rstd_c * (pre_grad * gain - first - normed * second)).astype(jnp.bfloat16)
    return (output, input_grad)


def solution(mesh):
    placed = (P("ta", "ha", None, None), P(), P(), P(), P("ta", "ha", None, None))
    return jax.shard_map(
        on_device,
        mesh=mesh,
        in_specs=placed,
        out_specs=(P("ta", "ha", None, None), P("ta", "ha", None, None)),
        check_vma=False,
    )
```

profile of v0, /device:TPU:1, one launch (start us, length us, event | category | flops | bytes accessed | tf_op | source)
XLA Modules:
  0.0 525.9 jit_solution(9192114921103517160)
XLA Ops:
  4.5 6.7 %fusion.73 = f32[2,2,160,3,512]{4,2,1,0,3:T(8,128)} fusion(bf16[2,2,160,512]{3,2,1,0:T(8,128)(2,1)S(1)} %copy-done, bf16[3,3,3,512,512]{4,3,2,1,0:T(8,128)(2,1)} %param.68), kind=kOutput, calls=%fused_computation.83 | convolution fusion | flops 1006632960 | bytes 6160384 | tf_op jit(solution)/shard_map/thwo,dio->thwdi/dot_general | solution.py:65
  11.2 4.5 fusion.71
  28.2 3.2 fusion.61
  38.1 5.8 %scatter-add.101 = f32[4,4,162,512]{3,2,1,0:T(8,128)} dynamic-update-slice(f32[4,4,162,512]{3,2,1,0:T(8,128)} %scatter-add.100, f32[2,2,160,512]{3,2,1,0:T(8,128)S(1)} %fusion.124, s32[]{:T(128)} %constant.972.clone.1, s32[]{:T(128)} %constant.972.clone.1, s32[]{:T(128)} %constant.978.clone.1, s32[]{:T(128)} %constant.972.clone.1) | dynamic-update-slice | bytes 2621444 | tf_op jit(solution)/shard_map/scatter-add | solution.py:69
  46.0 5.7 %scatter-add.104 = f32[4,4,162,512]{3,2,1,0:T(8,128)} dynamic-update-slice(f32[4,4,162,512]{3,2,1,0:T(8,128)} %scatter-add.101, f32[2,2,160,512]{3,2,1,0:T(8,128)S(1)} %fusion.160, s32[]{:T(128)} %constant.972.clone.1, s32[]{:T(128)} %constant.972.clone.1, s32[]{:T(128)} %constant.979.clone.1, s32[]{:T(128)} %constant.972.clone.1) | dynamic-update-slice | bytes 2621444 | tf_op jit(solution)/shard_map/scatter-add | solution.py:69
  56.8 5.7 %scatter-add.106 = f32[4,4,162,512]{3,2,1,0:T(8,128)} dynamic-update-slice(f32[4,4,162,512]{3,2,1,0:T(8,128)} %fusion.159, f32[2,2,160,512]{3,2,1,0:T(8,128)S(1)} %fusion.157, s32[]{:T(128)} %constant.972.clone.1, s32[]{:T(128)} %constant.978.clone.1, s32[]{:T(128)} %constant.978.clone.1, s32[]{:T(128)} %constant.972.clone.1) | dynamic-update-slice | bytes 2621444 | tf_op jit(solution)/shard_map/scatter-add | solution.py:69
  63.2 4.0 fusion.156
  67.1 7.6 %scatter-add.109 = f32[4,4,162,512]{3,2,1,0:T(8,128)} dynamic-update-slice(f32[4,4,162,512]{3,2,1,0:T(8,128)} %scatter-add.106, f32[2,2,160,512]{3,2,1,0:T(8,128)S(1)} %fusion.156, s32[]{:T(128)} %bitcast.40, s32[]{:T(128)} %bitcast.41, s32[]{:T(128)} %bitcast.42, s32[]{:T(128)} %constant.972.clone.1) | dynamic-update-slice | bytes 2621444 | tf_op jit(solution)/shard_map/scatter-add | solution.py:69
  79.9 5.8 %scatter-add.111 = f32[4,4,162,512]{3,2,1,0:T(8,128)} dynamic-update-slice(f32[4,4,162,512]{3,2,1,0:T(8,128)} %fusion.155, f32[2,2,160,512]{3,2,1,0:T(8,128)S(1)} %fusion.153, s32[]{:T(128)} %constant.972.clone.1, s32[]{:T(128)} %constant.979.clone.1, s32[]{:T(128)} %constant.978.clone.1, s32[]{:T(128)} %constant.972.clone.1) | dynamic-update-slice | bytes 2621444 | tf_op jit(solution)/shard_map/scatter-add | solution.py:69
  87.7 5.8 %scatter-add.114 = f32[4,4,162,512]{3,2,1,0:T(8,128)} dynamic-update-slice(f32[4,4,162,512]{3,2,1,0:T(8,128)} %scatter-add.111, f32[2,2,160,512]{3,2,1,0:T(8,128)S(1)} %fusion.152, s32[]{:T(128)} %constant.972.clone.1, s32[]{:T(128)} %constant.979.clone.1, s32[]{:T(128)} %constant.979.clone.1, s32[]{:T(128)} %constant.972.clone.1) | dynamic-update-slice | bytes 2621444 | tf_op jit(solution)/shard_map/scatter-add | solution.py:69
  98.6 5.7 %scatter-add.116 = f32[4,4,162,512]{3,2,1,0:T(8,128)} dynamic-update-slice(f32[4,4,162,512]{3,2,1,0:T(8,128)} %fusion.151, f32[2,2,160,512]{3,2,1,0:T(8,128)S(1)} %fusion.149, s32[]{:T(128)} %constant.978.clone.1, s32[]{:T(128)} %constant.972.clone.1, s32[]{:T(128)} %constant.978.clone.1, s32[]{:T(128)} %constant.972.clone.1) | dynamic-update-slice | bytes 2621444 | tf_op jit(solution)/shard_map/scatter-add | solution.py:69
  106.4 5.7 %scatter-add.119 = f32[4,4,162,512]{3,2,1,0:T(8,128)} dynamic-update-slice(f32[4,4,162,512]{3,2,1,0:T(8,128)} %scatter-add.116, f32[2,2,160,512]{3,2,1,0:T(8,128)S(1)} %fusion.148, s32[]{:T(128)} %constant.978.clone.1, s32[]{:T(128)} %constant.972.clone.1, s32[]{:T(128)} %constant.979.clone.1, s32[]{:T(128)} %constant.972.clone.1) | dynamic-update-slice | bytes 2621444 | tf_op jit(solution)/shard_map/scatter-add | solution.py:69
  117.2 5.7 %scatter-add.121 = f32[4,4,162,512]{3,2,1,0:T(8,128)} dynamic-update-slice(f32[4,4,162,512]{3,2,1,0:T(8,128)} %fusion.147, f32[2,2,160,512]{3,2,1,0:T(8,128)S(1)} %fusion.145, s32[]{:T(128)} %constant.978.clone.1, s32[]{:T(128)} %constant.978.clone.1, s32[]{:T(128)} %constant.978.clone.1, s32[]{:T(128)} %constant.972.clone.1) | dynamic-update-slice | bytes 2621444 | tf_op jit(solution)/shard_map/scatter-add | solution.py:69
  125.0 5.7 %scatter-add.124 = f32[4,4,162,512]{3,2,1,0:T(8,128)} dynamic-update-slice(f32[4,4,162,512]{3,2,1,0:T(8,128)} %scatter-add.121, f32[2,2,160,512]{3,2,1,0:T(8,128)S(1)} %fusion.144, s32[]{:T(128)} %constant.978.clone.1, s32[]{:T(128)} %constant.978.clone.1, s32[]{:T(128)} %constant.979.clone.1, s32[]{:T(128)} %constant.972.clone.1) | dynamic-update-slice | bytes 2621444 | tf_op jit(solution)/shard_map/scatter-add | solution.py:69
  135.8 5.7 %scatter-add.126 = f32[4,4,162,512]{3,2,1,0:T(8,128)} dynamic-update-slice(f32[4,4,162,512]{3,2,1,0:T(8,128)} %fusion.143, f32[2,2,160,512]{3,2,1,0:T(8,128)S(1)} %fusion.141, s32[]{:T(128)} %constant.978.clone.1, s32[]{:T(128)} %constant.979.clone.1, s32[]{:T(128)} %constant.978.clone.1, s32[]{:T(128)} %constant.972.clone.1) | dynamic-update-slice | bytes 2621444 | tf_op jit(solution)/shard_map/scatter-add | solution.py:69
  143.6 5.7 %scatter-add.129 = f32[4,4,162,512]{3,2,1,0:T(8,128)} dynamic-update-slice(f32[4,4,162,512]{3,2,1,0:T(8,128)} %scatter-add.126, f32[2,2,160,512]{3,2,1,0:T(8,128)S(1)} %fusion.140, s32[]{:T(128)} %constant.978.clone.1, s32[]{:T(128)} %constant.979.clone.1, s32[]{:T(128)} %constant.979.clone.1, s32[]{:T(128)} %constant.972.clone.1) | dynamic-update-slice | bytes 2621444 | tf_op jit(solution)/shard_map/scatter-add | solution.py:69
  154.5 5.7 %scatter-add.131 = f32[4,4,162,512]{3,2,1,0:T(8,128)} dynamic-update-slice(f32[4,4,162,512]{3,2,1,0:T(8,128)} %fusion.139, f32[2,2,160,512]{3,2,1,0:T(8,128)S(1)} %fusion.137, s32[]{:T(128)} %constant.979.clone.1, s32[]{:T(128)} %constant.972.clone.1, s32[]{:T(128)} %constant.978.clone.1, s32[]{:T(128)} %constant.972.clone.1) | dynamic-update-slice | bytes 2621444 | tf_op jit(solution)/shard_map/scatter-add | solution.py:69
  162.2 5.7 %scatter-add.134 = f32[4,4,162,512]{3,2,1,0:T(8,128)} dynamic-update-slice(f32[4,4,162,512]{3,2,1,0:T(8,128)} %scatter-add.131, f32[2,2,160,512]{3,2,1,0:T(8,128)S(1)} %fusion.136, s32[]{:T(128)} %constant.979.clone.1, s32[]{:T(128)} %constant.972.clone.1, s32[]{:T(128)} %constant.979.clone.1, s32[]{:T(128)} %constant.972.clone.1) | dynamic-update-slice | bytes 2621444 | tf_op jit(solution)/shard_map/scatter-add | solution.py:69
  173.1 5.7 %scatter-add.136 = f32[4,4,162,512]{3,2,1,0:T(8,128)} dynamic-update-slice(f32[4,4,162,512]{3,2,1,0:T(8,128)} %fusion.135, f32[2,2,160,512]{3,2,1,0:T(8,128)S(1)} %fusion.133, s32[]{:T(128)} %constant.979.clone.1, s32[]{:T(128)} %constant.978.clone.1, s32[]{:T(128)} %constant.978.clone.1, s32[]{:T(128)} %constant.972.clone.1) | dynamic-update-slice | bytes 2621444 | tf_op jit(solution)/shard_map/scatter-add | solution.py:69
  180.8 5.7 %scatter-add.139 = f32[4,4,162,512]{3,2,1,0:T(8,128)} dynamic-update-slice(f32[4,4,162,512]{3,2,1,0:T(8,128)} %scatter-add.136, f32[2,2,160,512]{3,2,1,0:T(8,128)S(1)} %fusion.132, s32[]{:T(128)} %constant.979.clone.1, s32[]{:T(128)} %constant.978.clone.1, s32[]{:T(128)} %constant.979.clone.1, s32[]{:T(128)} %constant.972.clone.1) | dynamic-update-slice | bytes 2621444 | tf_op jit(solution)/shard_map/scatter-add | solution.py:69
  191.7 5.7 %scatter-add.141 = f32[4,4,162,512]{3,2,1,0:T(8,128)} dynamic-update-slice(f32[4,4,162,512]{3,2,1,0:T(8,128)} %fusion.131, f32[2,2,160,512]{3,2,1,0:T(8,128)S(1)} %fusion.129, s32[]{:T(128)} %constant.979.clone.1, s32[]{:T(128)} %constant.979.clone.1, s32[]{:T(128)} %constant.978.clone.1, s32[]{:T(128)} %constant.972.clone.1) | dynamic-update-slice | bytes 2621444 | tf_op jit(solution)/shard_map/scatter-add | solution.py:69
  199.5 5.7 %scatter-add.144 = f32[4,4,162,512]{3,2,1,0:T(8,128)} dynamic-update-slice(f32[4,4,162,512]{3,2,1,0:T(8,128)} %scatter-add.141, f32[2,2,160,512]{3,2,1,0:T(8,128)S(1)} %fusion.128, s32[]{:T(128)} %constant.979.clone.1, s32[]{:T(128)} %constant.979.clone.1, s32[]{:T(128)} %constant.979.clone.1, s32[]{:T(128)} %constant.972.clone.1) | dynamic-update-slice | bytes 2621444 | tf_op jit(solution)/shard_map/scatter-add | solution.py:69
  207.5 3.5 collective-permute-start.3
  211.1 30.4 %collective-permute-done.3 = f32[2,4,160,512]{3,2,1,0:T(8,128)} collective-permute-done((f32[2,4,160,512]{3,2,1,0:T(8,128)S(1)}, f32[2,4,160,512]{3,2,1,0:T(8,128)}, u32[]{:S(2)}, u32[]{:S(2)}) %collective-permute-start.3) | collective-permute-done | bytes 2621472 | tf_op jit(solution)/shard_map/ppermute | solution.py:12
  241.5 3.3 slice_add_fusion
  250.0 75.2 %psum.28 = f32[32]{0:T(128)S(1)} all-reduce(f32[32]{0:T(128)S(1)} %reduce_sum.73), channel_id=1, replica_groups=mesh['ta'=8,'ha'=16] {'ta','ha'}, use_global_device_ids=true, to_apply=%region_2.0 | all-reduce | flops 32 | bytes 256 | tf_op jit(solution)/shard_map/psum | solution.py:38
  328.4 69.6 %psum.29 = f32[32]{0:T(128)S(1)} all-reduce(f32[32]{0:T(128)S(1)} %reduce_sum.75), channel_id=1, replica_groups=mesh['ta'=8,'ha'=16] {'ta','ha'}, use_global_device_ids=true, to_apply=%region_5.0 | all-reduce | flops 32 | bytes 256 | tf_op jit(solution)/shard_map/psum | solution.py:40
  405.8 9.4 %fusion.194 = (bf16[1,1,3,512,512]{4,3,2,1,0:T(8,128)(2,1)S(1)}, bf16[1,1,3,512,512]{4,3,2,1,0:T(8,128)(2,1)}, bf16[1,1,3,512,512]{4,3,2,1,0:T(8,128)(2,1)}, bf1...) fusion(bf16[3,3,3,512,512]{4,3,2,1,0:T(8,128)(2,1)} %param.68), kind=kLoop, calls=%fused_computation.225 | loop fusion | bytes 28311552 | tf_op jit(solution)/shard_map/slice | solution.py:57
  415.1 63.5 %all-reduce.2 = (f32[512]{0:T(512)S(1)}, f32[512]{0:T(512)S(1)}) all-reduce(f32[512]{0:T(512)S(1)} %get-tuple-element.363, f32[512]{0:T(512)S(1)} %get-tuple-element.362), channel_id=1, replica_groups=mesh['ta'=8,'ha'=16] {'ta','ha'}, use_global_device_ids=true, to_apply=%region_10.11 | all-reduce | flops 1024 | bytes 8192 | tf_op jit(solution)/shard_map/psum | solution.py:86
  491.8 6.5 %collective-permute-done.1 = bf16[4,1,160,512]{3,2,1,0:T(8,128)(2,1)} collective-permute-done((bf16[4,1,160,512]{3,2,1,0:T(8,128)(2,1)}, bf16[4,1,160,512]{3,2,1,0:T(8,128)(2,1)}, u32[]{:S(2)}, u32[]{:S(2)}) %collective-permute-start.1) | collective-permute-done | bytes 655392 | tf_op jit(solution)/shard_map/ppermute | solution.py:22
  498.2 4.7 collective-permute-done.2
  505.2 3.7 fusion.195
  (127 shorter events, 131.2 us)
Async XLA Ops:
  0.6 1.1 copy-start
  1.7 13.9 %copy-start.2 = (bf16[3,3,3,512,512]{4,3,2,1,0:T(8,128)(2,1)S(1)}, bf16[3,3,3,512,512]{4,3,2,1,0:T(8,128)(2,1)}, u32[]{:S(2)}) copy-start(bf16[3,3,3,512,512]{4,3,2,1,0:T(8,128)(2,1)} %param.68) | copy-start | bytes 42467332
  4.5 30.2 %copy-start.3 = (f32[2,2,160,3,512]{4,2,1,0,3:T(8,128)}, f32[2,2,160,3,512]{4,2,1,0,3:T(8,128)S(1)}, u32[]{:S(2)}) copy-start(f32[2,2,160,3,512]{4,2,1,0,3:T(8,128)S(1)} %fusion.75) | copy-start | bytes 11796484
  207.5 33.9 %collective-permute-start.3 = (f32[2,4,160,512]{3,2,1,0:T(8,128)S(1)}, f32[2,4,160,512]{3,2,1,0:T(8,128)}, u32[]{:S(2)}, u32[]{:S(2)}) collective-permute-start(f32[2,4,160,512]{3,2,1,0:T(8,128)S(1)} %slice.1639), channel_id=1, source_target_pairs={{16,0},{32,16},{48,32},{64,48},{80,64},{96,80},{112,96},{17,1},{33... | collective-permute-start | bytes 7864328 | tf_op jit(solution)/shard_map/ppermute | solution.py:12
  247.2 2.4 copy-start.4
  248.4 150.0 %collective-permute-start.4 = (f32[2,1,160,512]{3,2,1,0:T(8,128)}, f32[2,1,160,512]{3,2,1,0:T(8,128)}, u32[]{:S(2)}, u32[]{:S(2)}) collective-permute-start(f32[2,1,160,512]{3,2,1,0:T(8,128)} %get-tuple-element.395), channel_id=1, source_target_pairs={{1,0},{2,1},{3,2},{4,3},{5,4},{6,5},{7,6},{8,7},{9,8},{10,9},{11,1... | collective-permute-start | bytes 1966088 | tf_op jit(solution)/shard_map/ppermute | solution.py:12
  325.3 75.5 %copy-start.15 = (f32[512]{0:T(512)}, f32[512]{0:T(512)S(1)}, u32[]{:S(2)}) copy-start(f32[512]{0:T(512)S(1)} %sub.16) | copy-start | bytes 6148
  325.3 74.3 %collective-permute-start.5 = (f32[2,1,160,512]{3,2,1,0:T(8,128)}, f32[2,1,160,512]{3,2,1,0:T(8,128)}, u32[]{:S(2)}, u32[]{:S(2)}) collective-permute-start(f32[2,1,160,512]{3,2,1,0:T(8,128)} %get-tuple-element.394), channel_id=1, source_target_pairs={{0,1},{1,2},{2,3},{3,4},{4,5},{5,6},{6,7},{7,8},{8,9},{9,10},{10,1... | collective-permute-start | bytes 1966088 | tf_op jit(solution)/shard_map/ppermute | solution.py:12
  398.2 2.7 copy-start.17
  398.3 2.6 copy-start.5
  398.3 2.6 copy-start.16
  398.3 2.6 copy-start.18
  402.9 76.6 %collective-permute-start = (bf16[2,2,160,512]{3,2,1,0:T(8,128)(2,1)S(1)}, bf16[2,2,160,512]{3,2,1,0:T(8,128)(2,1)}, u32[]{:S(2)}, u32[]{:S(2)}) collective-permute-start(bf16[2,2,160,512]{3,2,1,0:T(8,128)(2,1)S(1)} %get-tuple-element.406), channel_id=1, source_target_pairs={{0,16},{16,32},{32,48},{48,64},{64,80},{80,96},{96,112},{1,17},{17... | collective-permute-start | bytes 1966088 | tf_op jit(solution)/shard_map/ppermute | solution.py:12
  479.4 9.8 %copy-start.6 = (bf16[2,2,160,512]{3,2,1,0:T(8,128)(2,1)S(1)}, bf16[2,2,160,512]{3,2,1,0:T(8,128)(2,1)}, u32[]{:S(2)}) copy-start(bf16[2,2,160,512]{3,2,1,0:T(8,128)(2,1)} %param.65) | copy-start | bytes 1966084
  481.8 16.4 %collective-permute-start.1 = (bf16[4,1,160,512]{3,2,1,0:T(8,128)(2,1)}, bf16[4,1,160,512]{3,2,1,0:T(8,128)(2,1)}, u32[]{:S(2)}, u32[]{:S(2)}) collective-permute-start(bf16[4,1,160,512]{3,2,1,0:T(8,128)(2,1)} %get-tuple-element.404), channel_id=1, source_target_pairs={{0,1},{1,2},{2,3},{3,4},{4,5},{5,6},{6,7},{7,8},{8,9},{9,10},{10,1... | collective-permute-start | bytes 1966088 | tf_op jit(solution)/shard_map/ppermute | solution.py:22
  484.2 18.7 %collective-permute-start.2 = (bf16[4,1,160,512]{3,2,1,0:T(8,128)(2,1)}, bf16[4,1,160,512]{3,2,1,0:T(8,128)(2,1)}, u32[]{:S(2)}, u32[]{:S(2)}) collective-permute-start(bf16[4,1,160,512]{3,2,1,0:T(8,128)(2,1)} %get-tuple-element.405), channel_id=1, source_target_pairs={{1,0},{2,1},{3,2},{4,3},{5,4},{6,5},{7,6},{8,7},{9,8},{10,9},{11,1... | collective-permute-start | bytes 1966088 | tf_op jit(solution)/shard_map/ppermute | solution.py:23
  510.4 1.4 copy-start.14
  511.8 1.4 copy-start.13
  513.3 1.4 copy-start.12
  514.7 1.4 copy-start.11
  516.1 1.4 copy-start.10
  517.5 1.4 copy-start.9
  518.9 1.4 copy-start.8
  520.3 1.4 copy-start.7
  522.9 2.6 copy-start.1
where the time goes:
time: 537 us; the launch traced here: 526 us
  blocking collectives  208 us (39%)
  local copies, waits for them, and re-layouts  132 us (25%)
  other arithmetic  83.1 us (15%)
  matrix products  44.8 us (8%)
  waiting for transfers between devices  41.6 us (8%)
  starting transfers between devices  14.3 us (3%)
    scatter-add x19, local copies, waits for them, and re-layouts, on_device(): padded_grad.at[a:a + frames, b:b + rows, c:c + cols].add(terms[:, :, :, c])  108 us
    psum x1, blocking collectives, on_device(): mean = lax.psum(group_sum(xf, GROUPS), ('ta', 'ha')) / count  75.2 us
    psum x1, blocking collectives, on_device(): var = lax.psum(group_sum(centered * centered, GROUPS), ('ta', 'ha')) / count  69.6 us
    psum x1, blocking collectives, on_device(): lax.psum((jnp.sum(pre_grad.reshape(-1, chans), axis=0), jnp.sum((pre_grad...  63.5 us
    add x18, other arithmetic, on_device(): padded_grad.at[a:a + frames, b:b + rows, c:c + cols].add(terms[:, :, :, c])  36.9 us
    dot_general x9, matrix products, on_device(): jnp.einsum('thwo,dio->thwdi', cotangent, weight[a, b], preferred_element_...  32.8 us
    ppermute x4, waiting for transfers between devices, shifted(): lax.ppermute(value, axis, [(source, source + steps) for source in range(f...  30.4 us
    scatter-add x8, other arithmetic, on_device(): padded_grad.at[a:a + frames, b:b + rows, c:c + cols].add(terms[:, :, :, c])  24.6 us
  transfers between devices with their start and end apart: 6, of which 3 were waited for; matrix products, arithmetic and copies ran while one was open for 4% of the time, Pallas kernels for 0%

commit v1 on v0

v1 whole, which is shorter than its diff:
```python
import jax
import jax.numpy as jnp
from jax import lax
from jax.experimental import pallas as pl
from jax.experimental.pallas import tpu as pltpu
from jax.sharding import PartitionSpec as P

GROUPS = 32
LANES = 128
F32 = jnp.float32
BF16 = jnp.bfloat16
ANY = pl.BlockSpec(memory_space=pl.ANY)
WHOLE = pl.BlockSpec(memory_space=pltpu.VMEM)
DMA = pltpu.SemaphoreType.DMA
BOTH = ("ta", "ha")


def params(mebibytes):
    return pltpu.CompilerParams(vmem_limit_bytes=mebibytes * 2**20)


def member(chans, offset, across):
    shape, chan_dim = ((LANES, chans), 1) if across else ((chans, LANES), 0)
    per_group = chans // GROUPS
    chan = lax.broadcasted_iota(jnp.int32, shape, chan_dim)
    lane = lax.broadcasted_iota(jnp.int32, shape, 1 - chan_dim) - offset
    inside = (chan >= lane * per_group) & (chan < (lane + 1) * per_group)
    return jnp.where(inside & (lane >= 0) & (lane < GROUPS), 1.0, 0.0).astype(F32)


def exact_dot(left, right):
    return jnp.dot(left, right, precision=lax.Precision.HIGHEST, preferred_element_type=F32)


def to_groups(by_chan, offset):
    lanes = exact_dot(by_chan, member(by_chan.shape[1], offset, False))
    return jnp.sum(lanes, axis=0, keepdims=True)


def to_chans(by_group, chans, offset):
    rows = jnp.broadcast_to(by_group, (8, LANES))
    return exact_dot(rows, member(chans, offset, True))


def eights(value):
    return value.reshape(value.shape[0] // 8, 8, value.shape[1])


def stats_kernel(act, cot, pay, up, down, block, load_sem, pack_sem):
    frames, rows, cols, chans = block.shape
    load = pltpu.make_async_copy(act, block, load_sem)
    load.start()
    packs = []
    for i, source in enumerate((act, cot)):
        packs.append(pltpu.make_async_copy(source.at[:, rows - 1], up.at[i], pack_sem.at[2 * i]))
        packs.append(pltpu.make_async_copy(source.at[:, 0], down.at[i], pack_sem.at[2 * i + 1]))
    for pack in packs:
        pack.start()
    load.wait()
    entries = frames * rows * cols * (chans // GROUPS)
    total = jnp.zeros((8, chans), F32)
    for t in range(frames):
        for h in range(rows):
            total = total + jnp.sum(eights(block[t, h].astype(F32)), axis=0)
    sums = to_groups(total, 0)
    mean = to_chans(sums / entries, chans, 0)
    spread = jnp.zeros((8, chans), F32)
    for t in range(frames):
        for h in range(rows):
            centered = eights(block[t, h].astype(F32)) - mean[None]
            spread = spread + jnp.sum(centered * centered, axis=0)
    row = sums + to_groups(spread, GROUPS)
    pay[...] = jnp.broadcast_to(row, pay.shape)
    for pack in packs:
        pack.wait()


def grad_kernel(full, part, source, target, pack_act, *refs):
    if pack_act:
        cot, above, below, weight, act, out, longer, ext, taps, acc, ext_sem, tap_sem, act_sem = refs
    else:
        cot, above, below, weight, out, ext, taps, acc, ext_sem, tap_sem = refs
    rows, cols, chans = cot.shape[1:]
    loads = [
        pltpu.make_async_copy(cot, ext.at[:, 1 : rows + 1], ext_sem.at[0]),
        pltpu.make_async_copy(above.at[1], ext.at[:, 0], ext_sem.at[1]),
        pltpu.make_async_copy(below.at[1], ext.at[:, rows + 1], ext_sem.at[2]),
    ]
    for load in loads:
        load.start()
    order = [(k, b) for k in range(2) for b in range(3)]
    fetches = []
    for n, (k, b) in enumerate(order):
        fetches.append(pltpu.make_async_copy(weight.at[(full, part)[k], b], taps.at[n], tap_sem.at[n]))
        fetches[-1].start()
    packs = []
    if pack_act:
        packs = [
            pltpu.make_async_copy(act, longer.at[:, 1 : rows + 1], act_sem.at[0]),
            pltpu.make_async_copy(above.at[0], longer.at[:, 0], act_sem.at[1]),
            pltpu.make_async_copy(below.at[0], longer.at[:, rows + 1], act_sem.at[2]),
        ]
        for pack in packs:
            pack.start()
    for load in loads:
        load.wait()
    half = rows * cols
    for n, (k, b) in enumerate(order):
        fetches[n].wait()
        if k == 0:
            left = ext[:, 2 - b : 2 - b + rows].reshape(2 * half, chans)
            where = slice(0, 2 * half)
        else:
            left = ext[source, 2 - b : 2 - b + rows].reshape(half, chans)
            where = slice(target * half, (target + 1) * half)
        for c in range(3):
            term = lax.dot_general(
                left, taps[n, c], (((1,), (1,)), ((), ())), preferred_element_type=F32
            )
            if n == 0:
                acc[c, where] = term
            else:
                acc[c, where] += term
    combine(acc, out, 2, 0)
    for pack in packs:
        pack.wait()


def combine(acc, out, earlier, later):
    frames, rows, cols, chans = out.shape
    col = lax.broadcasted_iota(jnp.int32, (cols, chans), 0)
    for t in range(frames):
        for h in range(rows):
            at = slice((t * rows + h) * cols, (t * rows + h + 1) * cols)
            before = jnp.where(col == 0, 0.0, pltpu.roll(acc[earlier, at], 1, 0))
            after = jnp.where(col == cols - 1, 0.0, pltpu.roll(acc[later, at], cols - 1, 0))
            out[t, h] = (before + acc[1, at] + after).astype(out.dtype)


def group_stats(gathered, entries, chans):
    parts = gathered.shape[0]
    count = parts * entries
    sums = jnp.sum(gathered, axis=0, keepdims=True)
    mean = sums / count
    apart = gathered * (1.0 / entries) - mean
    between = jnp.sum(apart * apart, axis=0, keepdims=True) * entries
    spread = to_chans(between, chans, 0) + to_chans(sums, chans, GROUPS)
    return to_chans(mean, chans, 0), lax.rsqrt(spread / count + 1e-06)


def point_kernel(own, incoming, early, act, gathered, gain, shift, pre_grad, pay, stats):
    frames, rows, cols, chans = act.shape
    entries = frames * rows * cols * (chans // GROUPS)
    mean, rstd = group_stats(gathered[...], entries, chans)
    stats[0] = mean
    stats[1] = rstd
    first = lax.axis_index("ta") == 0
    scale = jnp.where(first, 1.0, 0.0).astype(F32)
    gains = jnp.broadcast_to(gain[...], (8, chans))
    shifts = jnp.broadcast_to(shift[...], (8, chans))
    shift_sum = jnp.zeros((8, chans), F32)
    gain_sum = jnp.zeros((8, chans), F32)
    for t in range(frames):
        for h in range(rows):
            grad = own[t, h] + incoming[t, h].astype(F32)
            if t == 0:
                grad = grad + scale * (early[0, h].astype(F32) + early[1, h].astype(F32))
            normed = (eights(act[t, h].astype(F32)) - mean[None]) * rstd[None]
            pre = normed * gains[None] + shifts[None]
            sig = 1.0 / (1.0 + jnp.exp(-pre))
            local = eights(grad) * sig * (1.0 + pre * (1.0 - sig))
            pre_grad[t, h] = local.reshape(cols, chans)
            shift_sum = shift_sum + jnp.sum(local, axis=0)
            gain_sum = gain_sum + jnp.sum(local * normed, axis=0)
    row = to_groups(gains * shift_sum, 0) + to_groups(gains * gain_sum, GROUPS)
    pay[...] = jnp.broadcast_to(row, pay.shape)


def conv_kernel(act, above, below, prior, weight, stats, gain, shift, out, raw, ext, taps, acc, raw_sem, tap_sem):
    frames, rows, cols, chans = act.shape
    first = lax.axis_index("ta") == 0
    loads = [
        pltpu.make_async_copy(act, raw.at[2:4, 1 : rows + 1], raw_sem.at[0]),
        pltpu.make_async_copy(above.at[0], raw.at[2:4, 0], raw_sem.at[1]),
        pltpu.make_async_copy(below.at[0], raw.at[2:4, rows + 1], raw_sem.at[2]),
        pltpu.make_async_copy(prior, raw.at[0:2], raw_sem.at[3]),
    ]
    for load in loads:
        load.start()
    order = [(a, b) for a in (2, 1, 0) for b in range(3)]
    fetches = []
    for n, (a, b) in enumerate(order):
        fetches.append(pltpu.make_async_copy(weight.at[a, b], taps.at[n], tap_sem.at[n]))
        fetches[-1].start()
    for load in loads:
        load.wait()
    mean, rstd = stats[0], stats[1]
    gains = jnp.broadcast_to(gain[...], (8, chans))
    shifts = jnp.broadcast_to(shift[...], (8, chans))
    row_at = lax.axis_index("ha")
    last_row = lax.axis_size("ha") - 1

    def activate(t, i):
        normed = (eights(raw[t, i].astype(F32)) - mean[None]) * rstd[None]
        pre = normed * gains[None] + shifts[None]
        value = pre / (1.0 + jnp.exp(-pre))
        if i == 0:
            value = value * jnp.where(row_at == 0, 0.0, 1.0)
        if i == rows + 1:
            value = value * jnp.where(row_at == last_row, 0.0, 1.0)
        ext[t, i] = value.reshape(cols, chans).astype(BF16)

    for t in (2, 3, 0, 1):
        for i in range(rows + 2):
            activate(t, i)

    @pl.when(first)
    def _():
        ext[0] = ext[2]
        ext[1] = ext[2]

    for n, (a, b) in enumerate(order):
        fetches[n].wait()
        left = ext[a : a + frames, b : b + rows].reshape(frames * rows * cols, chans)
        for c in range(3):
            term = jnp.dot(left, taps[n, c], preferred_element_type=F32)
            if n == 0:
                acc[c] = term
            else:
                acc[c] += term
    combine(acc, out, 0, 2)


def final_kernel(pre_grad, act, gathered, stats, gain, out):
    frames, rows, cols, chans = act.shape
    count = gathered.shape[0] * frames * rows * cols * (chans // GROUPS)
    sums = jnp.sum(gathered[...], axis=0, keepdims=True) / count
    first = to_chans(sums, chans, 0)
    second = to_chans(sums, chans, GROUPS)
    mean, rstd = stats[0], stats[1]
    gains = jnp.broadcast_to(gain[...], (8, chans))
    for t in range(frames):
        for h in range(rows):
            normed = (eights(act[t, h].astype(F32)) - mean[None]) * rstd[None]
            value = rstd[None] * (eights(pre_grad[t, h]) * gains[None] - first[None] - normed * second[None])
            out[t, h] = value.reshape(cols, chans).astype(BF16)


def moved(value, frame_step, row_step):
    frames, rows = lax.axis_size("ta"), lax.axis_size("ha")
    pairs = []
    for t in range(frames):
        for h in range(rows):
            to_t, to_h = t + frame_step, h + row_step
            if 0 <= to_t < frames and 0 <= to_h < rows:
                pairs.append((t * rows + h, to_t * rows + to_h))
    return lax.ppermute(value, BOTH, pairs)


def on_device(activations, gain, shift, weight, cotangent):
    shape = activations.shape
    frames, rows, cols, chans = shape
    parts = lax.axis_size("ta") * lax.axis_size("ha")
    gain, shift = gain.reshape(1, chans), shift.reshape(1, chans)
    gathered_shape = jax.ShapeDtypeStruct((parts, LANES), F32)
    edge = jax.ShapeDtypeStruct((2, frames, cols, chans), BF16)
    longer_shape = (frames, rows + 2, cols, chans)
    positions = frames * rows * cols

    pay, up, down = pl.pallas_call(
        stats_kernel,
        in_specs=[ANY, ANY],
        out_specs=[WHOLE, ANY, ANY],
        out_shape=[gathered_shape, edge, edge],
        scratch_shapes=[pltpu.VMEM(shape, BF16), DMA, DMA((4,))],
        compiler_params=params(16),
    )(activations, cotangent)
    above = moved(up, 0, 1)
    below = moved(down, 0, -1)
    gathered = lax.all_to_all(pay, BOTH, 0, 0, tiled=True)

    def grad_scratch():
        return [
            pltpu.VMEM(longer_shape, BF16),
            pltpu.VMEM((6, 3, chans, chans), BF16),
            pltpu.VMEM((3, positions, chans), F32),
            DMA((3,)),
            DMA((6,)),
        ]

    early, longer = pl.pallas_call(
        lambda *refs: grad_kernel(0, 1, 0, 1, True, *refs),
        in_specs=[ANY] * 5,
        out_specs=[WHOLE, ANY],
        out_shape=[jax.ShapeDtypeStruct(shape, BF16), jax.ShapeDtypeStruct(longer_shape, BF16)],
        scratch_shapes=grad_scratch() + [DMA((3,))],
        compiler_params=params(32),
    )(cotangent, above, below, weight, activations)
    incoming = moved(early, -1, 0)
    prior = moved(longer, 1, 0)
    own = pl.pallas_call(
        lambda *refs: grad_kernel(2, 1, 1, 0, False, *refs),
        in_specs=[ANY] * 4,
        out_specs=WHOLE,
        out_shape=jax.ShapeDtypeStruct(shape, F32),
        scratch_shapes=grad_scratch(),
        compiler_params=params(32),
    )(cotangent, above, below, weight)
    pre_grad, pay, stats = pl.pallas_call(
        point_kernel,
        in_specs=[WHOLE] * 7,
        out_specs=[WHOLE] * 3,
        out_shape=[
            jax.ShapeDtypeStruct(shape, F32),
            gathered_shape,
            jax.ShapeDtypeStruct((2, 8, chans), F32),
        ],
        compiler_params=params(32),
    )(own, incoming, early, activations, gathered, gain, shift)
    gathered = lax.all_to_all(pay, BOTH, 0, 0, tiled=True)
    output = pl.pallas_call(
        conv_kernel,
        in_specs=[ANY] * 5 + [WHOLE] * 3,
        out_specs=WHOLE,
        out_shape=jax.ShapeDtypeStruct(shape, BF16),
        scratch_shapes=[
            pltpu.VMEM((frames + 2, rows + 2, cols, chans), BF16),
            pltpu.VMEM((frames + 2, rows + 2, cols, chans), BF16),
            pltpu.VMEM((9, 3, chans, chans), BF16),
            pltpu.VMEM((3, positions, chans), F32),
            DMA((4,)),
            DMA((9,)),
        ],
        compiler_params=params(44),
    )(activations, above, below, prior, weight, stats, gain, shift)
    input_grad = pl.pallas_call(
        final_kernel,
        in_specs=[WHOLE] * 5,
        out_specs=WHOLE,
        out_shape=jax.ShapeDtypeStruct(shape, BF16),
        compiler_params=params(32),
    )(pre_grad, activations, gathered, stats, gain)
    return (output, input_grad)


def solution(mesh):
    placed = (P("ta", "ha", None, None), P(), P(), P(), P("ta", "ha", None, None))
    return jax.shard_map(
        on_device,
        mesh=mesh,
        in_specs=placed,
        out_specs=(P("ta", "ha", None, None), P("ta", "ha", None, None)),
        check_vma=False,
    )
```

time: 537 us -> 114 us (0.21); the launches traced: 526 us -> 113 us
  blocking collectives: 208 us -> 19.1 us
  local copies, waits for them, and re-layouts: 132 us -> 14.6 us
  other arithmetic: 83.1 us -> 0 us
  matrix products: 44.8 us -> 0 us
  Pallas kernels: 0 us -> 39.3 us
  waiting for transfers between devices: 41.6 us -> 16.2 us
  starting transfers between devices: 14.3 us -> 23.3 us
    psum x3 -> x0, blocking collectives: 208 us -> none  [the longest x1 75.2 us: on_device(): mean = lax.psum(group_sum(xf, GROUPS), ('ta', 'ha')) / count]
    scatter-add x19 -> x0, local copies, waits for them, and re-layouts: 108 us -> none  [on_device(): padded_grad.at[a:a + frames, b:b + rows, c:c + cols].add(terms[:, :, :, c])]
    dot_general x18 -> x0, matrix products: 44.8 us -> none  [the longest x9 32.8 us: on_device(): jnp.einsum('thwo,dio->thwdi', cotangent, weight[a, b], preferred_element_...]
    add x19 -> x0, other arithmetic: 40.2 us -> none  [the longest x18 36.9 us: on_device(): padded_grad.at[a:a + frames, b:b + rows, c:c + cols].add(terms[:, :, :, c])]
    pallas_call x0 -> x6, Pallas kernels: none -> 39.3 us  [the longest x1 19.5 us: on_device(): pl.pallas_call(conv_kernel, in_specs=[ANY] * 5 + [WHOLE] * 3, out_specs=W...]
    scatter-add x11 -> x0, other arithmetic: 29.6 us -> none  [the longest x8 24.6 us: on_device(): padded_grad.at[a:a + frames, b:b + rows, c:c + cols].add(terms[:, :, :, c])]
    ppermute x6 -> x4, waiting for transfers between devices: 41.6 us -> 16.2 us  [moved(): return lax.ppermute(value, BOTH, pairs)]
    all_to_all x0 -> x1, blocking collectives: none -> 19.1 us  [on_device(): gathered = lax.all_to_all(pay, BOTH, 0, 0, tiled=True)]
  transfers between devices with their start and end apart: 6 -> 5, of which waited for: 3 -> 2; matrix products, arithmetic and copies ran while one was open for 4% -> 0% of each run, Pallas kernels for 0% -> 10%
where the time goes in v1:
time: 114 us; the launch traced here: 113 us
  Pallas kernels  39.3 us (34%)
  starting transfers between devices  23.3 us (20%)
  blocking collectives  19.1 us (17%)
  waiting for transfers between devices  16.2 us (14%)
  local copies, waits for them, and re-layouts  14.6 us (13%)
    pallas_call x1, Pallas kernels, on_device(): pl.pallas_call(conv_kernel, in_specs=[ANY] * 5 + [WHOLE] * 3, out_specs=W...  19.5 us
    all_to_all x1, blocking collectives, on_device(): gathered = lax.all_to_all(pay, BOTH, 0, 0, tiled=True)  19.1 us
    ppermute x4, waiting for transfers between devices, moved(): return lax.ppermute(value, BOTH, pairs)  16.2 us
    unnamed x20, local copies, waits for them, and re-layouts  14.6 us
    ppermute x4, starting transfers between devices, moved(): return lax.ppermute(value, BOTH, pairs)  12.3 us
    all_to_all x1, starting transfers between devices, on_device(): gathered = lax.all_to_all(pay, BOTH, 0, 0, tiled=True)  10.9 us
    pallas_call x1, Pallas kernels, on_device(): pl.pallas_call(lambda *refs: grad_kernel(2, 1, 1, 0, False, *refs), in_sp...  6.73 us
    pallas_call x1, Pallas kernels, on_device(): pl.pallas_call(lambda *refs: grad_kernel(0, 1, 0, 1, True, *refs), in_spe...  6.72 us
  transfers between devices with their start and end apart: 5, of which 2 were waited for; matrix products, arithmetic and copies ran while one was open for 0% of the time, Pallas kernels for 10%

profile of v1, /device:TPU:1, one launch (start us, length us, event | category | flops | bytes accessed | tf_op | source)
XLA Modules:
  0.0 113.4 jit_solution(4953957189227763046)
XLA Ops:
  0.6 0.0 copy-start.2
  0.6 1.1 copy-done.2
  1.7 0.0 copy-start.4
  1.7 1.1 copy-done.4
  2.8 2.0 %shard_map.68 = (f32[128,128]{1,0:T(8,128)}, bf16[2,2,160,512]{3,2,1,0:T(8,128)(2,1)S(1)}, bf16[2,2,160,512]{3,2,1,0:T(8,128)(2,1)S(1)}) custom-call(bf16[2,2,160,512]{3,2,1,0:T(8,128)(2,1)S(1)} %copy-done.2, bf16[2,2,160,512]{3,2,1,0:T(8,128)(2,1)S(1)} %copy-done.4), custom_call_target="tpu_custom_call" | custom-call | tf_op jit(solution)/shard_map/pallas_call | solution.py:270
  4.8 4.4 %collective-permute-start = (bf16[2,2,160,512]{3,2,1,0:T(8,128)(2,1)S(1)}, bf16[2,2,160,512]{3,2,1,0:T(8,128)(2,1)S(1)}, u32[]{:S(2)}, u32[]{:S(2)}) collective-permute-start(bf16[2,2,160,512]{3,2,1,0:T(8,128)(2,1)S(1)} %get-tuple-element.10), channel_id=1, source_target_pairs={{0,1},{1,2},{2,3},{3,4},{4,5},{5,6},{6,7},{7,8},{8,9},{9,10},{10,1... | collective-permute-start | bytes 1966088 | tf_op jit(solution)/shard_map/ppermute | solution.py:257
  9.3 1.3 %collective-permute-start.1 = (bf16[2,2,160,512]{3,2,1,0:T(8,128)(2,1)S(1)}, bf16[2,2,160,512]{3,2,1,0:T(8,128)(2,1)S(1)}, u32[]{:S(2)}, u32[]{:S(2)}) collective-permute-start(bf16[2,2,160,512]{3,2,1,0:T(8,128)(2,1)S(1)} %get-tuple-element.11), channel_id=1, source_target_pairs={{1,0},{2,1},{3,2},{4,3},{5,4},{6,5},{7,6},{8,7},{9,8},{10,9},{11,1... | collective-permute-start | bytes 1966088 | tf_op jit(solution)/shard_map/ppermute | solution.py:257
  10.6 12.0 %collective-permute-done.refs_1_.above = bf16[2,2,160,512]{3,2,1,0:T(8,128)(2,1)S(1)} collective-permute-done((bf16[2,2,160,512]{3,2,1,0:T(8,128)(2,1)S(1)}, bf16[2,2,160,512]{3,2,1,0:T(8,128)(2,1)S(1)}, u32[]{:S(2)}, u32[]{:S(2)}) %collective-permute-start) | collective-permute-done | bytes 655392 | tf_op jit(solution)/shard_map/ppermute | solution.py:257
  22.6 4.1 %collective-permute-done.1.refs_2_.below = bf16[2,2,160,512]{3,2,1,0:T(8,128)(2,1)S(1)} collective-permute-done((bf16[2,2,160,512]{3,2,1,0:T(8,128)(2,1)S(1)}, bf16[2,2,160,512]{3,2,1,0:T(8,128)(2,1)S(1)}, u32[]{:S(2)}, u32[]{:S(2)}) %collective-permute-start.1) | collective-permute-done | bytes 655392 | tf_op jit(solution)/shard_map/ppermute | solution.py:257
  26.8 0.0 copy-done.3
  26.8 0.0 copy-done.5
  26.8 5.0 %copy-done = bf16[3,3,3,512,512]{4,3,2,1,0:T(8,128)(2,1)S(1)} copy-done((bf16[3,3,3,512,512]{4,3,2,1,0:T(8,128)(2,1)S(1)}, bf16[3,3,3,512,512]{4,3,2,1,0:T(8,128)(2,1)}, u32[]{:S(2)}) %copy-start) | copy-done | bytes 14155800
  31.8 6.7 %shard_map.69 = (bf16[2,2,160,512]{3,2,1,0:T(8,128)(2,1)S(1)}, bf16[2,4,160,512]{3,2,1,0:T(8,128)(2,1)}) custom-call(bf16[2,2,160,512]{3,2,1,0:T(8,128)(2,1)S(1)} %copy-done.5, bf16[2,2,160,512]{3,2,1,0:T(8,128)(2,1)S(1)} %collective-permute-done.refs_1_.above, bf16[2,2,160,512]{3,2,1,0:T(8,128)(2,1)S(1)} %collective-permute-done.1.refs_2_.below, ...), custom_call_target="tpu_custom_call" | custom-call | tf_op jit(solution)/shard_map/pallas_call | solution.py:291
  38.5 4.7 %collective-permute-start.2 = (bf16[2,4,160,512]{3,2,1,0:T(8,128)(2,1)}, bf16[2,4,160,512]{3,2,1,0:T(8,128)(2,1)}, u32[]{:S(2)}, u32[]{:S(2)}) collective-permute-start(bf16[2,4,160,512]{3,2,1,0:T(8,128)(2,1)} %get-tuple-element.12), channel_id=1, source_target_pairs={{0,16},{1,17},{2,18},{3,19},{4,20},{5,21},{6,22},{7,23},{8,24},{9,... | collective-permute-start | bytes 3932168 | tf_op jit(solution)/shard_map/ppermute | solution.py:257
  43.2 1.9 %collective-permute-start.3 = (bf16[2,2,160,512]{3,2,1,0:T(8,128)(2,1)S(1)}, bf16[2,2,160,512]{3,2,1,0:T(8,128)(2,1)}, u32[]{:S(2)}, u32[]{:S(2)}) collective-permute-start(bf16[2,2,160,512]{3,2,1,0:T(8,128)(2,1)S(1)} %get-tuple-element.13.early), channel_id=1, source_target_pairs={{16,0},{17,1},{18,2},{19,3},{20,4},{21,5},{22,6},{23,7},{24,8},{25... | collective-permute-start | bytes 1966088 | tf_op jit(solution)/shard_map/ppermute | solution.py:257
  45.2 10.9 %all-to-all-start = ((f32[128,1,128]{2,1,0:T(1,128)}), f32[128,1,128]{2,1,0:T(1,128)S(1)}, u32[]{:S(2)}, u32[]{:S(2)}) async-start(f32[128,1,128]{2,1,0:T(1,128)} %bitcast.1), calls=%async_computation | async-start | bytes 131072 | tf_op jit(solution)/shard_map/all_to_all | solution.py:280
  56.1 0.0 copy-start.1
  56.1 5.0 %copy-done.1 = bf16[3,3,3,512,512]{4,3,2,1,0:T(8,128)(2,1)S(1)} copy-done((bf16[3,3,3,512,512]{4,3,2,1,0:T(8,128)(2,1)S(1)}, bf16[3,3,3,512,512]{4,3,2,1,0:T(8,128)(2,1)}, u32[]{:S(2)}) %copy-start.1) | copy-done | bytes 14155800
  61.1 6.7 %shard_map.70.own = f32[2,2,160,512]{3,2,1,0:T(8,128)S(1)} custom-call(bf16[2,2,160,512]{3,2,1,0:T(8,128)(2,1)S(1)} %copy-done.5, bf16[2,2,160,512]{3,2,1,0:T(8,128)(2,1)S(1)} %collective-permute-done.refs_1_.above, bf16[2,2,160,512]{3,2,1,0:T(8,128)(2,1)S(1)} %collective-permute-done.1.refs_2_.below, bf16[3,3,3,512,512]{4,3,2,1,0:T(8,128)(2,1)S(1)} %copy-done.1), custom_call_target="tpu_custom_call" | custom-call | tf_op jit(solution)/shard_map/pallas_call | solution.py:301
  67.9 0.0 copy-start.6
  67.9 1.1 copy-done.6
  68.9 0.0 all-to-all-done
  68.9 0.0 collective-permute-done.3.incoming
  68.9 0.0 copy-done.8
  69.0 0.0 copy-done.9
  69.0 0.0 copy-start.7
  69.0 1.3 %copy-done.7 = f32[2,2,160,512]{3,2,1,0:T(8,128)S(1)} copy-done((f32[2,2,160,512]{3,2,1,0:T(8,128)S(1)}, f32[2,2,160,512]{3,2,1,0:T(8,128)}, u32[]{:S(2)}) %copy-start.7) | copy-done | bytes 1310744
  70.3 3.0 %shard_map.71 = (f32[2,2,160,512]{3,2,1,0:T(8,128)S(1)}, f32[128,128]{1,0:T(8,128)S(1)}, f32[2,8,512]{2,1,0:T(8,128)S(1)}) custom-call(f32[2,2,160,512]{3,2,1,0:T(8,128)S(1)} %copy-done.7, bf16[2,2,160,512]{3,2,1,0:T(8,128)(2,1)} %collective-permute-done.3.incoming, bf16[2,2,160,512]{3,2,1,0:T(8,128)(2,1)S(1)} %get-tuple-element.13.early, ...), custom_call_target="tpu_custom_call" | custom-call | tf_op jit(solution)/shard_map/pallas_call | solution.py:309
  73.2 19.1 %all_to_all.22 = f32[128,1,128]{2,1,0:T(1,128)S(1)} all-to-all(f32[128,1,128]{2,1,0:T(1,128)S(1)} %bitcast.12), channel_id=1, replica_groups=mesh['ta'=8,'ha'=16] {'ta','ha'}, dimensions={0} | all-to-all | bytes 131072 | tf_op jit(solution)/shard_map/all_to_all | solution.py:320
  92.4 1.4 %shard_map.73 = bf16[2,2,160,512]{3,2,1,0:T(8,128)(2,1)} custom-call(f32[2,2,160,512]{3,2,1,0:T(8,128)S(1)} %get-tuple-element.16.pre_grad, bf16[2,2,160,512]{3,2,1,0:T(8,128)(2,1)S(1)} %copy-done.3, f32[128,128]{1,0:T(8,128)S(1)} %bitcast.11, f32[2,8,512]{2,1,0:T(8,128)S(1)} %get-tuple-element.15.stats, f32[1,512]{1,0:T(1,128)S(1)} %bitcast.14), custom_call_target="tpu_custom_call" | custom-call | tf_op jit(solution)/shard_map/pallas_call | solution.py:336
  93.8 0.0 collective-permute-done.2.prior
  93.8 19.5 %shard_map.72 = bf16[2,2,160,512]{3,2,1,0:T(8,128)(2,1)} custom-call(bf16[2,2,160,512]{3,2,1,0:T(8,128)(2,1)S(1)} %copy-done.3, bf16[2,2,160,512]{3,2,1,0:T(8,128)(2,1)S(1)} %collective-permute-done.refs_1_.above, bf16[2,2,160,512]{3,2,1,0:T(8,128)(2,1)S(1)} %collective-permute-done.1.refs_2_.below, bf16[2,4,160,512]{3,2,1,0:T(8,128)(2,1)} %collective-permute-done.2.prior, ...), custom_call_target="tpu_custom_call" | custom-call | tf_op jit(solution)/shard_map/pallas_call | solution.py:321
  (5 shorter events, 0.0 us)
Async XLA Ops:
  0.6 1.1 copy-start.2
  1.7 1.1 copy-start.4
  2.8 23.9 %copy-start.3 = (bf16[2,2,160,512]{3,2,1,0:T(8,128)(2,1)S(1)}, bf16[2,2,160,512]{3,2,1,0:T(8,128)(2,1)}, u32[]{:S(2)}) copy-start(bf16[2,2,160,512]{3,2,1,0:T(8,128)(2,1)} %act.7) | copy-start | bytes 1966084
  2.8 23.9 %copy-start.5 = (bf16[2,2,160,512]{3,2,1,0:T(8,128)(2,1)S(1)}, bf16[2,2,160,512]{3,2,1,0:T(8,128)(2,1)}, u32[]{:S(2)}) copy-start(bf16[2,2,160,512]{3,2,1,0:T(8,128)(2,1)} %refs_0_.3) | copy-start | bytes 1966084
  4.8 17.8 %collective-permute-start = (bf16[2,2,160,512]{3,2,1,0:T(8,128)(2,1)S(1)}, bf16[2,2,160,512]{3,2,1,0:T(8,128)(2,1)S(1)}, u32[]{:S(2)}, u32[]{:S(2)}) collective-permute-start(bf16[2,2,160,512]{3,2,1,0:T(8,128)(2,1)S(1)} %get-tuple-element.10), channel_id=1, source_target_pairs={{0,1},{1,2},{2,3},{3,4},{4,5},{5,6},{6,7},{7,8},{8,9},{9,10},{10,1... | collective-permute-start | bytes 1966088 | tf_op jit(solution)/shard_map/ppermute | solution.py:257
  9.3 17.5 %collective-permute-start.1 = (bf16[2,2,160,512]{3,2,1,0:T(8,128)(2,1)S(1)}, bf16[2,2,160,512]{3,2,1,0:T(8,128)(2,1)S(1)}, u32[]{:S(2)}, u32[]{:S(2)}) collective-permute-start(bf16[2,2,160,512]{3,2,1,0:T(8,128)(2,1)S(1)} %get-tuple-element.11), channel_id=1, source_target_pairs={{1,0},{2,1},{3,2},{4,3},{5,4},{6,5},{7,6},{8,7},{9,8},{10,9},{11,1... | collective-permute-start | bytes 1966088 | tf_op jit(solution)/shard_map/ppermute | solution.py:257
  26.8 5.0 %copy-start = (bf16[3,3,3,512,512]{4,3,2,1,0:T(8,128)(2,1)S(1)}, bf16[3,3,3,512,512]{4,3,2,1,0:T(8,128)(2,1)}, u32[]{:S(2)}) copy-start(bf16[3,3,3,512,512]{4,3,2,1,0:T(8,128)(2,1)} %weight.1) | copy-start | bytes 42467332
  38.5 55.3 %collective-permute-start.2 = (bf16[2,4,160,512]{3,2,1,0:T(8,128)(2,1)}, bf16[2,4,160,512]{3,2,1,0:T(8,128)(2,1)}, u32[]{:S(2)}, u32[]{:S(2)}) collective-permute-start(bf16[2,4,160,512]{3,2,1,0:T(8,128)(2,1)} %get-tuple-element.12), channel_id=1, source_target_pairs={{0,16},{1,17},{2,18},{3,19},{4,20},{5,21},{6,22},{7,23},{8,24},{9,... | collective-permute-start | bytes 3932168 | tf_op jit(solution)/shard_map/ppermute | solution.py:257
  43.2 25.7 %collective-permute-start.3 = (bf16[2,2,160,512]{3,2,1,0:T(8,128)(2,1)S(1)}, bf16[2,2,160,512]{3,2,1,0:T(8,128)(2,1)}, u32[]{:S(2)}, u32[]{:S(2)}) collective-permute-start(bf16[2,2,160,512]{3,2,1,0:T(8,128)(2,1)S(1)} %get-tuple-element.13.early), channel_id=1, source_target_pairs={{16,0},{17,1},{18,2},{19,3},{20,4},{21,5},{22,6},{23,7},{24,8},{25... | collective-permute-start | bytes 1966088 | tf_op jit(solution)/shard_map/ppermute | solution.py:257
  45.2 23.8 %all-to-all-start = ((f32[128,1,128]{2,1,0:T(1,128)}), f32[128,1,128]{2,1,0:T(1,128)S(1)}, u32[]{:S(2)}, u32[]{:S(2)}) async-start(f32[128,1,128]{2,1,0:T(1,128)} %bitcast.1), calls=%async_computation | async-start | bytes 131072 | tf_op jit(solution)/shard_map/all_to_all | solution.py:280
  56.1 5.0 %copy-start.1 = (bf16[3,3,3,512,512]{4,3,2,1,0:T(8,128)(2,1)S(1)}, bf16[3,3,3,512,512]{4,3,2,1,0:T(8,128)(2,1)}, u32[]{:S(2)}) copy-start(bf16[3,3,3,512,512]{4,3,2,1,0:T(8,128)(2,1)} %weight.1) | copy-start | bytes 42467332
  61.1 7.8 %copy-start.8 = (f32[512]{0:T(512)S(1)}, f32[512]{0:T(512)}, u32[]{:S(2)}) copy-start(f32[512]{0:T(512)} %param.6) | copy-start | bytes 6148
  61.1 7.8 %copy-start.9 = (f32[512]{0:T(512)S(1)}, f32[512]{0:T(512)}, u32[]{:S(2)}) copy-start(f32[512]{0:T(512)} %param.7) | copy-start | bytes 6148
  67.9 1.1 copy-start.6
  69.0 1.3 %copy-start.7 = (f32[2,2,160,512]{3,2,1,0:T(8,128)S(1)}, f32[2,2,160,512]{3,2,1,0:T(8,128)}, u32[]{:S(2)}) copy-start(f32[2,2,160,512]{3,2,1,0:T(8,128)} %copy-done.6) | copy-start | bytes 3932164

commit v2 on v1

--- a/solution.py
+++ b/solution.py
@@ -9,7 +9,7 @@
 LANES = 128
 F32 = jnp.float32
 BF16 = jnp.bfloat16
-ANY = pl.BlockSpec(memory_space=pl.ANY)
+HBM = pl.BlockSpec(memory_space=pltpu.HBM)
 WHOLE = pl.BlockSpec(memory_space=pltpu.VMEM)
 DMA = pltpu.SemaphoreType.DMA
 BOTH = ("ta", "ha")
@@ -257,9 +257,14 @@
     return lax.ppermute(value, BOTH, pairs)
 
 
+def in_hbm(value):
+    return pltpu.with_memory_space_constraint(value, pltpu.HBM)
+
+
 def on_device(activations, gain, shift, weight, cotangent):
     shape = activations.shape
     frames, rows, cols, chans = shape
+    act, cot, taps = in_hbm(activations), in_hbm(cotangent), in_hbm(weight)
     parts = lax.axis_size("ta") * lax.axis_size("ha")
     gain, shift = gain.reshape(1, chans), shift.reshape(1, chans)
     gathered_shape = jax.ShapeDtypeStruct((parts, LANES), F32)
@@ -269,12 +274,12 @@
 
     pay, up, down = pl.pallas_call(
         stats_kernel,
-        in_specs=[ANY, ANY],
-        out_specs=[WHOLE, ANY, ANY],
+        in_specs=[HBM, HBM],
+        out_specs=[WHOLE] * 3,
         out_shape=[gathered_shape, edge, edge],
         scratch_shapes=[pltpu.VMEM(shape, BF16), DMA, DMA((4,))],
         compiler_params=params(16),
-    )(activations, cotangent)
+    )(act, cot)
     above = moved(up, 0, 1)
     below = moved(down, 0, -1)
     gathered = lax.all_to_all(pay, BOTH, 0, 0, tiled=True)
@@ -290,22 +295,23 @@
 
     early, longer = pl.pallas_call(
         lambda *refs: grad_kernel(0, 1, 0, 1, True, *refs),
-        in_specs=[ANY] * 5,
-        out_specs=[WHOLE, ANY],
+        in_specs=[HBM] * 5,
+        out_specs=[WHOLE] * 2,
         out_shape=[jax.ShapeDtypeStruct(shape, BF16), jax.ShapeDtypeStruct(longer_shape, BF16)],
         scratch_shapes=grad_scratch() + [DMA((3,))],
         compiler_params=params(32),
-    )(cotangent, above, below, weight, activations)
+    )(cot, above, below, taps, act)
+    early, longer, gathered = lax.optimization_barrier((early, longer, gathered))
     incoming = moved(early, -1, 0)
     prior = moved(longer, 1, 0)
     own = pl.pallas_call(
         lambda *refs: grad_kernel(2, 1, 1, 0, False, *refs),
-        in_specs=[ANY] * 4,
+        in_specs=[HBM] * 4,
         out_specs=WHOLE,
         out_shape=jax.ShapeDtypeStruct(shape, F32),
         scratch_shapes=grad_scratch(),
         compiler_params=params(32),
-    )(cotangent, above, below, weight)
+    )(cot, above, below, taps)
     pre_grad, pay, stats = pl.pallas_call(
         point_kernel,
         in_specs=[WHOLE] * 7,
@@ -320,7 +326,7 @@
     gathered = lax.all_to_all(pay, BOTH, 0, 0, tiled=True)
     output = pl.pallas_call(
         conv_kernel,
-        in_specs=[ANY] * 5 + [WHOLE] * 3,
+        in_specs=[HBM] * 5 + [WHOLE] * 3,
         out_specs=WHOLE,
         out_shape=jax.ShapeDtypeStruct(shape, BF16),
         scratch_shapes=[
@@ -332,7 +338,8 @@
             DMA((9,)),
         ],
         compiler_params=params(44),
-    )(activations, above, below, prior, weight, stats, gain, shift)
+    )(act, above, below, prior, taps, stats, gain, shift)
+    output, gathered = lax.optimization_barrier((output, gathered))
     input_grad = pl.pallas_call(
         final_kernel,
         in_specs=[WHOLE] * 5,

time: 114 us -> 84.2 us (0.74)
  blocking collectives: 19.1 us -> 0 us
  starting transfers between devices: 23.3 us -> 35.1 us
  local copies, waits for them, and re-layouts: 14.6 us -> 3.47 us
  waiting for transfers between devices: 16.2 us -> 7.18 us
  Pallas kernels: 39.3 us -> 37.4 us
    all_to_all x1 -> x0, blocking collectives: 19.1 us -> none  [on_device(): gathered = lax.all_to_all(pay, BOTH, 0, 0, tiled=True)]
    all_to_all x1 -> x2, starting transfers between devices: 10.9 us -> 22.1 us  [on_device(): gathered = lax.all_to_all(pay, BOTH, 0, 0, tiled=True)]
    unnamed x20 -> x14, local copies, waits for them, and re-layouts: 14.6 us -> 3.47 us
    ppermute x4, waiting for transfers between devices: 16.2 us -> 7.17 us  [moved(): return lax.ppermute(value, BOTH, pairs)]
    pallas_call x2, Pallas kernels: 21.5 us -> 18.5 us  [the longest x1 15.4 us: on_device(): pl.pallas_call(conv_kernel, in_specs=[HBM] * 5 + [WHOLE] * 3, out_specs=W...]
  transfers between devices with their start and end apart: 5 -> 6, of which waited for: 2 -> 3; matrix products, arithmetic and copies ran while one was open for 0% -> 0% of each run, Pallas kernels for 10% -> 39%
where the time goes in v2:
time: 84.2 us; the launch traced here: 83.9 us
  Pallas kernels  37.4 us (44%)
  starting transfers between devices  35.1 us (42%)
  waiting for transfers between devices  7.18 us (9%)
  local copies, waits for them, and re-layouts  3.47 us (4%)
    all_to_all x2, starting transfers between devices, on_device(): gathered = lax.all_to_all(pay, BOTH, 0, 0, tiled=True)  22.1 us
    pallas_call x1, Pallas kernels, on_device(): pl.pallas_call(conv_kernel, in_specs=[HBM] * 5 + [WHOLE] * 3, out_specs=W...  15.4 us
    ppermute x4, starting transfers between devices, moved(): return lax.ppermute(value, BOTH, pairs)  12.9 us
    pallas_call x1, Pallas kernels, on_device(): pl.pallas_call(lambda *refs: grad_kernel(2, 1, 1, 0, False, *refs), in_sp...  7.5 us
    pallas_call x1, Pallas kernels, on_device(): pl.pallas_call(lambda *refs: grad_kernel(0, 1, 0, 1, True, *refs), in_spe...  7.49 us
    ppermute x4, waiting for transfers between devices, moved(): return lax.ppermute(value, BOTH, pairs)  7.17 us
    unnamed x14, local copies, waits for them, and re-layouts  3.47 us
    pallas_call x1, Pallas kernels, on_device(): pl.pallas_call(stats_kernel, in_specs=[HBM, HBM], out_specs=[WHOLE] * 3,...  3.03 us
  transfers between devices with their start and end apart: 6, of which 3 were waited for; matrix products, arithmetic and copies ran while one was open for 0% of the time, Pallas kernels for 39%

profile of v2, /device:TPU:1, one launch (start us, length us, event | category | flops | bytes accessed | tf_op | source)
XLA Modules:
  0.0 83.9 jit_solution(12557289562688822690)
XLA Ops:
  0.6 3.0 %shard_map.68 = (f32[128,128]{1,0:T(8,128)}, bf16[2,2,160,512]{3,2,1,0:T(8,128)(2,1)S(1)}, bf16[2,2,160,512]{3,2,1,0:T(8,128)(2,1)S(1)}) custom-call(bf16[2,2,160,512]{3,2,1,0:T(8,128)(2,1)} %act.7, bf16[2,2,160,512]{3,2,1,0:T(8,128)(2,1)} %refs_0_.3), custom_call_target="tpu_custom_call" | custom-call | tf_op jit(solution)/shard_map/pallas_call | solution.py:275
  3.7 4.4 %collective-permute-start = (bf16[2,2,160,512]{3,2,1,0:T(8,128)(2,1)S(1)}, bf16[2,2,160,512]{3,2,1,0:T(8,128)(2,1)S(1)}, u32[]{:S(2)}, u32[]{:S(2)}) collective-permute-start(bf16[2,2,160,512]{3,2,1,0:T(8,128)(2,1)S(1)} %get-tuple-element.15), channel_id=1, source_target_pairs={{0,1},{1,2},{2,3},{3,4},{4,5},{5,6},{6,7},{7,8},{8,9},{9,10},{10,1... | collective-permute-start | bytes 1966088 | tf_op jit(solution)/shard_map/ppermute | solution.py:257
  8.1 1.3 %collective-permute-start.1 = (bf16[2,2,160,512]{3,2,1,0:T(8,128)(2,1)S(1)}, bf16[2,2,160,512]{3,2,1,0:T(8,128)(2,1)S(1)}, u32[]{:S(2)}, u32[]{:S(2)}) collective-permute-start(bf16[2,2,160,512]{3,2,1,0:T(8,128)(2,1)S(1)} %get-tuple-element.16), channel_id=1, source_target_pairs={{1,0},{2,1},{3,2},{4,3},{5,4},{6,5},{7,6},{8,7},{9,8},{10,9},{11,1... | collective-permute-start | bytes 1966088 | tf_op jit(solution)/shard_map/ppermute | solution.py:257
  9.4 11.6 %all-to-all-start = ((f32[128,1,128]{2,1,0:T(1,128)}), f32[128,1,128]{2,1,0:T(1,128)S(1)}, u32[]{:S(2)}, u32[]{:S(2)}) async-start(f32[128,1,128]{2,1,0:T(1,128)} %bitcast.1), calls=%async_computation | async-start | bytes 131072 | tf_op jit(solution)/shard_map/all_to_all | solution.py:285
  21.0 0.4 collective-permute-done.refs_1_.above
  21.4 4.3 %collective-permute-done.1.refs_2_.below = bf16[2,2,160,512]{3,2,1,0:T(8,128)(2,1)S(1)} collective-permute-done((bf16[2,2,160,512]{3,2,1,0:T(8,128)(2,1)S(1)}, bf16[2,2,160,512]{3,2,1,0:T(8,128)(2,1)S(1)}, u32[]{:S(2)}, u32[]{:S(2)}) %collective-permute-start.1) | collective-permute-done | bytes 655392 | tf_op jit(solution)/shard_map/ppermute | solution.py:257
  25.7 7.5 %shard_map.69 = (bf16[2,2,160,512]{3,2,1,0:T(8,128)(2,1)S(1)}, bf16[2,4,160,512]{3,2,1,0:T(8,128)(2,1)S(1)}) custom-call(bf16[2,2,160,512]{3,2,1,0:T(8,128)(2,1)} %refs_0_.3, bf16[2,2,160,512]{3,2,1,0:T(8,128)(2,1)S(1)} %collective-permute-done.refs_1_.above, bf16[2,2,160,512]{3,2,1,0:T(8,128)(2,1)S(1)} %collective-permute-done.1.refs_2_.below, ...), custom_call_target="tpu_custom_call" | custom-call | tf_op jit(solution)/shard_map/pallas_call | solution.py:296
  33.2 0.0 copy-start.6
  33.2 1.1 %copy-done.6 = bf16[2,4,160,512]{3,2,1,0:T(8,128)(2,1)} copy-done((bf16[2,4,160,512]{3,2,1,0:T(8,128)(2,1)}, bf16[2,4,160,512]{3,2,1,0:T(8,128)(2,1)S(1)}, u32[]{:S(2)}) %copy-start.6) | copy-done | bytes 1310744
  34.3 0.0 all-to-all-done
  34.3 0.0 copy-start
  34.3 0.0 copy-start.4
  34.3 0.0 copy-start.5
  34.3 5.3 %collective-permute-start.2 = (bf16[2,4,160,512]{3,2,1,0:T(8,128)(2,1)}, bf16[2,4,160,512]{3,2,1,0:T(8,128)(2,1)S(1)}, u32[]{:S(2)}, u32[]{:S(2)}) collective-permute-start(bf16[2,4,160,512]{3,2,1,0:T(8,128)(2,1)} %copy-done.6), channel_id=1, source_target_pairs={{0,16},{1,17},{2,18},{3,19},{4,20},{5,21},{6,22},{7,23},{8,24},{9,... | collective-permute-start | bytes 3932168 | tf_op jit(solution)/shard_map/ppermute | solution.py:257
  39.6 1.9 %collective-permute-start.3 = (bf16[2,2,160,512]{3,2,1,0:T(8,128)(2,1)S(1)}, bf16[2,2,160,512]{3,2,1,0:T(8,128)(2,1)S(1)}, u32[]{:S(2)}, u32[]{:S(2)}) collective-permute-start(bf16[2,2,160,512]{3,2,1,0:T(8,128)(2,1)S(1)} %get-tuple-element.21.early), channel_id=1, source_target_pairs={{16,0},{17,1},{18,2},{19,3},{20,4},{21,5},{22,6},{23,7},{24,8},{25... | collective-permute-start | bytes 1966088 | tf_op jit(solution)/shard_map/ppermute | solution.py:257
  41.5 7.5 %shard_map.70.own = f32[2,2,160,512]{3,2,1,0:T(8,128)S(1)} custom-call(bf16[2,2,160,512]{3,2,1,0:T(8,128)(2,1)} %refs_0_.3, bf16[2,2,160,512]{3,2,1,0:T(8,128)(2,1)S(1)} %collective-permute-done.refs_1_.above, bf16[2,2,160,512]{3,2,1,0:T(8,128)(2,1)S(1)} %collective-permute-done.1.refs_2_.below, bf16[3,3,3,512,512]{4,3,2,1,0:T(8,128)(2,1)} %weight.1), custom_call_target="tpu_custom_call" | custom-call | tf_op jit(solution)/shard_map/pallas_call | solution.py:307
  49.0 2.5 %collective-permute-done.3.incoming = bf16[2,2,160,512]{3,2,1,0:T(8,128)(2,1)S(1)} collective-permute-done((bf16[2,2,160,512]{3,2,1,0:T(8,128)(2,1)S(1)}, bf16[2,2,160,512]{3,2,1,0:T(8,128)(2,1)S(1)}, u32[]{:S(2)}, u32[]{:S(2)}) %collective-permute-start.3) | collective-permute-done | bytes 655392 | tf_op jit(solution)/shard_map/ppermute | solution.py:257
  51.5 0.0 copy-done
  51.5 0.0 copy-done.4
  51.5 0.0 copy-done.5
  51.5 2.5 %shard_map.71 = (f32[2,2,160,512]{3,2,1,0:T(8,128)S(1)}, f32[128,128]{1,0:T(8,128)}, f32[2,8,512]{2,1,0:T(8,128)S(1)}) custom-call(f32[2,2,160,512]{3,2,1,0:T(8,128)S(1)} %shard_map.70.own, bf16[2,2,160,512]{3,2,1,0:T(8,128)(2,1)S(1)} %collective-permute-done.3.incoming, bf16[2,2,160,512]{3,2,1,0:T(8,128)(2,1)S(1)} %get-tuple-element.21.early, ...), custom_call_target="tpu_custom_call" | custom-call | tf_op jit(solution)/shard_map/pallas_call | solution.py:315
  54.1 0.0 copy-start.2
  54.1 1.1 %copy-done.2 = f32[2,2,160,512]{3,2,1,0:T(8,128)} copy-done((f32[2,2,160,512]{3,2,1,0:T(8,128)}, f32[2,2,160,512]{3,2,1,0:T(8,128)S(1)}, u32[]{:S(2)}) %copy-start.2) | copy-done | bytes 1310744
  55.2 10.5 %all-to-all-start.1 = ((f32[128,1,128]{2,1,0:T(1,128)}), f32[128,1,128]{2,1,0:T(1,128)S(1)}, u32[]{:S(2)}, u32[]{:S(2)}) async-start(f32[128,1,128]{2,1,0:T(1,128)} %bitcast.6), calls=%async_computation.1 | async-start | bytes 131072 | tf_op jit(solution)/shard_map/all_to_all | solution.py:326
  65.7 0.0 collective-permute-done.2.prior
  65.7 0.0 copy-start.1
  65.7 15.4 %shard_map.72 = bf16[2,2,160,512]{3,2,1,0:T(8,128)(2,1)} custom-call(bf16[2,2,160,512]{3,2,1,0:T(8,128)(2,1)} %act.7, bf16[2,2,160,512]{3,2,1,0:T(8,128)(2,1)S(1)} %collective-permute-done.refs_1_.above, bf16[2,2,160,512]{3,2,1,0:T(8,128)(2,1)S(1)} %collective-permute-done.1.refs_2_.below, bf16[2,4,160,512]{3,2,1,0:T(8,128)(2,1)S(1)} %collective-permute-done.2.prior, ...), custom_call_target="tpu_custom_call" | custom-call | tf_op jit(solution)/shard_map/pallas_call | solution.py:327
  81.1 0.0 all-to-all-done.1
  81.2 0.0 copy-done.1
  81.2 0.0 copy-start.3
  81.2 1.3 %copy-done.3 = f32[2,2,160,512]{3,2,1,0:T(8,128)S(1)} copy-done((f32[2,2,160,512]{3,2,1,0:T(8,128)S(1)}, f32[2,2,160,512]{3,2,1,0:T(8,128)}, u32[]{:S(2)}) %copy-start.3) | copy-done | bytes 1310744
  82.5 1.4 %shard_map.73 = bf16[2,2,160,512]{3,2,1,0:T(8,128)(2,1)} custom-call(f32[2,2,160,512]{3,2,1,0:T(8,128)S(1)} %copy-done.3, bf16[2,2,160,512]{3,2,1,0:T(8,128)(2,1)S(1)} %copy-done.1, f32[128,128]{1,0:T(8,128)S(1)} %bitcast.11, f32[2,8,512]{2,1,0:T(8,128)S(1)} %get-tuple-element.23.stats, f32[1,512]{1,0:T(1,128)S(1)} %bitcast.14), custom_call_target="tpu_custom_call" | custom-call | tf_op jit(solution)/shard_map/pallas_call | solution.py:343
Async XLA Ops:
  3.7 17.8 %collective-permute-start = (bf16[2,2,160,512]{3,2,1,0:T(8,128)(2,1)S(1)}, bf16[2,2,160,512]{3,2,1,0:T(8,128)(2,1)S(1)}, u32[]{:S(2)}, u32[]{:S(2)}) collective-permute-start(bf16[2,2,160,512]{3,2,1,0:T(8,128)(2,1)S(1)} %get-tuple-element.15), channel_id=1, source_target_pairs={{0,1},{1,2},{2,3},{3,4},{4,5},{5,6},{6,7},{7,8},{8,9},{9,10},{10,1... | collective-permute-start | bytes 1966088 | tf_op jit(solution)/shard_map/ppermute | solution.py:257
  8.1 17.6 %collective-permute-start.1 = (bf16[2,2,160,512]{3,2,1,0:T(8,128)(2,1)S(1)}, bf16[2,2,160,512]{3,2,1,0:T(8,128)(2,1)S(1)}, u32[]{:S(2)}, u32[]{:S(2)}) collective-permute-start(bf16[2,2,160,512]{3,2,1,0:T(8,128)(2,1)S(1)} %get-tuple-element.16), channel_id=1, source_target_pairs={{1,0},{2,1},{3,2},{4,3},{5,4},{6,5},{7,6},{8,7},{9,8},{10,9},{11,1... | collective-permute-start | bytes 1966088 | tf_op jit(solution)/shard_map/ppermute | solution.py:257
  9.4 24.9 %all-to-all-start = ((f32[128,1,128]{2,1,0:T(1,128)}), f32[128,1,128]{2,1,0:T(1,128)S(1)}, u32[]{:S(2)}, u32[]{:S(2)}) async-start(f32[128,1,128]{2,1,0:T(1,128)} %bitcast.1), calls=%async_computation | async-start | bytes 131072 | tf_op jit(solution)/shard_map/all_to_all | solution.py:285
  33.2 1.1 %copy-start.6 = (bf16[2,4,160,512]{3,2,1,0:T(8,128)(2,1)}, bf16[2,4,160,512]{3,2,1,0:T(8,128)(2,1)S(1)}, u32[]{:S(2)}) copy-start(bf16[2,4,160,512]{3,2,1,0:T(8,128)(2,1)S(1)} %get-tuple-element.20) | copy-start | bytes 3932164
  34.3 17.2 %copy-start = (bf16[2,2,160,512]{3,2,1,0:T(8,128)(2,1)S(1)}, bf16[2,2,160,512]{3,2,1,0:T(8,128)(2,1)}, u32[]{:S(2)}) copy-start(bf16[2,2,160,512]{3,2,1,0:T(8,128)(2,1)} %act.7) | copy-start | bytes 1966084
  34.3 17.2 %copy-start.4 = (f32[512]{0:T(512)S(1)}, f32[512]{0:T(512)}, u32[]{:S(2)}) copy-start(f32[512]{0:T(512)} %param.6) | copy-start | bytes 6148
  34.3 17.2 %copy-start.5 = (f32[512]{0:T(512)S(1)}, f32[512]{0:T(512)}, u32[]{:S(2)}) copy-start(f32[512]{0:T(512)} %param.7) | copy-start | bytes 6148
  34.3 31.3 %collective-permute-start.2 = (bf16[2,4,160,512]{3,2,1,0:T(8,128)(2,1)}, bf16[2,4,160,512]{3,2,1,0:T(8,128)(2,1)S(1)}, u32[]{:S(2)}, u32[]{:S(2)}) collective-permute-start(bf16[2,4,160,512]{3,2,1,0:T(8,128)(2,1)} %copy-done.6), channel_id=1, source_target_pairs={{0,16},{1,17},{2,18},{3,19},{4,20},{5,21},{6,22},{7,23},{8,24},{9,... | collective-permute-start | bytes 3932168 | tf_op jit(solution)/shard_map/ppermute | solution.py:257
  39.6 11.9 %collective-permute-start.3 = (bf16[2,2,160,512]{3,2,1,0:T(8,128)(2,1)S(1)}, bf16[2,2,160,512]{3,2,1,0:T(8,128)(2,1)S(1)}, u32[]{:S(2)}, u32[]{:S(2)}) collective-permute-start(bf16[2,2,160,512]{3,2,1,0:T(8,128)(2,1)S(1)} %get-tuple-element.21.early), channel_id=1, source_target_pairs={{16,0},{17,1},{18,2},{19,3},{20,4},{21,5},{22,6},{23,7},{24,8},{25... | collective-permute-start | bytes 1966088 | tf_op jit(solution)/shard_map/ppermute | solution.py:257
  54.1 1.1 %copy-start.2 = (f32[2,2,160,512]{3,2,1,0:T(8,128)}, f32[2,2,160,512]{3,2,1,0:T(8,128)S(1)}, u32[]{:S(2)}) copy-start(f32[2,2,160,512]{3,2,1,0:T(8,128)S(1)} %get-tuple-element.26.pre_grad) | copy-start | bytes 3932164
  55.2 26.0 %all-to-all-start.1 = ((f32[128,1,128]{2,1,0:T(1,128)}), f32[128,1,128]{2,1,0:T(1,128)S(1)}, u32[]{:S(2)}, u32[]{:S(2)}) async-start(f32[128,1,128]{2,1,0:T(1,128)} %bitcast.6), calls=%async_computation.1 | async-start | bytes 131072 | tf_op jit(solution)/shard_map/all_to_all | solution.py:326
  65.7 15.5 %copy-start.1 = (bf16[2,2,160,512]{3,2,1,0:T(8,128)(2,1)S(1)}, bf16[2,2,160,512]{3,2,1,0:T(8,128)(2,1)}, u32[]{:S(2)}) copy-start(bf16[2,2,160,512]{3,2,1,0:T(8,128)(2,1)} %act.7) | copy-start | bytes 1966084
  81.2 1.3 %copy-start.3 = (f32[2,2,160,512]{3,2,1,0:T(8,128)S(1)}, f32[2,2,160,512]{3,2,1,0:T(8,128)}, u32[]{:S(2)}) copy-start(f32[2,2,160,512]{3,2,1,0:T(8,128)} %copy-done.2) | copy-start | bytes 3932164

commit v3 on v2

v3 whole, which is shorter than its diff:
```python
import jax
import jax.numpy as jnp
from jax import lax
from jax.experimental import pallas as pl
from jax.experimental.pallas import tpu as pltpu
from jax.sharding import PartitionSpec as P

GROUPS = 32
LANES = 128
F32 = jnp.float32
BF16 = jnp.bfloat16
HBM = pl.BlockSpec(memory_space=pltpu.HBM)
ANY = pl.BlockSpec(memory_space=pl.ANY)
WHOLE = pl.BlockSpec(memory_space=pltpu.VMEM)
DMA = pltpu.SemaphoreType.DMA
BOTH = ("ta", "ha")


def params(mebibytes):
    return pltpu.CompilerParams(vmem_limit_bytes=mebibytes * 2**20)


def member(chans, offset, across):
    shape, chan_dim = ((LANES, chans), 1) if across else ((chans, LANES), 0)
    per_group = chans // GROUPS
    chan = lax.broadcasted_iota(jnp.int32, shape, chan_dim)
    lane = lax.broadcasted_iota(jnp.int32, shape, 1 - chan_dim) - offset
    inside = (chan >= lane * per_group) & (chan < (lane + 1) * per_group)
    return jnp.where(inside & (lane >= 0) & (lane < GROUPS), 1.0, 0.0).astype(F32)


def exact_dot(left, right):
    return jnp.dot(left, right, precision=lax.Precision.HIGHEST, preferred_element_type=F32)


def to_groups(by_chan, offset):
    lanes = exact_dot(by_chan, member(by_chan.shape[1], offset, False))
    return jnp.sum(lanes, axis=0, keepdims=True)


def to_chans(by_group, chans, offset):
    rows = jnp.broadcast_to(by_group, (8, LANES))
    return exact_dot(rows, member(chans, offset, True))


def eights(value):
    return value.reshape(value.shape[0] // 8, 8, value.shape[1])


def stats_kernel(act, cot, pay, up, down, block, load_sem, pack_sem):
    frames, rows, cols, chans = block.shape
    load = pltpu.make_async_copy(act, block, load_sem)
    load.start()
    packs = []
    for i, source in enumerate((act, cot)):
        packs.append(pltpu.make_async_copy(source.at[:, rows - 1], up.at[i], pack_sem.at[2 * i]))
        packs.append(pltpu.make_async_copy(source.at[:, 0], down.at[i], pack_sem.at[2 * i + 1]))
    for pack in packs:
        pack.start()
    load.wait()
    entries = frames * rows * cols * (chans // GROUPS)
    total = jnp.zeros((8, chans), F32)
    for t in range(frames):
        for h in range(rows):
            total = total + jnp.sum(eights(block[t, h].astype(F32)), axis=0)
    sums = to_groups(total, 0)
    mean = to_chans(sums / entries, chans, 0)
    spread = jnp.zeros((8, chans), F32)
    for t in range(frames):
        for h in range(rows):
            centered = eights(block[t, h].astype(F32)) - mean[None]
            spread = spread + jnp.sum(centered * centered, axis=0)
    row = sums + to_groups(spread, GROUPS)
    pay[...] = jnp.broadcast_to(row, pay.shape)
    for pack in packs:
        pack.wait()


def centre_kernel(cot, weight, taps, early, own, block, acc, late, load_sem, tap_sem, late_sem):
    rows, cols, chans = cot.shape[1:]
    half = rows * cols
    load = pltpu.make_async_copy(cot, block, load_sem)
    load.start()
    order = [(2, 1), (1, 1), (0, 1), (0, 0), (0, 2), (1, 0), (1, 2)]
    fetches = [pltpu.make_async_copy(weight.at[a, b], taps.at[a, b], tap_sem.at[a, b]) for a, b in order]
    fetches[0].start()
    fetches[1].start()
    load.wait()
    left = block[...].reshape(2 * half, chans)
    for n, a in enumerate((2, 1, 0)):
        fetches[n].wait()
        for fetch in (fetches[2:4], fetches[4:6], [])[n]:
            fetch.start()
        for c in range(3):
            term = transposed_dot(left, taps[a, 1, c])
            if a == 2:
                acc[1, c] = term
            elif a == 1:
                acc[1, c, :half] += term[half:]
                acc[0, c, half:] = term[:half]
            else:
                acc[0, c, :half] = term[:half]
                acc[0, c, half:] += term[half:]
        if a == 1:
            for fetch in fetches[6:]:
                fetch.start()
            combine(acc.at[1], late, 2, 0, None)
            send = pltpu.make_async_copy(late, own, late_sem)
            send.start()
    combine(acc.at[0], early, 2, 0, None)
    send.wait()
    for fetch in fetches[3:]:
        fetch.wait()


def transposed_dot(left, right):
    return lax.dot_general(left, right, (((1,), (1,)), ((), ())), preferred_element_type=F32)


def grad_products(full, part, source, target, ext, taps, acc, fetches=None):
    rows, cols, chans = ext.shape[1] - 2, ext.shape[2], ext.shape[3]
    half = rows * cols
    for b in (0, 2):
        both = ext[:, 2 - b : 2 - b + rows].reshape(2 * half, chans)
        one = ext[source, 2 - b : 2 - b + rows].reshape(half, chans)
        if fetches:
            fetches.pop(0).wait()
            fetches.pop(0).wait()
            for fetch in fetches:
                fetch.start()
        for c in range(3):
            term = transposed_dot(both, taps[full, b, c])
            if b == 0:
                acc[c] = term
            else:
                acc[c] += term
            acc[c, target * half : (target + 1) * half] += transposed_dot(one, taps[part, b, c])


def halo_copies(cot, above, below, ext, sem):
    rows = cot.shape[1]
    return [
        pltpu.make_async_copy(cot, ext.at[:, 1 : rows + 1], sem.at[0]),
        pltpu.make_async_copy(above.at[1], ext.at[:, 0], sem.at[1]),
        pltpu.make_async_copy(below.at[1], ext.at[:, rows + 1], sem.at[2]),
    ]


def early_kernel(cot, above, below, taps, centre, out, ext, acc, ext_sem):
    loads = halo_copies(cot, above, below, ext, ext_sem)
    for load in loads:
        load.start()
    for load in loads:
        load.wait()
    grad_products(0, 1, 0, 1, ext, taps, acc)
    combine(acc, out, 2, 0, centre)


def own_kernel(cot, above, below, weight, centre, act, gathered, gain, shift, out, longer, stats, ext, taps, acc, more, raw, acts, tap_sem, ext_sem, more_sem, raw_sem, acts_sem):
    frames, rows, cols, chans = act.shape
    load_act = pltpu.make_async_copy(act, raw, raw_sem)
    load_act.start()
    loads = halo_copies(cot, above, below, ext, ext_sem)
    loads.append(pltpu.make_async_copy(centre, more, more_sem))
    for load in loads:
        load.start()
    fetches = [
        pltpu.make_async_copy(weight.at[a, b], taps.at[a - 1, b], tap_sem.at[a - 1, b])
        for b in (0, 2)
        for a in (2, 1)
    ]
    fetches[0].start()
    fetches[1].start()
    entries = frames * rows * cols * (chans // GROUPS)
    mean, rstd = group_stats(gathered[...], entries, chans)
    stats[0] = mean
    stats[1] = rstd
    gains = jnp.broadcast_to(gain[...], (8, chans))
    shifts = jnp.broadcast_to(shift[...], (8, chans))
    row_at = lax.axis_index("ha")
    last_row = lax.axis_size("ha") - 1
    top = jnp.where(row_at == 0, 0.0, 1.0).astype(F32)
    bottom = jnp.where(row_at == last_row, 0.0, 1.0).astype(F32)

    def activate(values, t, i):
        normed = (eights(values.astype(F32)) - mean[None]) * rstd[None]
        pre = normed * gains[None] + shifts[None]
        value = pre / (1.0 + jnp.exp(-pre))
        if i == 0:
            value = value * top
        if i == rows + 1:
            value = value * bottom
        acts[t, i] = value.reshape(cols, chans).astype(BF16)

    for t in range(frames):
        activate(above[0, t], t, 0)
        activate(below[0, t], t, rows + 1)
    load_act.wait()
    sends = []
    for t in range(frames):
        for h in range(rows):
            activate(raw[t, h], t, 1 + h)
        sends.append(pltpu.make_async_copy(acts.at[t], longer.at[t], acts_sem.at[t]))
        sends[t].start()
    for load in loads:
        load.wait()
    grad_products(1, 0, 1, 0, ext, taps, acc, fetches)
    combine(acc, out, 2, 0, more)
    for send in sends:
        send.wait()


def combine(acc, out, earlier, later, more):
    frames, rows, cols, chans = out.shape
    col = lax.broadcasted_iota(jnp.int32, (cols, chans), 0)
    for t in range(frames):
        for h in range(rows):
            at = slice((t * rows + h) * cols, (t * rows + h + 1) * cols)
            before = jnp.where(col == 0, 0.0, pltpu.roll(acc[earlier, at], 1, 0))
            after = jnp.where(col == cols - 1, 0.0, pltpu.roll(acc[later, at], cols - 1, 0))
            total = before + acc[1, at] + after
            if more is not None:
                total = total + more[t, h]
            out[t, h] = total.astype(out.dtype)


def group_stats(gathered, entries, chans):
    parts = gathered.shape[0]
    count = parts * entries
    sums = jnp.sum(gathered, axis=0, keepdims=True)
    mean = sums / count
    apart = gathered * (1.0 / entries) - mean
    between = jnp.sum(apart * apart, axis=0, keepdims=True) * entries
    spread = to_chans(between, chans, 0) + to_chans(sums, chans, GROUPS)
    return to_chans(mean, chans, 0), lax.rsqrt(spread / count + 1e-06)


def point_kernel(own, incoming, early, act, stats, gain, shift, pre_grad, pay, block, block_sem):
    frames, rows, cols, chans = act.shape
    mean, rstd = stats[0], stats[1]
    first = lax.axis_index("ta") == 0
    scale = jnp.where(first, 1.0, 0.0).astype(F32)
    gains = jnp.broadcast_to(gain[...], (8, chans))
    shifts = jnp.broadcast_to(shift[...], (8, chans))
    shift_sum = jnp.zeros((8, chans), F32)
    gain_sum = jnp.zeros((8, chans), F32)
    sends = []
    for t in range(frames):
        for h in range(rows):
            grad = own[t, h] + incoming[t, h].astype(F32)
            if t == 0:
                grad = grad + scale * (early[0, h].astype(F32) + early[1, h].astype(F32))
            normed = (eights(act[t, h].astype(F32)) - mean[None]) * rstd[None]
            pre = normed * gains[None] + shifts[None]
            sig = 1.0 / (1.0 + jnp.exp(-pre))
            local = eights(grad) * sig * (1.0 + pre * (1.0 - sig))
            block[t, h] = local.reshape(cols, chans)
            shift_sum = shift_sum + jnp.sum(local, axis=0)
            gain_sum = gain_sum + jnp.sum(local * normed, axis=0)
            sends.append(pltpu.make_async_copy(block.at[t, h], pre_grad.at[t, h], block_sem.at[t, h]))
            sends[-1].start()
    row = to_groups(gains * shift_sum, 0) + to_groups(gains * gain_sum, GROUPS)
    pay[...] = jnp.broadcast_to(row, pay.shape)
    for send in sends:
        send.wait()


def conv_kernel(longer, prior, weight, out, ext, wide, taps, acc, ext_sem, tap_sem):
    frames, rows, cols, chans = out.shape
    first = lax.axis_index("ta") == 0
    own = pltpu.make_async_copy(longer, ext.at[frames:], ext_sem.at[0])
    own.start()

    @pl.when(first)
    def _():
        for t in range(frames):
            pltpu.make_async_copy(longer.at[0], ext.at[t], ext_sem.at[1 + t]).start()

    @pl.when(jnp.logical_not(first))
    def _():
        for t in range(frames):
            pltpu.make_async_copy(prior.at[t], ext.at[t], ext_sem.at[1 + t]).start()

    fetches = [pltpu.make_async_copy(weight.at[:, :, c], taps.at[c], tap_sem.at[c]) for c in range(3)]
    fetches[0].start()

    def widen(a):
        for b in range(3):
            k = (3 * a + b) * chans
            wide[:, :, :, k : k + chans] = ext[a : a + frames, b : b + rows]

    own.wait()
    widen(2)
    for t in range(frames):
        pltpu.make_async_copy(prior.at[t], ext.at[t], ext_sem.at[1 + t]).wait()
    widen(1)
    widen(0)
    left = wide[...].reshape(frames * rows * cols, 9 * chans)
    for c in range(3):
        fetches[c].wait()
        if c < 2:
            fetches[c + 1].start()
        acc[c] = jnp.dot(left, taps[c].reshape(9 * chans, chans), preferred_element_type=F32)
    combine(acc, out, 0, 2, None)


def final_kernel(pre_grad, act, gathered, stats, gain, out):
    frames, rows, cols, chans = act.shape
    count = gathered.shape[0] * frames * rows * cols * (chans // GROUPS)
    sums = jnp.sum(gathered[...], axis=0, keepdims=True) / count
    first = to_chans(sums, chans, 0)
    second = to_chans(sums, chans, GROUPS)
    mean, rstd = stats[0], stats[1]
    gains = jnp.broadcast_to(gain[...], (8, chans))
    for t in range(frames):
        for h in range(rows):
            normed = (eights(act[t, h].astype(F32)) - mean[None]) * rstd[None]
            value = rstd[None] * (eights(pre_grad[t, h]) * gains[None] - first[None] - normed * second[None])
            out[t, h] = value.reshape(cols, chans).astype(BF16)


def moved(value, frame_step, row_step):
    frames, rows = lax.axis_size("ta"), lax.axis_size("ha")
    pairs = []
    for t in range(frames):
        for h in range(rows):
            to_t, to_h = t + frame_step, h + row_step
            if 0 <= to_t < frames and 0 <= to_h < rows:
                pairs.append((t * rows + h, to_t * rows + to_h))
    return lax.ppermute(value, BOTH, pairs)


def in_hbm(value):
    return pltpu.with_memory_space_constraint(value, pltpu.HBM)


def in_vmem(value):
    return pltpu.with_memory_space_constraint(value, pltpu.VMEM)


def on_device(activations, gain, shift, weight, cotangent):
    shape = activations.shape
    frames, rows, cols, chans = shape
    act, cot, taps = in_hbm(activations), in_hbm(cotangent), in_hbm(weight)
    parts = lax.axis_size("ta") * lax.axis_size("ha")
    gain, shift = gain.reshape(1, chans), shift.reshape(1, chans)
    gathered_shape = jax.ShapeDtypeStruct((parts, LANES), F32)
    edge = jax.ShapeDtypeStruct((2, frames, cols, chans), BF16)
    longer_shape = (frames, rows + 2, cols, chans)
    positions = frames * rows * cols

    pay, up, down = pl.pallas_call(
        stats_kernel,
        in_specs=[HBM, HBM],
        out_specs=[WHOLE] * 3,
        out_shape=[gathered_shape, edge, edge],
        scratch_shapes=[pltpu.VMEM(shape, BF16), DMA, DMA((4,))],
        compiler_params=params(16),
    )(act, cot)
    above = moved(up, 0, 1)
    below = moved(down, 0, -1)
    gathered = lax.all_to_all(pay, BOTH, 0, 0, tiled=True)

    f32_block = jax.ShapeDtypeStruct(shape, F32)
    sums = (3, positions, chans)
    held, early_centre, own_centre = pl.pallas_call(
        centre_kernel,
        in_specs=[HBM] * 2,
        out_specs=[WHOLE, WHOLE, HBM],
        out_shape=[pltpu.VMEM(weight.shape, BF16), f32_block, pltpu.HBM(shape, F32)],
        scratch_shapes=[
            pltpu.VMEM(shape, BF16),
            pltpu.VMEM((2,) + sums, F32),
            pltpu.VMEM(shape, F32),
            DMA,
            DMA((3, 3)),
            DMA,
        ],
        compiler_params=params(16),
    )(cot, taps)
    held = in_vmem(held)
    early = pl.pallas_call(
        early_kernel,
        in_specs=[HBM, WHOLE, WHOLE, WHOLE, WHOLE],
        out_specs=WHOLE,
        out_shape=jax.ShapeDtypeStruct(shape, BF16),
        scratch_shapes=[pltpu.VMEM(longer_shape, BF16), pltpu.VMEM(sums, F32), DMA((3,))],
        compiler_params=params(12),
    )(cot, above, below, held, early_centre)
    early, gathered = lax.optimization_barrier((early, gathered))
    incoming = moved(early, -1, 0)
    own, longer, stats = pl.pallas_call(
        own_kernel,
        in_specs=[HBM, WHOLE, WHOLE, HBM, HBM, HBM, WHOLE, WHOLE, WHOLE],
        out_specs=[WHOLE, HBM, WHOLE],
        out_shape=[f32_block, pltpu.HBM(longer_shape, BF16), jax.ShapeDtypeStruct((2, 8, chans), F32)],
        scratch_shapes=[
            pltpu.VMEM(longer_shape, BF16),
            pltpu.VMEM((2, 3, 3, chans, chans), BF16),
            pltpu.VMEM(sums, F32),
            pltpu.VMEM(shape, F32),
            pltpu.VMEM(shape, BF16),
            pltpu.VMEM(longer_shape, BF16),
            DMA((2, 3)),
            DMA((3,)),
            DMA,
            DMA,
            DMA((frames,)),
        ],
        compiler_params=params(28),
    )(cot, above, below, taps, in_hbm(own_centre), act, gathered, gain, shift)
    longer, incoming = lax.optimization_barrier((longer, incoming))
    prior = moved(longer, 1, 0)
    pre_grad, pay = pl.pallas_call(
        point_kernel,
        in_specs=[WHOLE] * 7,
        out_specs=[HBM, WHOLE],
        out_shape=[pltpu.HBM(shape, F32), gathered_shape],
        scratch_shapes=[pltpu.VMEM(shape, F32), DMA((frames, rows))],
        compiler_params=params(16),
    )(own, incoming, early, activations, stats, gain, shift)
    gathered = lax.all_to_all(pay, BOTH, 0, 0, tiled=True)
    output = pl.pallas_call(
        conv_kernel,
        in_specs=[HBM, ANY, HBM],
        out_specs=WHOLE,
        out_shape=jax.ShapeDtypeStruct(shape, BF16),
        scratch_shapes=[
            pltpu.VMEM((frames + 2, rows + 2, cols, chans), BF16),
            pltpu.VMEM((frames, rows, cols, 9 * chans), BF16),
            pltpu.VMEM((3, 3, 3, chans, chans), BF16),
            pltpu.VMEM(sums, F32),
            DMA((1 + frames,)),
            DMA((3,)),
        ],
        compiler_params=params(36),
    )(in_hbm(longer), prior, taps)
    output, gathered = lax.optimization_barrier((output, gathered))
    input_grad = pl.pallas_call(
        final_kernel,
        in_specs=[WHOLE] * 5,
        out_specs=WHOLE,
        out_shape=jax.ShapeDtypeStruct(shape, BF16),
        compiler_params=params(16),
    )(pre_grad, activations, gathered, stats, gain)
    return (output, input_grad)


def solution(mesh):
    placed = (P("ta", "ha", None, None), P(), P(), P(), P("ta", "ha", None, None))
    return jax.shard_map(
        on_device,
        mesh=mesh,
        in_specs=placed,
        out_specs=(P("ta", "ha", None, None), P("ta", "ha", None, None)),
        check_vma=False,
    )
```

time: 84.2 us -> 76.4 us (0.907); the launches traced: 83.9 us -> 75.2 us
  waiting for transfers between devices: 7.18 us -> 3.2 us
  local copies, waits for them, and re-layouts: 3.47 us -> 0.02 us
  starting transfers between devices: 35.1 us -> 33 us
    ppermute x4, waiting for transfers between devices: 7.17 us -> 3.19 us  [moved(): return lax.ppermute(value, BOTH, pairs)]
    unnamed x14 -> x8, local copies, waits for them, and re-layouts: 3.47 us -> 0.02 us
    ppermute x4, starting transfers between devices: 12.9 us -> 10.8 us  [moved(): return lax.ppermute(value, BOTH, pairs)]
    pallas_call x4 -> x5, Pallas kernels: 33 us -> 33.8 us  [the longest x1 13.4 us: on_device(): pl.pallas_call(conv_kernel, in_specs=[HBM, ANY, HBM], out_specs=WHOLE, ou...]
  transfers between devices with their start and end apart: 6 -> 6, of which waited for: 3 -> 2; matrix products, arithmetic and copies ran while one was open for 0% -> 0% of each run, Pallas kernels for 39% -> 45%
where the time goes in v3:
time: 76.4 us; the launch traced here: 75.2 us
  Pallas kernels  38.2 us (50%)
  starting transfers between devices  33 us (43%)
  waiting for transfers between devices  3.2 us (4%)
  between operations  0.82 us (1%)
    all_to_all x2, starting transfers between devices, on_device(): gathered = lax.all_to_all(pay, BOTH, 0, 0, tiled=True)  22.2 us
    pallas_call x1, Pallas kernels, on_device(): pl.pallas_call(conv_kernel, in_specs=[HBM, ANY, HBM], out_specs=WHOLE, ou...  13.4 us
    ppermute x4, starting transfers between devices, moved(): return lax.ppermute(value, BOTH, pairs)  10.8 us
    pallas_call x1, Pallas kernels, on_device(): pl.pallas_call(own_kernel, in_specs=[HBM, WHOLE, WHOLE, HBM, HBM, HBM, WH...  7.11 us
    pallas_call x1, Pallas kernels, on_device(): pl.pallas_call(centre_kernel, in_specs=[HBM] * 2, out_specs=[WHOLE, WHOLE...  5.66 us
    pallas_call x1, Pallas kernels, on_device(): pl.pallas_call(early_kernel, in_specs=[HBM, WHOLE, WHOLE, WHOLE, WHOLE],...  4.45 us
    ppermute x4, waiting for transfers between devices, moved(): return lax.ppermute(value, BOTH, pairs)  3.19 us
    pallas_call x1, Pallas kernels, on_device(): pl.pallas_call(point_kernel, in_specs=[WHOLE] * 7, out_specs=[HBM, WHOLE]...  3.13 us
  transfers between devices with their start and end apart: 6, of which 2 were waited for; matrix products, arithmetic and copies ran while one was open for 0% of the time, Pallas kernels for 45%

profile of v3, /device:TPU:1, one launch (start us, length us, event | category | flops | bytes accessed | tf_op | source)
XLA Modules:
  0.0 75.2 jit_solution(10952423973337551912)
XLA Ops:
  0.6 3.0 %shard_map.68 = (f32[128,128]{1,0:T(8,128)}, bf16[2,2,160,512]{3,2,1,0:T(8,128)(2,1)S(1)}, bf16[2,2,160,512]{3,2,1,0:T(8,128)(2,1)S(1)}) custom-call(bf16[2,2,160,512]{3,2,1,0:T(8,128)(2,1)} %act.7, bf16[2,2,160,512]{3,2,1,0:T(8,128)(2,1)} %cot.7), custom_call_target="tpu_custom_call" | custom-call | tf_op jit(solution)/shard_map/pallas_call | solution.py:352
  3.7 4.4 %collective-permute-start = (bf16[2,2,160,512]{3,2,1,0:T(8,128)(2,1)S(1)}, bf16[2,2,160,512]{3,2,1,0:T(8,128)(2,1)S(1)}, u32[]{:S(2)}, u32[]{:S(2)}) collective-permute-start(bf16[2,2,160,512]{3,2,1,0:T(8,128)(2,1)S(1)} %get-tuple-element.19), channel_id=1, source_target_pairs={{0,1},{1,2},{2,3},{3,4},{4,5},{5,6},{6,7},{7,8},{8,9},{9,10},{10,1... | collective-permute-start | bytes 1966088 | tf_op jit(solution)/shard_map/ppermute | solution.py:330
  8.1 1.3 %collective-permute-start.1 = (bf16[2,2,160,512]{3,2,1,0:T(8,128)(2,1)S(1)}, bf16[2,2,160,512]{3,2,1,0:T(8,128)(2,1)S(1)}, u32[]{:S(2)}, u32[]{:S(2)}) collective-permute-start(bf16[2,2,160,512]{3,2,1,0:T(8,128)(2,1)S(1)} %get-tuple-element.20), channel_id=1, source_target_pairs={{1,0},{2,1},{3,2},{4,3},{5,4},{6,5},{7,6},{8,7},{9,8},{10,9},{11,1... | collective-permute-start | bytes 1966088 | tf_op jit(solution)/shard_map/ppermute | solution.py:330
  9.4 11.6 %all-to-all-start = ((f32[128,1,128]{2,1,0:T(1,128)}), f32[128,1,128]{2,1,0:T(1,128)S(1)}, u32[]{:S(2)}, u32[]{:S(2)}) async-start(f32[128,1,128]{2,1,0:T(1,128)} %bitcast.1), calls=%async_computation | async-start | bytes 131072 | tf_op jit(solution)/shard_map/all_to_all | solution.py:362
  21.0 5.7 %shard_map.69 = (bf16[3,3,3,512,512]{4,3,2,1,0:T(8,128)(2,1)S(1)}, f32[2,2,160,512]{3,2,1,0:T(8,128)S(1)}, f32[2,2,160,512]{3,2,1,0:T(8,128)}) custom-call(bf16[2,2,160,512]{3,2,1,0:T(8,128)(2,1)} %cot.7, bf16[3,3,3,512,512]{4,3,2,1,0:T(8,128)(2,1)} %weight.5), custom_call_target="tpu_custom_call" | custom-call | tf_op jit(solution)/shard_map/pallas_call | solution.py:366
  26.7 0.0 collective-permute-done.above
  26.7 0.0 collective-permute-done.1.below
  26.7 0.0 copy-start.2
  26.7 0.0 copy-start.3
  26.8 4.4 %shard_map.70.early = bf16[2,2,160,512]{3,2,1,0:T(8,128)(2,1)S(1)} custom-call(bf16[2,2,160,512]{3,2,1,0:T(8,128)(2,1)} %cot.7, bf16[2,2,160,512]{3,2,1,0:T(8,128)(2,1)S(1)} %collective-permute-done.above, bf16[2,2,160,512]{3,2,1,0:T(8,128)(2,1)S(1)} %collective-permute-done.1.below, bf16[3,3,3,512,512]{4,3,2,1,0:T(8,128)(2,1)S(1)} %get-tuple-element.22.taps, ...), custom_call_target="tpu_custom_call" | custom-call | tf_op jit(solution)/shard_map/pallas_call | solution.py:382
  31.2 0.0 all-to-all-done
  31.2 3.0 %collective-permute-start.2 = (bf16[2,2,160,512]{3,2,1,0:T(8,128)(2,1)S(1)}, bf16[2,2,160,512]{3,2,1,0:T(8,128)(2,1)S(1)}, u32[]{:S(2)}, u32[]{:S(2)}) collective-permute-start(bf16[2,2,160,512]{3,2,1,0:T(8,128)(2,1)S(1)} %shard_map.70.early), channel_id=1, source_target_pairs={{16,0},{17,1},{18,2},{19,3},{20,4},{21,5},{22,6},{23,7},{24,8},{25... | collective-permute-start | bytes 1966088 | tf_op jit(solution)/shard_map/ppermute | solution.py:330
  34.2 0.0 copy-done.2
  34.2 0.0 copy-done.3
  34.2 0.0 copy-start
  34.2 7.1 %shard_map.71 = (f32[2,2,160,512]{3,2,1,0:T(8,128)S(1)}, bf16[2,4,160,512]{3,2,1,0:T(8,128)(2,1)}, f32[2,8,512]{2,1,0:T(8,128)S(1)}) custom-call(bf16[2,2,160,512]{3,2,1,0:T(8,128)(2,1)} %cot.7, bf16[2,2,160,512]{3,2,1,0:T(8,128)(2,1)S(1)} %collective-permute-done.above, bf16[2,2,160,512]{3,2,1,0:T(8,128)(2,1)S(1)} %collective-permute-done.1.below, ...), custom_call_target="tpu_custom_call" | custom-call | tf_op jit(solution)/shard_map/pallas_call | solution.py:392
  41.4 2.3 %collective-permute-done.2.incoming = bf16[2,2,160,512]{3,2,1,0:T(8,128)(2,1)S(1)} collective-permute-done((bf16[2,2,160,512]{3,2,1,0:T(8,128)(2,1)S(1)}, bf16[2,2,160,512]{3,2,1,0:T(8,128)(2,1)S(1)}, u32[]{:S(2)}, u32[]{:S(2)}) %collective-permute-start.2) | collective-permute-done | bytes 655392 | tf_op jit(solution)/shard_map/ppermute | solution.py:330
  43.6 2.1 %collective-permute-start.3 = (bf16[2,4,160,512]{3,2,1,0:T(8,128)(2,1)}, bf16[2,4,160,512]{3,2,1,0:T(8,128)(2,1)S(1)}, u32[]{:S(2)}, u32[]{:S(2)}) collective-permute-start(bf16[2,4,160,512]{3,2,1,0:T(8,128)(2,1)} %get-tuple-element.28.longer), channel_id=1, source_target_pairs={{0,16},{1,17},{2,18},{3,19},{4,20},{5,21},{6,22},{7,23},{8,24},{9,... | collective-permute-start | bytes 3932168 | tf_op jit(solution)/shard_map/ppermute | solution.py:330
  45.7 0.0 copy-done
  45.7 3.1 %shard_map.73 = (f32[2,2,160,512]{3,2,1,0:T(8,128)}, f32[128,128]{1,0:T(8,128)}) custom-call(f32[2,2,160,512]{3,2,1,0:T(8,128)S(1)} %get-tuple-element.29.own, bf16[2,2,160,512]{3,2,1,0:T(8,128)(2,1)S(1)} %collective-permute-done.2.incoming, bf16[2,2,160,512]{3,2,1,0:T(8,128)(2,1)S(1)} %shard_map.70.early, bf16[2,2,160,512]{3,2,1,0:T(8,128)(2,1)S(1)} %copy-done, ...), custom_call_target="tpu_custom_call" | custom-call | tf_op jit(solution)/shard_map/pallas_call | solution.py:414
  48.9 10.6 %all-to-all-start.1 = ((f32[128,1,128]{2,1,0:T(1,128)}), f32[128,1,128]{2,1,0:T(1,128)S(1)}, u32[]{:S(2)}, u32[]{:S(2)}) async-start(f32[128,1,128]{2,1,0:T(1,128)} %bitcast.6), calls=%async_computation.1 | async-start | bytes 131072 | tf_op jit(solution)/shard_map/all_to_all | solution.py:422
  59.5 0.0 copy-start.1
  59.5 0.9 %collective-permute-done.3.prior = bf16[2,4,160,512]{3,2,1,0:T(8,128)(2,1)S(1)} collective-permute-done((bf16[2,4,160,512]{3,2,1,0:T(8,128)(2,1)}, bf16[2,4,160,512]{3,2,1,0:T(8,128)(2,1)S(1)}, u32[]{:S(2)}, u32[]{:S(2)}) %collective-permute-start.3) | collective-permute-done | bytes 1310752 | tf_op jit(solution)/shard_map/ppermute | solution.py:330
  60.4 13.4 %shard_map.72 = bf16[2,2,160,512]{3,2,1,0:T(8,128)(2,1)} custom-call(bf16[2,4,160,512]{3,2,1,0:T(8,128)(2,1)} %get-tuple-element.28.longer, bf16[2,4,160,512]{3,2,1,0:T(8,128)(2,1)S(1)} %collective-permute-done.3.prior, bf16[3,3,3,512,512]{4,3,2,1,0:T(8,128)(2,1)} %weight.5), custom_call_target="tpu_custom_call" | custom-call | tf_op jit(solution)/shard_map/pallas_call | solution.py:423
  73.8 0.0 all-to-all-done.1
  73.8 0.0 copy-done.1
  73.8 1.4 %shard_map.74 = bf16[2,2,160,512]{3,2,1,0:T(8,128)(2,1)} custom-call(f32[2,2,160,512]{3,2,1,0:T(8,128)S(1)} %copy-done.1, bf16[2,2,160,512]{3,2,1,0:T(8,128)(2,1)S(1)} %copy-done, f32[128,128]{1,0:T(8,128)S(1)} %bitcast.11, f32[2,8,512]{2,1,0:T(8,128)S(1)} %get-tuple-element.31.stats, f32[1,512]{1,0:T(1,128)S(1)} %bitcast.14), custom_call_target="tpu_custom_call" | custom-call | tf_op jit(solution)/shard_map/pallas_call | solution.py:439
Async XLA Ops:
  3.7 23.0 %collective-permute-start = (bf16[2,2,160,512]{3,2,1,0:T(8,128)(2,1)S(1)}, bf16[2,2,160,512]{3,2,1,0:T(8,128)(2,1)S(1)}, u32[]{:S(2)}, u32[]{:S(2)}) collective-permute-start(bf16[2,2,160,512]{3,2,1,0:T(8,128)(2,1)S(1)} %get-tuple-element.19), channel_id=1, source_target_pairs={{0,1},{1,2},{2,3},{3,4},{4,5},{5,6},{6,7},{7,8},{8,9},{9,10},{10,1... | collective-permute-start | bytes 1966088 | tf_op jit(solution)/shard_map/ppermute | solution.py:330
  8.1 18.6 %collective-permute-start.1 = (bf16[2,2,160,512]{3,2,1,0:T(8,128)(2,1)S(1)}, bf16[2,2,160,512]{3,2,1,0:T(8,128)(2,1)S(1)}, u32[]{:S(2)}, u32[]{:S(2)}) collective-permute-start(bf16[2,2,160,512]{3,2,1,0:T(8,128)(2,1)S(1)} %get-tuple-element.20), channel_id=1, source_target_pairs={{1,0},{2,1},{3,2},{4,3},{5,4},{6,5},{7,6},{8,7},{9,8},{10,9},{11,1... | collective-permute-start | bytes 1966088 | tf_op jit(solution)/shard_map/ppermute | solution.py:330
  9.4 21.8 %all-to-all-start = ((f32[128,1,128]{2,1,0:T(1,128)}), f32[128,1,128]{2,1,0:T(1,128)S(1)}, u32[]{:S(2)}, u32[]{:S(2)}) async-start(f32[128,1,128]{2,1,0:T(1,128)} %bitcast.1), calls=%async_computation | async-start | bytes 131072 | tf_op jit(solution)/shard_map/all_to_all | solution.py:362
  26.7 7.5 %copy-start.2 = (f32[512]{0:T(512)S(1)}, f32[512]{0:T(512)}, u32[]{:S(2)}) copy-start(f32[512]{0:T(512)} %param.6) | copy-start | bytes 6148
  26.7 7.5 %copy-start.3 = (f32[512]{0:T(512)S(1)}, f32[512]{0:T(512)}, u32[]{:S(2)}) copy-start(f32[512]{0:T(512)} %param.7) | copy-start | bytes 6148
  31.2 12.4 %collective-permute-start.2 = (bf16[2,2,160,512]{3,2,1,0:T(8,128)(2,1)S(1)}, bf16[2,2,160,512]{3,2,1,0:T(8,128)(2,1)S(1)}, u32[]{:S(2)}, u32[]{:S(2)}) collective-permute-start(bf16[2,2,160,512]{3,2,1,0:T(8,128)(2,1)S(1)} %shard_map.70.early), channel_id=1, source_target_pairs={{16,0},{17,1},{18,2},{19,3},{20,4},{21,5},{22,6},{23,7},{24,8},{25... | collective-permute-start | bytes 1966088 | tf_op jit(solution)/shard_map/ppermute | solution.py:330
  34.2 11.5 %copy-start = (bf16[2,2,160,512]{3,2,1,0:T(8,128)(2,1)S(1)}, bf16[2,2,160,512]{3,2,1,0:T(8,128)(2,1)}, u32[]{:S(2)}) copy-start(bf16[2,2,160,512]{3,2,1,0:T(8,128)(2,1)} %act.7) | copy-start | bytes 1966084
  43.6 16.8 %collective-permute-start.3 = (bf16[2,4,160,512]{3,2,1,0:T(8,128)(2,1)}, bf16[2,4,160,512]{3,2,1,0:T(8,128)(2,1)S(1)}, u32[]{:S(2)}, u32[]{:S(2)}) collective-permute-start(bf16[2,4,160,512]{3,2,1,0:T(8,128)(2,1)} %get-tuple-element.28.longer), channel_id=1, source_target_pairs={{0,16},{1,17},{2,18},{3,19},{4,20},{5,21},{6,22},{7,23},{8,24},{9,... | collective-permute-start | bytes 3932168 | tf_op jit(solution)/shard_map/ppermute | solution.py:330
  48.9 24.9 %all-to-all-start.1 = ((f32[128,1,128]{2,1,0:T(1,128)}), f32[128,1,128]{2,1,0:T(1,128)S(1)}, u32[]{:S(2)}, u32[]{:S(2)}) async-start(f32[128,1,128]{2,1,0:T(1,128)} %bitcast.6), calls=%async_computation.1 | async-start | bytes 131072 | tf_op jit(solution)/shard_map/all_to_all | solution.py:422
  59.5 14.3 %copy-start.1 = (f32[2,2,160,512]{3,2,1,0:T(8,128)S(1)}, f32[2,2,160,512]{3,2,1,0:T(8,128)}, u32[]{:S(2)}) copy-start(f32[2,2,160,512]{3,2,1,0:T(8,128)} %get-tuple-element.34.pre_grad) | copy-start | bytes 3932164

commit v4 on v3

--- a/solution.py
+++ b/solution.py
@@ -20,57 +20,69 @@
     return pltpu.CompilerParams(vmem_limit_bytes=mebibytes * 2**20)
 
 
-def member(chans, offset, across):
+def member(chans, across):
     shape, chan_dim = ((LANES, chans), 1) if across else ((chans, LANES), 0)
     per_group = chans // GROUPS
     chan = lax.broadcasted_iota(jnp.int32, shape, chan_dim)
-    lane = lax.broadcasted_iota(jnp.int32, shape, 1 - chan_dim) - offset
+    lane = lax.broadcasted_iota(jnp.int32, shape, 1 - chan_dim)
     inside = (chan >= lane * per_group) & (chan < (lane + 1) * per_group)
-    return jnp.where(inside & (lane >= 0) & (lane < GROUPS), 1.0, 0.0).astype(F32)
+    return jnp.where(inside, 1.0, 0.0).astype(BF16)
 
 
 def exact_dot(left, right):
-    return jnp.dot(left, right, precision=lax.Precision.HIGHEST, preferred_element_type=F32)
-
-
-def to_groups(by_chan, offset):
-    lanes = exact_dot(by_chan, member(by_chan.shape[1], offset, False))
-    return jnp.sum(lanes, axis=0, keepdims=True)
-
-
-def to_chans(by_group, chans, offset):
-    rows = jnp.broadcast_to(by_group, (8, LANES))
-    return exact_dot(rows, member(chans, offset, True))
+    high = left.astype(BF16).astype(F32)
+    rest = left - high
+    middle = rest.astype(BF16).astype(F32)
+    parts = jnp.concatenate([high, middle, rest - middle], axis=0).astype(BF16)
+    out = jnp.dot(parts, right, preferred_element_type=F32)
+    rows = left.shape[0]
+    return out[2 * rows :] + out[rows : 2 * rows] + out[:rows]
+
+
+def to_groups(one, two):
+    lanes = exact_dot(jnp.concatenate([one, two], axis=0), member(one.shape[1], False))
+    return jnp.sum(lanes[:8] + pltpu.roll(lanes[8:], GROUPS, 1), axis=0, keepdims=True)
+
+
+def to_chans(one, two, chans):
+    rows = jnp.concatenate([jnp.broadcast_to(one, (8, LANES)), jnp.broadcast_to(two, (8, LANES))], axis=0)
+    out = exact_dot(rows, member(chans, True))
+    return out[:8], out[8:]
+
+
+def second_part(row):
+    return pltpu.roll(jnp.broadcast_to(row, (8, LANES)), LANES - GROUPS, 1)[:1]
 
 
 def eights(value):
     return value.reshape(value.shape[0] // 8, 8, value.shape[1])
 
 
-def stats_kernel(act, cot, pay, up, down, block, load_sem, pack_sem):
-    frames, rows, cols, chans = block.shape
-    load = pltpu.make_async_copy(act, block, load_sem)
-    load.start()
-    packs = []
-    for i, source in enumerate((act, cot)):
-        packs.append(pltpu.make_async_copy(source.at[:, rows - 1], up.at[i], pack_sem.at[2 * i]))
-        packs.append(pltpu.make_async_copy(source.at[:, 0], down.at[i], pack_sem.at[2 * i + 1]))
+def stats_kernel(act, cot, pay, up, down, act_sem, cot_sem):
+    frames, rows, cols, chans = act.shape
+    sides = ((0, down), (rows - 1, up))
+    loads = []
+    for t in range(frames):
+        for n, (h, side) in enumerate(sides):
+            loads.append(pltpu.make_async_copy(act.at[t, h], side.at[0, t], act_sem.at[t, n]))
+            loads[-1].start()
+    packs = [pltpu.make_async_copy(cot.at[:, h], side.at[1], cot_sem.at[n]) for n, (h, side) in enumerate(sides)]
     for pack in packs:
         pack.start()
-    load.wait()
+    blocks = [(t, side) for t in range(frames) for _, side in sides]
     entries = frames * rows * cols * (chans // GROUPS)
-    total = jnp.zeros((8, chans), F32)
-    for t in range(frames):
-        for h in range(rows):
-            total = total + jnp.sum(eights(block[t, h].astype(F32)), axis=0)
-    sums = to_groups(total, 0)
-    mean = to_chans(sums / entries, chans, 0)
-    spread = jnp.zeros((8, chans), F32)
-    for t in range(frames):
-        for h in range(rows):
-            centered = eights(block[t, h].astype(F32)) - mean[None]
-            spread = spread + jnp.sum(centered * centered, axis=0)
-    row = sums + to_groups(spread, GROUPS)
+    none = jnp.zeros((8, chans), F32)
+    total = none
+    for load, (t, side) in zip(loads, blocks):
+        load.wait()
+        total = total + jnp.sum(eights(side[0, t].astype(F32)), axis=0)
+    sums = to_groups(total, none)
+    mean, _ = to_chans(sums / entries, sums, chans)
+    spread = none
+    for t, side in blocks:
+        centered = eights(side[0, t].astype(F32)) - mean[None]
+        spread = spread + jnp.sum(centered * centered, axis=0)
+    row = sums + to_groups(none, spread)
     pay[...] = jnp.broadcast_to(row, pay.shape)
     for pack in packs:
         pack.wait()
@@ -117,17 +129,14 @@
     return lax.dot_general(left, right, (((1,), (1,)), ((), ())), preferred_element_type=F32)
 
 
-def grad_products(full, part, source, target, ext, taps, acc, fetches=None):
-    rows, cols, chans = ext.shape[1] - 2, ext.shape[2], ext.shape[3]
-    half = rows * cols
-    for b in (0, 2):
-        both = ext[:, 2 - b : 2 - b + rows].reshape(2 * half, chans)
-        one = ext[source, 2 - b : 2 - b + rows].reshape(half, chans)
-        if fetches:
-            fetches.pop(0).wait()
-            fetches.pop(0).wait()
-            for fetch in fetches:
-                fetch.start()
+def grad_products(full, part, source, target, lefts, taps, acc, before=None):
+    half = lefts[0].shape[1] * lefts[0].shape[2]
+    chans = lefts[0].shape[3]
+    for n, b in enumerate((0, 2)):
+        if before is not None:
+            before(n)
+        both = lefts[n][...].reshape(2 * half, chans)
+        one = lefts[n][source].reshape(half, chans)
         for c in range(3):
             term = transposed_dot(both, taps[full, b, c])
             if b == 0:
@@ -137,40 +146,33 @@
             acc[c, target * half : (target + 1) * half] += transposed_dot(one, taps[part, b, c])
 
 
-def halo_copies(cot, above, below, ext, sem):
-    rows = cot.shape[1]
-    return [
-        pltpu.make_async_copy(cot, ext.at[:, 1 : rows + 1], sem.at[0]),
-        pltpu.make_async_copy(above.at[1], ext.at[:, 0], sem.at[1]),
-        pltpu.make_async_copy(below.at[1], ext.at[:, rows + 1], sem.at[2]),
-    ]
-
-
-def early_kernel(cot, above, below, taps, centre, out, ext, acc, ext_sem):
-    loads = halo_copies(cot, above, below, ext, ext_sem)
-    for load in loads:
-        load.start()
-    for load in loads:
-        load.wait()
-    grad_products(0, 1, 0, 1, ext, taps, acc)
+def fill_lefts(cot, above, below, lefts):
+    for t in range(cot.shape[0]):
+        lefts[0, t, 0] = cot[t, 1]
+        lefts[0, t, 1] = below[1, t]
+        lefts[1, t, 0] = above[1, t]
+        lefts[1, t, 1] = cot[t, 0]
+
+
+def early_kernel(cot, above, below, taps, centre, out, lefts, acc):
+    fill_lefts(cot, above, below, lefts)
+    grad_products(0, 1, 0, 1, (lefts.at[0], lefts.at[1]), taps, acc)
     combine(acc, out, 2, 0, centre)
 
 
-def own_kernel(cot, above, below, weight, centre, act, gathered, gain, shift, out, longer, stats, ext, taps, acc, more, raw, acts, tap_sem, ext_sem, more_sem, raw_sem, acts_sem):
+def own_kernel(cot, above, below, weight, centre, act, gathered, gain, shift, out, longer, stats, lefts, taps, acc, more, raw, block, acts, tap_sem, more_sem, raw_sem, block_sem, acts_sem):
     frames, rows, cols, chans = act.shape
     load_act = pltpu.make_async_copy(act, raw, raw_sem)
     load_act.start()
-    loads = halo_copies(cot, above, below, ext, ext_sem)
-    loads.append(pltpu.make_async_copy(centre, more, more_sem))
-    for load in loads:
-        load.start()
+    load_cot = pltpu.make_async_copy(cot, block, block_sem)
+    load_cot.start()
     fetches = [
-        pltpu.make_async_copy(weight.at[a, b], taps.at[a - 1, b], tap_sem.at[a - 1, b])
+        [pltpu.make_async_copy(weight.at[a, b], taps.at[a - 1, b], tap_sem.at[a - 1, b]) for a in (2, 1)]
         for b in (0, 2)
-        for a in (2, 1)
     ]
-    fetches[0].start()
-    fetches[1].start()
+    for fetch in fetches[0]:
+        fetch.start()
+    load_more = pltpu.make_async_copy(centre, more, more_sem)
     entries = frames * rows * cols * (chans // GROUPS)
     mean, rstd = group_stats(gathered[...], entries, chans)
     stats[0] = mean
@@ -202,9 +204,19 @@
             activate(raw[t, h], t, 1 + h)
         sends.append(pltpu.make_async_copy(acts.at[t], longer.at[t], acts_sem.at[t]))
         sends[t].start()
-    for load in loads:
-        load.wait()
-    grad_products(1, 0, 1, 0, ext, taps, acc, fetches)
+    load_cot.wait()
+    fill_lefts(block, above, below, lefts)
+
+    def before(n):
+        for fetch in fetches[n]:
+            fetch.wait()
+        if n == 0:
+            for fetch in fetches[1]:
+                fetch.start()
+            load_more.start()
+
+    grad_products(1, 0, 1, 0, (lefts.at[0], lefts.at[1]), taps, acc, before)
+    load_more.wait()
     combine(acc, out, 2, 0, more)
     for send in sends:
         send.wait()
@@ -231,8 +243,10 @@
     mean = sums / count
     apart = gathered * (1.0 / entries) - mean
     between = jnp.sum(apart * apart, axis=0, keepdims=True) * entries
-    spread = to_chans(between, chans, 0) + to_chans(sums, chans, GROUPS)
-    return to_chans(mean, chans, 0), lax.rsqrt(spread / count + 1e-06)
+    var = (between + second_part(sums)) / count
+    lane = lax.broadcasted_iota(jnp.int32, (1, LANES), 1)
+    rstd = jnp.where(lane < GROUPS, lax.rsqrt(jnp.where(lane < GROUPS, var, 1.0) + 1e-06), 0.0)
+    return to_chans(mean, rstd, chans)
 
 
 def point_kernel(own, incoming, early, act, stats, gain, shift, pre_grad, pay, block, block_sem):
@@ -259,17 +273,21 @@
             gain_sum = gain_sum + jnp.sum(local * normed, axis=0)
             sends.append(pltpu.make_async_copy(block.at[t, h], pre_grad.at[t, h], block_sem.at[t, h]))
             sends[-1].start()
-    row = to_groups(gains * shift_sum, 0) + to_groups(gains * gain_sum, GROUPS)
+    row = to_groups(gains * shift_sum, gains * gain_sum)
     pay[...] = jnp.broadcast_to(row, pay.shape)
     for send in sends:
         send.wait()
 
 
-def conv_kernel(longer, prior, weight, out, ext, wide, taps, acc, ext_sem, tap_sem):
+def conv_kernel(longer, prior, weight, out, ext, near, far, near_taps, far_taps, acc, ext_sem, near_sem, far_sem):
     frames, rows, cols, chans = out.shape
+    positions = frames * rows * cols
     first = lax.axis_index("ta") == 0
     own = pltpu.make_async_copy(longer, ext.at[frames:], ext_sem.at[0])
     own.start()
+    fetches = [pltpu.make_async_copy(weight.at[2, :, c], near_taps.at[c], near_sem.at[c]) for c in range(3)]
+    fetches += [pltpu.make_async_copy(weight.at[0:2, :, c], far_taps.at[c], far_sem.at[c]) for c in range(3)]
+    fetches[0].start()
 
     @pl.when(first)
     def _():
@@ -281,26 +299,27 @@
         for t in range(frames):
             pltpu.make_async_copy(prior.at[t], ext.at[t], ext_sem.at[1 + t]).start()
 
-    fetches = [pltpu.make_async_copy(weight.at[:, :, c], taps.at[c], tap_sem.at[c]) for c in range(3)]
-    fetches[0].start()
-
-    def widen(a):
+    fetches[1].start()
+    own.wait()
+    for b in range(3):
+        near[:, :, :, b * chans : (b + 1) * chans] = ext[2 : 2 + frames, b : b + rows]
+    left = near[...].reshape(positions, 3 * chans)
+    for c in range(3):
+        fetches[c].wait()
+        fetches[c + 2].start()
+        acc[c] = jnp.dot(left, near_taps[c].reshape(3 * chans, chans), preferred_element_type=F32)
+    for t in range(frames):
+        pltpu.make_async_copy(prior.at[t], ext.at[t], ext_sem.at[1 + t]).wait()
+    for a in range(2):
         for b in range(3):
             k = (3 * a + b) * chans
-            wide[:, :, :, k : k + chans] = ext[a : a + frames, b : b + rows]
-
-    own.wait()
-    widen(2)
-    for t in range(frames):
-        pltpu.make_async_copy(prior.at[t], ext.at[t], ext_sem.at[1 + t]).wait()
-    widen(1)
-    widen(0)
-    left = wide[...].reshape(frames * rows * cols, 9 * chans)
+            far[:, :, :, k : k + chans] = ext[a : a + frames, b : b + rows]
+    left = far[...].reshape(positions, 6 * chans)
     for c in range(3):
-        fetches[c].wait()
-        if c < 2:
-            fetches[c + 1].start()
-        acc[c] = jnp.dot(left, taps[c].reshape(9 * chans, chans), preferred_element_type=F32)
+        fetches[3 + c].wait()
+        if c == 0:
+            fetches[5].start()
+        acc[c] += jnp.dot(left, far_taps[c].reshape(6 * chans, chans), preferred_element_type=F32)
     combine(acc, out, 0, 2, None)
 
 
@@ -308,8 +327,7 @@
     frames, rows, cols, chans = act.shape
     count = gathered.shape[0] * frames * rows * cols * (chans // GROUPS)
     sums = jnp.sum(gathered[...], axis=0, keepdims=True) / count
-    first = to_chans(sums, chans, 0)
-    second = to_chans(sums, chans, GROUPS)
+    first, second = to_chans(sums, second_part(sums), chans)
     mean, rstd = stats[0], stats[1]
     gains = jnp.broadcast_to(gain[...], (8, chans))
     for t in range(frames):
@@ -354,7 +372,7 @@
         in_specs=[HBM, HBM],
         out_specs=[WHOLE] * 3,
         out_shape=[gathered_shape, edge, edge],
-        scratch_shapes=[pltpu.VMEM(shape, BF16), DMA, DMA((4,))],
+        scratch_shapes=[DMA((frames, rows)), DMA((2,))],
         compiler_params=params(16),
     )(act, cot)
     above = moved(up, 0, 1)
@@ -363,13 +381,12 @@
 
     f32_block = jax.ShapeDtypeStruct(shape, F32)
     sums = (3, positions, chans)
-    held, early_centre, own_centre = pl.pallas_call(
+    held, early_centre, own_centre, cot_held = pl.pallas_call(
         centre_kernel,
         in_specs=[HBM] * 2,
-        out_specs=[WHOLE, WHOLE, HBM],
-        out_shape=[pltpu.VMEM(weight.shape, BF16), f32_block, pltpu.HBM(shape, F32)],
+        out_specs=[WHOLE, WHOLE, HBM, WHOLE],
+        out_shape=[pltpu.VMEM(weight.shape, BF16), f32_block, pltpu.HBM(shape, F32), jax.ShapeDtypeStruct(shape, BF16)],
         scratch_shapes=[
-            pltpu.VMEM(shape, BF16),
             pltpu.VMEM((2,) + sums, F32),
             pltpu.VMEM(shape, F32),
             DMA,
@@ -381,12 +398,12 @@
     held = in_vmem(held)
     early = pl.pallas_call(
         early_kernel,
-        in_specs=[HBM, WHOLE, WHOLE, WHOLE, WHOLE],
+        in_specs=[WHOLE] * 5,
         out_specs=WHOLE,
         out_shape=jax.ShapeDtypeStruct(shape, BF16),
-        scratch_shapes=[pltpu.VMEM(longer_shape, BF16), pltpu.VMEM(sums, F32), DMA((3,))],
-        compiler_params=params(12),
-    )(cot, above, below, held, early_centre)
+        scratch_shapes=[pltpu.VMEM((2,) + shape, BF16), pltpu.VMEM(sums, F32)],
+        compiler_params=params(16),
+    )(cot_held, above, below, held, early_centre)
     early, gathered = lax.optimization_barrier((early, gathered))
     incoming = moved(early, -1, 0)
     own, longer, stats = pl.pallas_call(
@@ -395,14 +412,15 @@
         out_specs=[WHOLE, HBM, WHOLE],
         out_shape=[f32_block, pltpu.HBM(longer_shape, BF16), jax.ShapeDtypeStruct((2, 8, chans), F32)],
         scratch_shapes=[
-            pltpu.VMEM(longer_shape, BF16),
+            pltpu.VMEM((2,) + shape, BF16),
             pltpu.VMEM((2, 3, 3, chans, chans), BF16),
             pltpu.VMEM(sums, F32),
             pltpu.VMEM(shape, F32),
             pltpu.VMEM(shape, BF16),
+            pltpu.VMEM(shape, BF16),
             pltpu.VMEM(longer_shape, BF16),
             DMA((2, 3)),
-            DMA((3,)),
+            DMA,
             DMA,
             DMA,
             DMA((frames,)),
@@ -427,10 +445,13 @@
         out_shape=jax.ShapeDtypeStruct(shape, BF16),
         scratch_shapes=[
             pltpu.VMEM((frames + 2, rows + 2, cols, chans), BF16),
-            pltpu.VMEM((frames, rows, cols, 9 * chans), BF16),
-            pltpu.VMEM((3, 3, 3, chans, chans), BF16),
+            pltpu.VMEM((frames, rows, cols, 3 * chans), BF16),
+            pltpu.VMEM((frames, rows, cols, 6 * chans), BF16),
+            pltpu.VMEM((3, 3, chans, chans), BF16),
+            pltpu.VMEM((3, 2, 3, chans, chans), BF16),
             pltpu.VMEM(sums, F32),
             DMA((1 + frames,)),
+            DMA((3,)),
             DMA((3,)),
         ],
         compiler_params=params(36),

time: 76.4 us -> 74.6 us (0.976)
  Pallas kernels: 38.2 us -> 35.8 us
  waiting for transfers between devices: 3.2 us -> 3.99 us
    pallas_call x1, Pallas kernels: 4.45 us -> 3.32 us  [on_device(): pl.pallas_call(early_kernel, in_specs=[WHOLE] * 5, out_specs=WHOLE, out_s...]
  transfers between devices with their start and end apart: 6 -> 6, of which waited for: 2 -> 3; matrix products, arithmetic and copies ran while one was open for 0% -> 0% of each run, Pallas kernels for 45% -> 43%
where the time goes in v4:
time: 74.6 us; the launch traced here: 73.5 us
  Pallas kernels  35.8 us (48%)
  starting transfers between devices  32.9 us (44%)
  waiting for transfers between devices  3.99 us (5%)
  between operations  0.81 us (1%)
    all_to_all x2, starting transfers between devices, on_device(): gathered = lax.all_to_all(pay, BOTH, 0, 0, tiled=True)  22.2 us
    pallas_call x1, Pallas kernels, on_device(): pl.pallas_call(conv_kernel, in_specs=[HBM, ANY, HBM], out_specs=WHOLE, ou...  13.1 us
    ppermute x4, starting transfers between devices, moved(): return lax.ppermute(value, BOTH, pairs)  10.7 us
    pallas_call x1, Pallas kernels, on_device(): pl.pallas_call(own_kernel, in_specs=[HBM, WHOLE, WHOLE, HBM, HBM, HBM, WH...  6.65 us
    pallas_call x1, Pallas kernels, on_device(): pl.pallas_call(centre_kernel, in_specs=[HBM] * 2, out_specs=[WHOLE, WHOLE...  5.66 us
    ppermute x4, waiting for transfers between devices, moved(): return lax.ppermute(value, BOTH, pairs)  3.53 us
    pallas_call x1, Pallas kernels, on_device(): pl.pallas_call(early_kernel, in_specs=[WHOLE] * 5, out_specs=WHOLE, out_s...  3.32 us
    pallas_call x1, Pallas kernels, on_device(): pl.pallas_call(point_kernel, in_specs=[WHOLE] * 7, out_specs=[HBM, WHOLE]...  2.92 us
  transfers between devices with their start and end apart: 6, of which 3 were waited for; matrix products, arithmetic and copies ran while one was open for 0% of the time, Pallas kernels for 43%

profile of v4, /device:TPU:1, one launch (start us, length us, event | category | flops | bytes accessed | tf_op | source)
XLA Modules:
  0.0 73.5 jit_solution(14044999129855618211)
XLA Ops:
  0.6 2.7 %shard_map.68 = (f32[128,128]{1,0:T(8,128)}, bf16[2,2,160,512]{3,2,1,0:T(8,128)(2,1)S(1)}, bf16[2,2,160,512]{3,2,1,0:T(8,128)(2,1)S(1)}) custom-call(bf16[2,2,160,512]{3,2,1,0:T(8,128)(2,1)} %act.7, bf16[2,2,160,512]{3,2,1,0:T(8,128)(2,1)} %cot.5), custom_call_target="tpu_custom_call" | custom-call | tf_op jit(solution)/shard_map/pallas_call | solution.py:370
  3.3 4.4 %collective-permute-start = (bf16[2,2,160,512]{3,2,1,0:T(8,128)(2,1)S(1)}, bf16[2,2,160,512]{3,2,1,0:T(8,128)(2,1)S(1)}, u32[]{:S(2)}, u32[]{:S(2)}) collective-permute-start(bf16[2,2,160,512]{3,2,1,0:T(8,128)(2,1)S(1)} %get-tuple-element.20), channel_id=1, source_target_pairs={{0,1},{1,2},{2,3},{3,4},{4,5},{5,6},{6,7},{7,8},{8,9},{9,10},{10,1... | collective-permute-start | bytes 1966088 | tf_op jit(solution)/shard_map/ppermute | solution.py:348
  7.7 1.3 %collective-permute-start.1 = (bf16[2,2,160,512]{3,2,1,0:T(8,128)(2,1)S(1)}, bf16[2,2,160,512]{3,2,1,0:T(8,128)(2,1)S(1)}, u32[]{:S(2)}, u32[]{:S(2)}) collective-permute-start(bf16[2,2,160,512]{3,2,1,0:T(8,128)(2,1)S(1)} %get-tuple-element.21), channel_id=1, source_target_pairs={{1,0},{2,1},{3,2},{4,3},{5,4},{6,5},{7,6},{8,7},{9,8},{10,9},{11,1... | collective-permute-start | bytes 1966088 | tf_op jit(solution)/shard_map/ppermute | solution.py:348
  9.0 11.6 %all-to-all-start = ((f32[128,1,128]{2,1,0:T(1,128)}), f32[128,1,128]{2,1,0:T(1,128)S(1)}, u32[]{:S(2)}, u32[]{:S(2)}) async-start(f32[128,1,128]{2,1,0:T(1,128)} %bitcast.1), calls=%async_computation | async-start | bytes 131072 | tf_op jit(solution)/shard_map/all_to_all | solution.py:380
  20.7 5.7 %shard_map.69 = (bf16[3,3,3,512,512]{4,3,2,1,0:T(8,128)(2,1)S(1)}, f32[2,2,160,512]{3,2,1,0:T(8,128)S(1)}, f32[2,2,160,512]{3,2,1,0:T(8,128)}, bf16[2,2,160,512]{3,2,1,0:T(8,128)(2,1)S(1)}) custom-call(bf16[2,2,160,512]{3,2,1,0:T(8,128)(2,1)} %cot.5, bf16[3,3,3,512,512]{4,3,2,1,0:T(8,128)(2,1)} %weight.5), custom_call_target="tpu_custom_call" | custom-call | tf_op jit(solution)/shard_map/pallas_call | solution.py:384
  26.3 0.0 collective-permute-done.above
  26.3 0.0 collective-permute-done.1.below
  26.4 0.0 copy-start.2
  26.4 0.0 copy-start.3
  26.4 3.3 %shard_map.70.early = bf16[2,2,160,512]{3,2,1,0:T(8,128)(2,1)S(1)} custom-call(bf16[2,2,160,512]{3,2,1,0:T(8,128)(2,1)S(1)} %get-tuple-element.23.cot, bf16[2,2,160,512]{3,2,1,0:T(8,128)(2,1)S(1)} %collective-permute-done.above, bf16[2,2,160,512]{3,2,1,0:T(8,128)(2,1)S(1)} %collective-permute-done.1.below, ...), custom_call_target="tpu_custom_call" | custom-call | tf_op jit(solution)/shard_map/pallas_call | solution.py:399
  29.7 0.5 all-to-all-done
  30.2 2.9 %collective-permute-start.2 = (bf16[2,2,160,512]{3,2,1,0:T(8,128)(2,1)S(1)}, bf16[2,2,160,512]{3,2,1,0:T(8,128)(2,1)S(1)}, u32[]{:S(2)}, u32[]{:S(2)}) collective-permute-start(bf16[2,2,160,512]{3,2,1,0:T(8,128)(2,1)S(1)} %shard_map.70.early), channel_id=1, source_target_pairs={{16,0},{17,1},{18,2},{19,3},{20,4},{21,5},{22,6},{23,7},{24,8},{25... | collective-permute-start | bytes 1966088 | tf_op jit(solution)/shard_map/ppermute | solution.py:348
  33.0 0.0 copy-done.2
  33.0 0.0 copy-done.3
  33.1 0.0 copy-start
  33.1 6.6 %shard_map.71 = (f32[2,2,160,512]{3,2,1,0:T(8,128)S(1)}, bf16[2,4,160,512]{3,2,1,0:T(8,128)(2,1)}, f32[2,8,512]{2,1,0:T(8,128)S(1)}) custom-call(bf16[2,2,160,512]{3,2,1,0:T(8,128)(2,1)} %cot.5, bf16[2,2,160,512]{3,2,1,0:T(8,128)(2,1)S(1)} %collective-permute-done.above, bf16[2,2,160,512]{3,2,1,0:T(8,128)(2,1)S(1)} %collective-permute-done.1.below, ...), custom_call_target="tpu_custom_call" | custom-call | tf_op jit(solution)/shard_map/pallas_call | solution.py:409
  39.7 2.4 %collective-permute-done.2.incoming = bf16[2,2,160,512]{3,2,1,0:T(8,128)(2,1)S(1)} collective-permute-done((bf16[2,2,160,512]{3,2,1,0:T(8,128)(2,1)S(1)}, bf16[2,2,160,512]{3,2,1,0:T(8,128)(2,1)S(1)}, u32[]{:S(2)}, u32[]{:S(2)}) %collective-permute-start.2) | collective-permute-done | bytes 655392 | tf_op jit(solution)/shard_map/ppermute | solution.py:348
  42.1 2.1 %collective-permute-start.3 = (bf16[2,4,160,512]{3,2,1,0:T(8,128)(2,1)}, bf16[2,4,160,512]{3,2,1,0:T(8,128)(2,1)S(1)}, u32[]{:S(2)}, u32[]{:S(2)}) collective-permute-start(bf16[2,4,160,512]{3,2,1,0:T(8,128)(2,1)} %get-tuple-element.30.longer), channel_id=1, source_target_pairs={{0,16},{1,17},{2,18},{3,19},{4,20},{5,21},{6,22},{7,23},{8,24},{9,... | collective-permute-start | bytes 3932168 | tf_op jit(solution)/shard_map/ppermute | solution.py:348
  44.2 0.0 copy-done
  44.2 2.9 %shard_map.73 = (f32[2,2,160,512]{3,2,1,0:T(8,128)}, f32[128,128]{1,0:T(8,128)}) custom-call(f32[2,2,160,512]{3,2,1,0:T(8,128)S(1)} %get-tuple-element.31.own, bf16[2,2,160,512]{3,2,1,0:T(8,128)(2,1)S(1)} %collective-permute-done.2.incoming, bf16[2,2,160,512]{3,2,1,0:T(8,128)(2,1)S(1)} %shard_map.70.early, bf16[2,2,160,512]{3,2,1,0:T(8,128)(2,1)S(1)} %copy-done, ...), custom_call_target="tpu_custom_call" | custom-call | tf_op jit(solution)/shard_map/pallas_call | solution.py:432
  47.2 10.6 %all-to-all-start.1 = ((f32[128,1,128]{2,1,0:T(1,128)}), f32[128,1,128]{2,1,0:T(1,128)S(1)}, u32[]{:S(2)}, u32[]{:S(2)}) async-start(f32[128,1,128]{2,1,0:T(1,128)} %bitcast.6), calls=%async_computation.1 | async-start | bytes 131072 | tf_op jit(solution)/shard_map/all_to_all | solution.py:440
  57.8 0.0 copy-start.1
  57.8 1.1 %collective-permute-done.3.prior = bf16[2,4,160,512]{3,2,1,0:T(8,128)(2,1)S(1)} collective-permute-done((bf16[2,4,160,512]{3,2,1,0:T(8,128)(2,1)}, bf16[2,4,160,512]{3,2,1,0:T(8,128)(2,1)S(1)}, u32[]{:S(2)}, u32[]{:S(2)}) %collective-permute-start.3) | collective-permute-done | bytes 1310752 | tf_op jit(solution)/shard_map/ppermute | solution.py:348
  58.9 13.1 %shard_map.72 = bf16[2,2,160,512]{3,2,1,0:T(8,128)(2,1)} custom-call(bf16[2,4,160,512]{3,2,1,0:T(8,128)(2,1)} %get-tuple-element.30.longer, bf16[2,4,160,512]{3,2,1,0:T(8,128)(2,1)S(1)} %collective-permute-done.3.prior, bf16[3,3,3,512,512]{4,3,2,1,0:T(8,128)(2,1)} %weight.5), custom_call_target="tpu_custom_call" | custom-call | tf_op jit(solution)/shard_map/pallas_call | solution.py:441
  72.0 0.0 all-to-all-done.1
  72.0 0.0 copy-done.1
  72.0 1.5 %shard_map.74 = bf16[2,2,160,512]{3,2,1,0:T(8,128)(2,1)} custom-call(f32[2,2,160,512]{3,2,1,0:T(8,128)S(1)} %copy-done.1, bf16[2,2,160,512]{3,2,1,0:T(8,128)(2,1)S(1)} %copy-done, f32[128,128]{1,0:T(8,128)S(1)} %bitcast.11, f32[2,8,512]{2,1,0:T(8,128)S(1)} %get-tuple-element.33.stats, f32[1,512]{1,0:T(1,128)S(1)} %bitcast.14), custom_call_target="tpu_custom_call" | custom-call | tf_op jit(solution)/shard_map/pallas_call | solution.py:460
Async XLA Ops:
  3.3 23.0 %collective-permute-start = (bf16[2,2,160,512]{3,2,1,0:T(8,128)(2,1)S(1)}, bf16[2,2,160,512]{3,2,1,0:T(8,128)(2,1)S(1)}, u32[]{:S(2)}, u32[]{:S(2)}) collective-permute-start(bf16[2,2,160,512]{3,2,1,0:T(8,128)(2,1)S(1)} %get-tuple-element.20), channel_id=1, source_target_pairs={{0,1},{1,2},{2,3},{3,4},{4,5},{5,6},{6,7},{7,8},{8,9},{9,10},{10,1... | collective-permute-start | bytes 1966088 | tf_op jit(solution)/shard_map/ppermute | solution.py:348
  7.7 18.6 %collective-permute-start.1 = (bf16[2,2,160,512]{3,2,1,0:T(8,128)(2,1)S(1)}, bf16[2,2,160,512]{3,2,1,0:T(8,128)(2,1)S(1)}, u32[]{:S(2)}, u32[]{:S(2)}) collective-permute-start(bf16[2,2,160,512]{3,2,1,0:T(8,128)(2,1)S(1)} %get-tuple-element.21), channel_id=1, source_target_pairs={{1,0},{2,1},{3,2},{4,3},{5,4},{6,5},{7,6},{8,7},{9,8},{10,9},{11,1... | collective-permute-start | bytes 1966088 | tf_op jit(solution)/shard_map/ppermute | solution.py:348
  9.0 21.1 %all-to-all-start = ((f32[128,1,128]{2,1,0:T(1,128)}), f32[128,1,128]{2,1,0:T(1,128)S(1)}, u32[]{:S(2)}, u32[]{:S(2)}) async-start(f32[128,1,128]{2,1,0:T(1,128)} %bitcast.1), calls=%async_computation | async-start | bytes 131072 | tf_op jit(solution)/shard_map/all_to_all | solution.py:380
  26.4 6.7 %copy-start.2 = (f32[512]{0:T(512)S(1)}, f32[512]{0:T(512)}, u32[]{:S(2)}) copy-start(f32[512]{0:T(512)} %param.6) | copy-start | bytes 6148
  26.4 6.7 %copy-start.3 = (f32[512]{0:T(512)S(1)}, f32[512]{0:T(512)}, u32[]{:S(2)}) copy-start(f32[512]{0:T(512)} %param.7) | copy-start | bytes 6148
  30.2 12.0 %collective-permute-start.2 = (bf16[2,2,160,512]{3,2,1,0:T(8,128)(2,1)S(1)}, bf16[2,2,160,512]{3,2,1,0:T(8,128)(2,1)S(1)}, u32[]{:S(2)}, u32[]{:S(2)}) collective-permute-start(bf16[2,2,160,512]{3,2,1,0:T(8,128)(2,1)S(1)} %shard_map.70.early), channel_id=1, source_target_pairs={{16,0},{17,1},{18,2},{19,3},{20,4},{21,5},{22,6},{23,7},{24,8},{25... | collective-permute-start | bytes 1966088 | tf_op jit(solution)/shard_map/ppermute | solution.py:348
  33.1 11.2 %copy-start = (bf16[2,2,160,512]{3,2,1,0:T(8,128)(2,1)S(1)}, bf16[2,2,160,512]{3,2,1,0:T(8,128)(2,1)}, u32[]{:S(2)}) copy-start(bf16[2,2,160,512]{3,2,1,0:T(8,128)(2,1)} %act.7) | copy-start | bytes 1966084
  42.1 16.8 %collective-permute-start.3 = (bf16[2,4,160,512]{3,2,1,0:T(8,128)(2,1)}, bf16[2,4,160,512]{3,2,1,0:T(8,128)(2,1)S(1)}, u32[]{:S(2)}, u32[]{:S(2)}) collective-permute-start(bf16[2,4,160,512]{3,2,1,0:T(8,128)(2,1)} %get-tuple-element.30.longer), channel_id=1, source_target_pairs={{0,16},{1,17},{2,18},{3,19},{4,20},{5,21},{6,22},{7,23},{8,24},{9,... | collective-permute-start | bytes 3932168 | tf_op jit(solution)/shard_map/ppermute | solution.py:348
  47.2 24.8 %all-to-all-start.1 = ((f32[128,1,128]{2,1,0:T(1,128)}), f32[128,1,128]{2,1,0:T(1,128)S(1)}, u32[]{:S(2)}, u32[]{:S(2)}) async-start(f32[128,1,128]{2,1,0:T(1,128)} %bitcast.6), calls=%async_computation.1 | async-start | bytes 131072 | tf_op jit(solution)/shard_map/all_to_all | solution.py:440
  57.8 14.2 %copy-start.1 = (f32[2,2,160,512]{3,2,1,0:T(8,128)S(1)}, f32[2,2,160,512]{3,2,1,0:T(8,128)}, u32[]{:S(2)}) copy-start(f32[2,2,160,512]{3,2,1,0:T(8,128)} %get-tuple-element.36.pre_grad) | copy-start | bytes 3932164

commit v5 on v4

--- a/solution.py
+++ b/solution.py
@@ -88,22 +88,25 @@
         pack.wait()
 
 
-def centre_kernel(cot, weight, taps, early, own, block, acc, late, load_sem, tap_sem, late_sem):
-    rows, cols, chans = cot.shape[1:]
+def centre_kernel(up, down, weight, taps, early, own, block, acc, late, tap_sem, late_sem):
+    frames, cols, chans = up.shape[1:]
+    rows = 2
     half = rows * cols
-    load = pltpu.make_async_copy(cot, block, load_sem)
-    load.start()
     order = [(2, 1), (1, 1), (0, 1), (0, 0), (0, 2), (1, 0), (1, 2)]
     fetches = [pltpu.make_async_copy(weight.at[a, b], taps.at[a, b], tap_sem.at[a, b]) for a, b in order]
     fetches[0].start()
     fetches[1].start()
-    load.wait()
+    for t in range(frames):
+        block[t, 0] = down[1, t]
+        block[t, 1] = up[1, t]
     left = block[...].reshape(2 * half, chans)
     for n, a in enumerate((2, 1, 0)):
         fetches[n].wait()
         for fetch in (fetches[2:4], fetches[4:6], [])[n]:
             fetch.start()
-        for c in range(3):
+        for c in (0, 2, 1):
+            if a < 2 and c == 1:
+                sides(acc.at[a], 2, 0, 2 * rows)
             term = transposed_dot(left, taps[a, 1, c])
             if a == 2:
                 acc[1, c] = term
@@ -116,10 +119,10 @@
         if a == 1:
             for fetch in fetches[6:]:
                 fetch.start()
-            combine(acc.at[1], late, 2, 0, None)
+            finish(acc.at[1], late, 2, None)
             send = pltpu.make_async_copy(late, own, late_sem)
             send.start()
-    combine(acc.at[0], early, 2, 0, None)
+    finish(acc.at[0], early, 2, None)
     send.wait()
     for fetch in fetches[3:]:
         fetch.wait()
@@ -129,7 +132,7 @@
     return lax.dot_general(left, right, (((1,), (1,)), ((), ())), preferred_element_type=F32)
 
 
-def grad_products(full, part, source, target, lefts, taps, acc, before=None):
+def grad_products(full, part, source, target, lefts, taps, acc, before=None, between=None):
     half = lefts[0].shape[1] * lefts[0].shape[2]
     chans = lefts[0].shape[3]
     for n, b in enumerate((0, 2)):
@@ -137,35 +140,71 @@
             before(n)
         both = lefts[n][...].reshape(2 * half, chans)
         one = lefts[n][source].reshape(half, chans)
-        for c in range(3):
+        for c in (0, 2, 1):
+            if b == 2 and c == 1:
+                sides(acc, 2, 0, half // lefts[0].shape[2] * 2)
             term = transposed_dot(both, taps[full, b, c])
             if b == 0:
                 acc[c] = term
             else:
                 acc[c] += term
+            if between is not None:
+                between(b, c)
             acc[c, target * half : (target + 1) * half] += transposed_dot(one, taps[part, b, c])
 
 
 def fill_lefts(cot, above, below, lefts):
-    for t in range(cot.shape[0]):
-        lefts[0, t, 0] = cot[t, 1]
+    for t in range(lefts.shape[1]):
+        lefts[0, t, 0] = cot[1][1, t]
         lefts[0, t, 1] = below[1, t]
         lefts[1, t, 0] = above[1, t]
-        lefts[1, t, 1] = cot[t, 0]
-
-
-def early_kernel(cot, above, below, taps, centre, out, lefts, acc):
-    fill_lefts(cot, above, below, lefts)
+        lefts[1, t, 1] = cot[0][1, t]
+
+
+def early_kernel(up, down, above, below, taps, centre, out, longer, lefts, acc, send_sem):
+    sends = [
+        pltpu.make_async_copy(side.at[0, t], longer.at[t, n], send_sem.at[t, n])
+        for n, side in enumerate((above, down, up, below))
+        for t in range(out.shape[0])
+    ]
+    for send in sends:
+        send.start()
+    fill_lefts((down, up), above, below, lefts)
     grad_products(0, 1, 0, 1, (lefts.at[0], lefts.at[1]), taps, acc)
-    combine(acc, out, 2, 0, centre)
-
-
-def own_kernel(cot, above, below, weight, centre, act, gathered, gain, shift, out, longer, stats, lefts, taps, acc, more, raw, block, acts, tap_sem, more_sem, raw_sem, block_sem, acts_sem):
+    finish(acc, out, 2, centre)
+    for send in sends:
+        send.wait()
+
+
+def activation(mean, rstd, gain, shift, out):
+    chans, rows = out.shape[3], out.shape[1]
+    gains = jnp.broadcast_to(gain[...], (8, chans))
+    shifts = jnp.broadcast_to(shift[...], (8, chans))
+    row_at = lax.axis_index("ha")
+    last_row = lax.axis_size("ha") - 1
+    top = jnp.where(row_at == 0, 0.0, 1.0).astype(F32)
+    bottom = jnp.where(row_at == last_row, 0.0, 1.0).astype(F32)
+
+    def activate(values, t, i):
+        normed = (eights(values.astype(F32)) - mean[None]) * rstd[None]
+        pre = normed * gains[None] + shifts[None]
+        value = pre / (1.0 + jnp.exp(-pre))
+        if i == 0:
+            value = value * top
+        if i == rows - 1:
+            value = value * bottom
+        out[t, i] = value.reshape(values.shape).astype(BF16)
+
+    return activate
+
+
+def own_kernel(cot, above, below, weight, centre, act, gathered, gain, shift, out, longer, stats, raw, lefts, taps, acc, more, block, acts, tap_sem, more_sem, raw_sem, block_sem, acts_sem):
     frames, rows, cols, chans = act.shape
     load_act = pltpu.make_async_copy(act, raw, raw_sem)
     load_act.start()
-    load_cot = pltpu.make_async_copy(cot, block, block_sem)
-    load_cot.start()
+    load_cot = [pltpu.make_async_copy(cot.at[:, h], block.at[h, 1], block_sem.at[h]) for h in range(rows)]
+    for load in load_cot:
+        load.start()
     fetches = [
         [pltpu.make_async_copy(weight.at[a, b], taps.at[a - 1, b], tap_sem.at[a - 1, b]) for a in (2, 1)]
         for b in (0, 2)
@@ -177,35 +216,15 @@
     mean, rstd = group_stats(gathered[...], entries, chans)
     stats[0] = mean
     stats[1] = rstd
-    gains = jnp.broadcast_to(gain[...], (8, chans))
-    shifts = jnp.broadcast_to(shift[...], (8, chans))
-    row_at = lax.axis_index("ha")
-    last_row = lax.axis_size("ha") - 1
-    top = jnp.where(row_at == 0, 0.0, 1.0).astype(F32)
-    bottom = jnp.where(row_at == last_row, 0.0, 1.0).astype(F32)
-
-    def activate(values, t, i):
-        normed = (eights(values.astype(F32)) - mean[None]) * rstd[None]
-        pre = normed * gains[None] + shifts[None]
-        value = pre / (1.0 + jnp.exp(-pre))
-        if i == 0:
-            value = value * top
-        if i == rows + 1:
-            value = value * bottom
-        acts[t, i] = value.reshape(cols, chans).astype(BF16)
-
+    activate = activation(mean, rstd, gain, shift, acts)
     for t in range(frames):
         activate(above[0, t], t, 0)
         activate(below[0, t], t, rows + 1)
     load_act.wait()
-    sends = []
-    for t in range(frames):
-        for h in range(rows):
-            activate(raw[t, h], t, 1 + h)
-        sends.append(pltpu.make_async_copy(acts.at[t], longer.at[t], acts_sem.at[t]))
-        sends[t].start()
-    load_cot.wait()
-    fill_lefts(block, above, below, lefts)
+    sends = [pltpu.make_async_copy(acts.at[t], longer.at[t], acts_sem.at[t]) for t in range(frames)]
+    for load in load_cot:
+        load.wait()
+    fill_lefts((block.at[0], block.at[1]), above, below, lefts)
 
     def before(n):
         for fetch in fetches[n]:
@@ -214,23 +233,40 @@
             for fetch in fetches[1]:
                 fetch.start()
             load_more.start()
-
-    grad_products(1, 0, 1, 0, (lefts.at[0], lefts.at[1]), taps, acc, before)
+        else:
+            for send in sends:
+                send.start()
+
+    def between(b, c):
+        if b == 0 and c != 1:
+            t = 0 if c == 0 else 1
+            for h in range(rows):
+                activate(raw[t, h], t, 1 + h)
+
+    grad_products(1, 0, 1, 0, (lefts.at[0], lefts.at[1]), taps, acc, before, between)
     load_more.wait()
-    combine(acc, out, 2, 0, more)
+    finish(acc, out, 2, more)
     for send in sends:
         send.wait()
 
 
-def combine(acc, out, earlier, later, more):
+def sides(acc, earlier, later, frames_rows):
+    positions, chans = acc.shape[1:]
+    cols = positions // frames_rows
+    col = lax.broadcasted_iota(jnp.int32, (cols, chans), 0)
+    for n in range(frames_rows):
+        at = slice(n * cols, (n + 1) * cols)
+        before = jnp.where(col == 0, 0.0, pltpu.roll(acc[earlier, at], 1, 0))
+        after = jnp.where(col == cols - 1, 0.0, pltpu.roll(acc[later, at], cols - 1, 0))
+        acc[earlier, at] = before + after
+
+
+def finish(acc, out, beside, more):
     frames, rows, cols, chans = out.shape
-    col = lax.broadcasted_iota(jnp.int32, (cols, chans), 0)
     for t in range(frames):
         for h in range(rows):
             at = slice((t * rows + h) * cols, (t * rows + h + 1) * cols)
-            before = jnp.where(col == 0, 0.0, pltpu.roll(acc[earlier, at], 1, 0))
-            after = jnp.where(col == cols - 1, 0.0, pltpu.roll(acc[later, at], cols - 1, 0))
-            total = before + acc[1, at] + after
+            total = acc[beside, at] + acc[1, at]
             if more is not None:
                 total = total + more[t, h]
             out[t, h] = total.astype(out.dtype)
@@ -249,11 +285,23 @@
     return to_chans(mean, rstd, chans)
 
 
-def point_kernel(own, incoming, early, act, stats, gain, shift, pre_grad, pay, block, block_sem):
+def point_kernel(own, incoming, act, stats, gain, shift, early, pre_grad, pay, block, extra, block_sem, extra_sem):
     frames, rows, cols, chans = act.shape
     mean, rstd = stats[0], stats[1]
     first = lax.axis_index("ta") == 0
-    scale = jnp.where(first, 1.0, 0.0).astype(F32)
+
+    @pl.when(first)
+    def _():
+        load = pltpu.make_async_copy(early, extra, extra_sem)
+        load.start()
+        load.wait()
+        for h in range(rows):
+            block[0, h] = extra[0, h].astype(F32) + extra[1, h].astype(F32)
+
+    @pl.when(jnp.logical_not(first))
+    def _():
+        block[0] = jnp.zeros_like(block[0])
+
     gains = jnp.broadcast_to(gain[...], (8, chans))
     shifts = jnp.broadcast_to(shift[...], (8, chans))
     shift_sum = jnp.zeros((8, chans), F32)
@@ -263,7 +311,7 @@
         for h in range(rows):
             grad = own[t, h] + incoming[t, h].astype(F32)
             if t == 0:
-                grad = grad + scale * (early[0, h].astype(F32) + early[1, h].astype(F32))
+                grad = grad + block[0, h]
             normed = (eights(act[t, h].astype(F32)) - mean[None]) * rstd[None]
             pre = normed * gains[None] + shifts[None]
             sig = 1.0 / (1.0 + jnp.exp(-pre))
@@ -279,62 +327,79 @@
         send.wait()
 
 
-def conv_kernel(longer, prior, weight, out, ext, near, far, near_taps, far_taps, acc, ext_sem, near_sem, far_sem):
+def conv_kernel(acts, prior, weight, stats, gain, shift, out, raw, ext, near, far, near_taps, far_taps, acc, raw_sem, ext_sem, near_sem, far_sem):
     frames, rows, cols, chans = out.shape
     positions = frames * rows * cols
+    order = (0, 2, 1)
     first = lax.axis_index("ta") == 0
-    own = pltpu.make_async_copy(longer, ext.at[frames:], ext_sem.at[0])
+    load = pltpu.make_async_copy(prior, raw, raw_sem)
+    load.start()
+    own = pltpu.make_async_copy(acts, ext.at[frames:], ext_sem)
     own.start()
-    fetches = [pltpu.make_async_copy(weight.at[2, :, c], near_taps.at[c], near_sem.at[c]) for c in range(3)]
-    fetches += [pltpu.make_async_copy(weight.at[0:2, :, c], far_taps.at[c], far_sem.at[c]) for c in range(3)]
+    fetches = [pltpu.make_async_copy(weight.at[2, :, c], near_taps.at[c], near_sem.at[c]) for c in order]
+    fetches += [pltpu.make_async_copy(weight.at[0:2, :, c], far_taps.at[c], far_sem.at[c]) for c in order]
     fetches[0].start()
+    fetches[1].start()
+    activate = activation(stats[0], stats[1], gain, shift, ext)
+
+    load.wait()
+
+    @pl.when(jnp.logical_not(first))
+    def _():
+        for t in range(frames):
+            for i in range(rows + 2):
+                activate(raw[t, i], t, i)
+
+    own.wait()
 
     @pl.when(first)
     def _():
         for t in range(frames):
-            pltpu.make_async_copy(longer.at[0], ext.at[t], ext_sem.at[1 + t]).start()
-
-    @pl.when(jnp.logical_not(first))
-    def _():
-        for t in range(frames):
-            pltpu.make_async_copy(prior.at[t], ext.at[t], ext_sem.at[1 + t]).start()
-
-    fetches[1].start()
-    own.wait()
+            ext[t] = ext[frames]
+
     for b in range(3):
         near[:, :, :, b * chans : (b + 1) * chans] = ext[2 : 2 + frames, b : b + rows]
     left = near[...].reshape(positions, 3 * chans)
-    for c in range(3):
-        fetches[c].wait()
-        fetches[c + 2].start()
+    for n, c in enumerate(order):
+        fetches[n].wait()
+        fetches[n + 2].start()
         acc[c] = jnp.dot(left, near_taps[c].reshape(3 * chans, chans), preferred_element_type=F32)
-    for t in range(frames):
-        pltpu.make_async_copy(prior.at[t], ext.at[t], ext_sem.at[1 + t]).wait()
     for a in range(2):
         for b in range(3):
             k = (3 * a + b) * chans
             far[:, :, :, k : k + chans] = ext[a : a + frames, b : b + rows]
     left = far[...].reshape(positions, 6 * chans)
-    for c in range(3):
-        fetches[3 + c].wait()
-        if c == 0:
+    for n, c in enumerate(order):
+        fetches[3 + n].wait()
+        if n == 0:
             fetches[5].start()
+        if c == 1:
+            sides(acc, 0, 2, frames * rows)
         acc[c] += jnp.dot(left, far_taps[c].reshape(6 * chans, chans), preferred_element_type=F32)
-    combine(acc, out, 0, 2, None)
-
-
-def final_kernel(pre_grad, act, gathered, stats, gain, out):
+    finish(acc, out, 0, None)
+
+
+def final_kernel(pre_grad, act, gathered, stats, gain, out, block, done, block_sem, done_sem):
     frames, rows, cols, chans = act.shape
+    places = [(t, h) for t in range(frames) for h in range(rows)]
+    loads = [pltpu.make_async_copy(pre_grad.at[at], block.at[at], block_sem.at[at]) for at in places]
+    for load in loads:
+        load.start()
     count = gathered.shape[0] * frames * rows * cols * (chans // GROUPS)
     sums = jnp.sum(gathered[...], axis=0, keepdims=True) / count
     first, second = to_chans(sums, second_part(sums), chans)
     mean, rstd = stats[0], stats[1]
     gains = jnp.broadcast_to(gain[...], (8, chans))
-    for t in range(frames):
-        for h in range(rows):
-            normed = (eights(act[t, h].astype(F32)) - mean[None]) * rstd[None]
-            value = rstd[None] * (eights(pre_grad[t, h]) * gains[None] - first[None] - normed * second[None])
-            out[t, h] = value.reshape(cols, chans).astype(BF16)
+    sends = []
+    for at, load in zip(places, loads):
+        load.wait()
+        normed = (eights(act[at].astype(F32)) - mean[None]) * rstd[None]
+        value = rstd[None] * (eights(block[at]) * gains[None] - first[None] - normed * second[None])
+        done[at] = value.reshape(cols, chans).astype(BF16)
+        sends.append(pltpu.make_async_copy(done.at[at], out.at[at], done_sem.at[at]))
+        sends[-1].start()
+    for send in sends:
+        send.wait()
 
 
 def moved(value, frame_step, row_step):
@@ -381,89 +446,96 @@
 
     f32_block = jax.ShapeDtypeStruct(shape, F32)
     sums = (3, positions, chans)
-    held, early_centre, own_centre, cot_held = pl.pallas_call(
+    held, early_centre, own_centre = pl.pallas_call(
         centre_kernel,
-        in_specs=[HBM] * 2,
-        out_specs=[WHOLE, WHOLE, HBM, WHOLE],
-        out_shape=[pltpu.VMEM(weight.shape, BF16), f32_block, pltpu.HBM(shape, F32), jax.ShapeDtypeStruct(shape, BF16)],
+        in_specs=[WHOLE, WHOLE, HBM],
+        out_specs=[WHOLE, WHOLE, HBM],
+        out_shape=[pltpu.VMEM(weight.shape, BF16), f32_block, pltpu.HBM(shape, F32)],
         scratch_shapes=[
+            pltpu.VMEM(shape, BF16),
             pltpu.VMEM((2,) + sums, F32),
             pltpu.VMEM(shape, F32),
-            DMA,
             DMA((3, 3)),
             DMA,
         ],
         compiler_params=params(16),
-    )(cot, taps)
+    )(up, down, taps)
     held = in_vmem(held)
-    early = pl.pallas_call(
+    early, longer = pl.pallas_call(
         early_kernel,
-        in_specs=[WHOLE] * 5,
-        out_specs=WHOLE,
-        out_shape=jax.ShapeDtypeStruct(shape, BF16),
-        scratch_shapes=[pltpu.VMEM((2,) + shape, BF16), pltpu.VMEM(sums, F32)],
+        in_specs=[WHOLE] * 6,
+        out_specs=[WHOLE, HBM],
+        out_shape=[pltpu.VMEM(shape, BF16), pltpu.HBM(longer_shape, BF16)],
+        scratch_shapes=[pltpu.VMEM((2,) + shape, BF16), pltpu.VMEM(sums, F32), DMA((frames, rows + 2))],
         compiler_params=params(16),
-    )(cot_held, above, below, held, early_centre)
+    )(up, down, above, below, held, early_centre)
     early, gathered = lax.optimization_barrier((early, gathered))
     incoming = moved(early, -1, 0)
-    own, longer, stats = pl.pallas_call(
+    prior = moved(longer, 1, 0)
+    own, acts, stats, act_held = pl.pallas_call(
         own_kernel,
         in_specs=[HBM, WHOLE, WHOLE, HBM, HBM, HBM, WHOLE, WHOLE, WHOLE],
-        out_specs=[WHOLE, HBM, WHOLE],
-        out_shape=[f32_block, pltpu.HBM(longer_shape, BF16), jax.ShapeDtypeStruct((2, 8, chans), F32)],
+        out_specs=[WHOLE, HBM, WHOLE, WHOLE],
+        out_shape=[f32_block, pltpu.HBM(longer_shape, BF16), jax.ShapeDtypeStruct((2, 8, chans), F32), jax.ShapeDtypeStruct(shape, BF16)],
         scratch_shapes=[
             pltpu.VMEM((2,) + shape, BF16),
             pltpu.VMEM((2, 3, 3, chans, chans), BF16),
             pltpu.VMEM(sums, F32),
             pltpu.VMEM(shape, F32),
-            pltpu.VMEM(shape, BF16),
-            pltpu.VMEM(shape, BF16),
+            pltpu.VMEM((rows, 2, frames, cols, chans), BF16),
             pltpu.VMEM(longer_shape, BF16),
             DMA((2, 3)),
             DMA,
             DMA,
-            DMA,
+            DMA((rows,)),
             DMA((frames,)),
         ],
         compiler_params=params(28),
     )(cot, above, below, taps, in_hbm(own_centre), act, gathered, gain, shift)
-    longer, incoming = lax.optimization_barrier((longer, incoming))
-    prior = moved(longer, 1, 0)
     pre_grad, pay = pl.pallas_call(
         point_kernel,
-        in_specs=[WHOLE] * 7,
+        in_specs=[WHOLE] * 6 + [ANY],
         out_specs=[HBM, WHOLE],
         out_shape=[pltpu.HBM(shape, F32), gathered_shape],
-        scratch_shapes=[pltpu.VMEM(shape, F32), DMA((frames, rows))],
+        scratch_shapes=[pltpu.VMEM(shape, F32), pltpu.VMEM(shape, BF16), DMA((frames, rows)), DMA],
+        cost_estimate=pl.CostEstimate(flops=2 * 10**10, bytes_accessed=10**6, transcendentals=0),
         compiler_params=params(16),
-    )(own, incoming, early, activations, stats, gain, shift)
+    )(own, incoming, act_held, stats, gain, shift, early)
     gathered = lax.all_to_all(pay, BOTH, 0, 0, tiled=True)
     output = pl.pallas_call(
         conv_kernel,
-        in_specs=[HBM, ANY, HBM],
+        in_specs=[HBM, ANY, HBM, WHOLE, WHOLE, WHOLE],
         out_specs=WHOLE,
         out_shape=jax.ShapeDtypeStruct(shape, BF16),
         scratch_shapes=[
+            pltpu.VMEM(longer_shape, BF16),
             pltpu.VMEM((frames + 2, rows + 2, cols, chans), BF16),
             pltpu.VMEM((frames, rows, cols, 3 * chans), BF16),
             pltpu.VMEM((frames, rows, cols, 6 * chans), BF16),
             pltpu.VMEM((3, 3, chans, chans), BF16),
             pltpu.VMEM((3, 2, 3, chans, chans), BF16),
             pltpu.VMEM(sums, F32),
-            DMA((1 + frames,)),
+            DMA,
+            DMA,
             DMA((3,)),
             DMA((3,)),
         ],
         compiler_params=params(36),
-    )(in_hbm(longer), prior, taps)
+    )(in_hbm(acts), prior, taps, stats, gain, shift)
     output, gathered = lax.optimization_barrier((output, gathered))
     input_grad = pl.pallas_call(
         final_kernel,
-        in_specs=[WHOLE] * 5,
-        out_specs=WHOLE,
-        out_shape=jax.ShapeDtypeStruct(shape, BF16),
+        in_specs=[HBM] + [WHOLE] * 4,
+        out_specs=HBM,
+        out_shape=pltpu.HBM(shape, BF16),
+        scratch_shapes=[
+            pltpu.VMEM(shape, F32),
+            pltpu.VMEM(shape, BF16),
+            DMA((frames, rows)),
+            DMA((frames, rows)),
+        ],
         compiler_params=params(16),
-    )(pre_grad, activations, gathered, stats, gain)
+    )(in_hbm(pre_grad), activations, gathered, stats, gain)
     return (output, input_grad)
 
 

time: 74.6 us -> 71.6 us (0.960); the launches traced: 73.5 us -> 71.3 us
  waiting for transfers between devices: 3.99 us -> 0.62 us
    ppermute x4, waiting for transfers between devices: 3.53 us -> 0.01 us  [moved(): return lax.ppermute(value, BOTH, pairs)]
    ppermute x4, starting transfers between devices: 10.7 us -> 11.5 us  [moved(): return lax.ppermute(value, BOTH, pairs)]
  transfers between devices with their start and end apart: 6 -> 6, of which waited for: 3 -> 1; matrix products, arithmetic and copies ran while one was open for 0% -> 0% of each run, Pallas kernels for 43% -> 44%
where the time goes in v5:
time: 71.6 us; the launch traced here: 71.3 us
  Pallas kernels  36 us (50%)
  starting transfers between devices  33.6 us (47%)
  between operations  0.97 us (1%)
    all_to_all x2, starting transfers between devices, on_device(): gathered = lax.all_to_all(pay, BOTH, 0, 0, tiled=True)  22.1 us
    pallas_call x1, Pallas kernels, on_device(): pl.pallas_call(conv_kernel, in_specs=[HBM, ANY, HBM, WHOLE, WHOLE, WHOLE]...  13.2 us
    ppermute x4, starting transfers between devices, moved(): return lax.ppermute(value, BOTH, pairs)  11.5 us
    pallas_call x1, Pallas kernels, on_device(): pl.pallas_call(own_kernel, in_specs=[HBM, WHOLE, WHOLE, HBM, HBM, HBM, WH...  6.29 us
    pallas_call x1, Pallas kernels, on_device(): pl.pallas_call(centre_kernel, in_specs=[WHOLE, WHOLE, HBM], out_specs=[WH...  5.35 us
    pallas_call x1, Pallas kernels, on_device(): pl.pallas_call(early_kernel, in_specs=[WHOLE] * 6, out_specs=[WHOLE, HBM]...  3.5 us
    pallas_call x1, Pallas kernels, on_device(): pl.pallas_call(point_kernel, in_specs=[WHOLE] * 6 + [ANY], out_specs=[HBM...  2.94 us
    pallas_call x1, Pallas kernels, on_device(): pl.pallas_call(stats_kernel, in_specs=[HBM, HBM], out_specs=[WHOLE] * 3,...  2.66 us
  transfers between devices with their start and end apart: 6, of which 1 were waited for; matrix products, arithmetic and copies ran while one was open for 0% of the time, Pallas kernels for 44%

profile of v5, /device:TPU:1, one launch (start us, length us, event | category | flops | bytes accessed | tf_op | source)
XLA Modules:
  0.0 71.3 jit_solution(4244896197988505506)
XLA Ops:
  0.6 2.7 %shard_map.68 = (f32[128,128]{1,0:T(8,128)}, bf16[2,2,160,512]{3,2,1,0:T(8,128)(2,1)S(1)}, bf16[2,2,160,512]{3,2,1,0:T(8,128)(2,1)S(1)}) custom-call(bf16[2,2,160,512]{3,2,1,0:T(8,128)(2,1)} %act.5, bf16[2,2,160,512]{3,2,1,0:T(8,128)(2,1)} %cot.3), custom_call_target="tpu_custom_call" | custom-call | tf_op jit(solution)/shard_map/pallas_call | solution.py:435
  3.3 4.4 %collective-permute-start = (bf16[2,2,160,512]{3,2,1,0:T(8,128)(2,1)S(1)}, bf16[2,2,160,512]{3,2,1,0:T(8,128)(2,1)S(1)}, u32[]{:S(2)}, u32[]{:S(2)}) collective-permute-start(bf16[2,2,160,512]{3,2,1,0:T(8,128)(2,1)S(1)} %get-tuple-element.20.up), channel_id=1, source_target_pairs={{0,1},{1,2},{2,3},{3,4},{4,5},{5,6},{6,7},{7,8},{8,9},{9,10},{10,1... | collective-permute-start | bytes 1966088 | tf_op jit(solution)/shard_map/ppermute | solution.py:413
  7.7 1.3 %collective-permute-start.1 = (bf16[2,2,160,512]{3,2,1,0:T(8,128)(2,1)S(1)}, bf16[2,2,160,512]{3,2,1,0:T(8,128)(2,1)S(1)}, u32[]{:S(2)}, u32[]{:S(2)}) collective-permute-start(bf16[2,2,160,512]{3,2,1,0:T(8,128)(2,1)S(1)} %get-tuple-element.21.down), channel_id=1, source_target_pairs={{1,0},{2,1},{3,2},{4,3},{5,4},{6,5},{7,6},{8,7},{9,8},{10,9},{11,1... | collective-permute-start | bytes 1966088 | tf_op jit(solution)/shard_map/ppermute | solution.py:413
  9.0 11.6 %all-to-all-start = ((f32[128,1,128]{2,1,0:T(1,128)}), f32[128,1,128]{2,1,0:T(1,128)S(1)}, u32[]{:S(2)}, u32[]{:S(2)}) async-start(f32[128,1,128]{2,1,0:T(1,128)} %bitcast.1), calls=%async_computation | async-start | bytes 131072 | tf_op jit(solution)/shard_map/all_to_all | solution.py:445
  20.7 5.3 %shard_map.69 = (bf16[3,3,3,512,512]{4,3,2,1,0:T(8,128)(2,1)S(1)}, f32[2,2,160,512]{3,2,1,0:T(8,128)S(1)}, f32[2,2,160,512]{3,2,1,0:T(8,128)}) custom-call(bf16[2,2,160,512]{3,2,1,0:T(8,128)(2,1)S(1)} %get-tuple-element.20.up, bf16[2,2,160,512]{3,2,1,0:T(8,128)(2,1)S(1)} %get-tuple-element.21.down, bf16[3,3,3,512,512]{4,3,2,1,0:T(8,128)(2,1)} %weight.5), custom_call_target="tpu_custom_call" | custom-call | tf_op jit(solution)/shard_map/pallas_call | solution.py:449
  26.0 0.0 collective-permute-done.above
  26.0 0.0 collective-permute-done.1.below
  26.0 0.0 copy-start.1
  26.0 0.0 copy-start.2
  26.1 3.5 %shard_map.70 = (bf16[2,2,160,512]{3,2,1,0:T(8,128)(2,1)S(1)}, bf16[2,4,160,512]{3,2,1,0:T(8,128)(2,1)}) custom-call(bf16[2,2,160,512]{3,2,1,0:T(8,128)(2,1)S(1)} %get-tuple-element.20.up, bf16[2,2,160,512]{3,2,1,0:T(8,128)(2,1)S(1)} %get-tuple-element.21.down, bf16[2,2,160,512]{3,2,1,0:T(8,128)(2,1)S(1)} %collective-permute-done.above, ...), custom_call_target="tpu_custom_call" | custom-call | tf_op jit(solution)/shard_map/pallas_call | solution.py:464
  29.6 0.6 all-to-all-done
  30.2 2.9 %collective-permute-start.3 = (bf16[2,2,160,512]{3,2,1,0:T(8,128)(2,1)S(1)}, bf16[2,2,160,512]{3,2,1,0:T(8,128)(2,1)S(1)}, u32[]{:S(2)}, u32[]{:S(2)}) collective-permute-start(bf16[2,2,160,512]{3,2,1,0:T(8,128)(2,1)S(1)} %get-tuple-element.32.early), channel_id=1, source_target_pairs={{16,0},{17,1},{18,2},{19,3},{20,4},{21,5},{22,6},{23,7},{24,8},{25... | collective-permute-start | bytes 1966088 | tf_op jit(solution)/shard_map/ppermute | solution.py:413
  33.0 2.9 %collective-permute-start.2 = (bf16[2,4,160,512]{3,2,1,0:T(8,128)(2,1)}, bf16[2,4,160,512]{3,2,1,0:T(8,128)(2,1)S(1)}, u32[]{:S(2)}, u32[]{:S(2)}) collective-permute-start(bf16[2,4,160,512]{3,2,1,0:T(8,128)(2,1)} %get-tuple-element.29), channel_id=1, source_target_pairs={{0,16},{1,17},{2,18},{3,19},{4,20},{5,21},{6,22},{7,23},{8,24},{9,... | collective-permute-start | bytes 3932168 | tf_op jit(solution)/shard_map/ppermute | solution.py:413
  36.0 0.0 copy-done.1
  36.0 0.0 copy-done.2
  36.0 6.3 %shard_map.71 = (f32[2,2,160,512]{3,2,1,0:T(8,128)S(1)}, bf16[2,4,160,512]{3,2,1,0:T(8,128)(2,1)}, f32[2,8,512]{2,1,0:T(8,128)S(1)}, bf16[2,2,160,512]{3,2,1,0:T(8,128)(2,1)S(1)}) custom-call(bf16[2,2,160,512]{3,2,1,0:T(8,128)(2,1)} %cot.3, bf16[2,2,160,512]{3,2,1,0:T(8,128)(2,1)S(1)} %collective-permute-done.above, ...), custom_call_target="tpu_custom_call" | custom-call | tf_op jit(solution)/shard_map/pallas_call | solution.py:475
  42.3 0.0 collective-permute-done.3.incoming
  42.3 2.9 %shard_map.73 = (f32[2,2,160,512]{3,2,1,0:T(8,128)}, f32[128,128]{1,0:T(8,128)}) custom-call(f32[2,2,160,512]{3,2,1,0:T(8,128)S(1)} %get-tuple-element.31.own, bf16[2,2,160,512]{3,2,1,0:T(8,128)(2,1)S(1)} %collective-permute-done.3.incoming, bf16[2,2,160,512]{3,2,1,0:T(8,128)(2,1)S(1)} %get-tuple-element.33.act, f32[2,8,512]{2,1,0:T(8,128)S(1)} %get-tuple-element.30.stats, ...), custom_call_target="tpu_custom_call" | custom-call | flops 20000000000 | bytes 1000000 | tf_op jit(solution)/shard_map/pallas_call | solution.py:495
  45.3 10.5 %all-to-all-start.1 = ((f32[128,1,128]{2,1,0:T(1,128)}), f32[128,1,128]{2,1,0:T(1,128)S(1)}, u32[]{:S(2)}, u32[]{:S(2)}) async-start(f32[128,1,128]{2,1,0:T(1,128)} %bitcast.6), calls=%async_computation.1 | async-start | bytes 131072 | tf_op jit(solution)/shard_map/all_to_all | solution.py:504
  55.7 0.0 collective-permute-done.2.prior
  55.8 0.0 copy-start
  55.8 13.2 %shard_map.72 = bf16[2,2,160,512]{3,2,1,0:T(8,128)(2,1)} custom-call(bf16[2,4,160,512]{3,2,1,0:T(8,128)(2,1)} %get-tuple-element.28.acts, bf16[2,4,160,512]{3,2,1,0:T(8,128)(2,1)S(1)} %collective-permute-done.2.prior, bf16[3,3,3,512,512]{4,3,2,1,0:T(8,128)(2,1)} %weight.5, f32[2,8,512]{2,1,0:T(8,128)S(1)} %get-tuple-element.30.stats, f32[1,512]{1,0:T(1,128)S(1)} %bitcast.14, ...), custom_call_target="tpu_custom_call" | custom-call | tf_op jit(solution)/shard_map/pallas_call | solution.py:505
  69.0 0.0 all-to-all-done.1
  69.0 0.0 copy-done
  69.0 2.1 %shard_map.74 = bf16[2,2,160,512]{3,2,1,0:T(8,128)(2,1)} custom-call(f32[2,2,160,512]{3,2,1,0:T(8,128)} %get-tuple-element.36.pre_grad, bf16[2,2,160,512]{3,2,1,0:T(8,128)(2,1)S(1)} %copy-done, f32[128,128]{1,0:T(8,128)S(1)} %bitcast.11, f32[2,8,512]{2,1,0:T(8,128)S(1)} %get-tuple-element.30.stats, f32[1,512]{1,0:T(1,128)S(1)} %bitcast.15), custom_call_target="tpu_custom_call" | custom-call | tf_op jit(solution)/shard_map/pallas_call | solution.py:526
Async XLA Ops:
  3.3 22.7 %collective-permute-start = (bf16[2,2,160,512]{3,2,1,0:T(8,128)(2,1)S(1)}, bf16[2,2,160,512]{3,2,1,0:T(8,128)(2,1)S(1)}, u32[]{:S(2)}, u32[]{:S(2)}) collective-permute-start(bf16[2,2,160,512]{3,2,1,0:T(8,128)(2,1)S(1)} %get-tuple-element.20.up), channel_id=1, source_target_pairs={{0,1},{1,2},{2,3},{3,4},{4,5},{5,6},{6,7},{7,8},{8,9},{9,10},{10,1... | collective-permute-start | bytes 1966088 | tf_op jit(solution)/shard_map/ppermute | solution.py:413
  7.7 18.3 %collective-permute-start.1 = (bf16[2,2,160,512]{3,2,1,0:T(8,128)(2,1)S(1)}, bf16[2,2,160,512]{3,2,1,0:T(8,128)(2,1)S(1)}, u32[]{:S(2)}, u32[]{:S(2)}) collective-permute-start(bf16[2,2,160,512]{3,2,1,0:T(8,128)(2,1)S(1)} %get-tuple-element.21.down), channel_id=1, source_target_pairs={{1,0},{2,1},{3,2},{4,3},{5,4},{6,5},{7,6},{8,7},{9,8},{10,9},{11,1... | collective-permute-start | bytes 1966088 | tf_op jit(solution)/shard_map/ppermute | solution.py:413
  9.0 21.1 %all-to-all-start = ((f32[128,1,128]{2,1,0:T(1,128)}), f32[128,1,128]{2,1,0:T(1,128)S(1)}, u32[]{:S(2)}, u32[]{:S(2)}) async-start(f32[128,1,128]{2,1,0:T(1,128)} %bitcast.1), calls=%async_computation | async-start | bytes 131072 | tf_op jit(solution)/shard_map/all_to_all | solution.py:445
  26.0 9.9 %copy-start.1 = (f32[512]{0:T(512)S(1)}, f32[512]{0:T(512)}, u32[]{:S(2)}) copy-start(f32[512]{0:T(512)} %param.6) | copy-start | bytes 6148
  26.0 9.9 %copy-start.2 = (f32[512]{0:T(512)S(1)}, f32[512]{0:T(512)}, u32[]{:S(2)}) copy-start(f32[512]{0:T(512)} %param.7) | copy-start | bytes 6148
  30.2 12.1 %collective-permute-start.3 = (bf16[2,2,160,512]{3,2,1,0:T(8,128)(2,1)S(1)}, bf16[2,2,160,512]{3,2,1,0:T(8,128)(2,1)S(1)}, u32[]{:S(2)}, u32[]{:S(2)}) collective-permute-start(bf16[2,2,160,512]{3,2,1,0:T(8,128)(2,1)S(1)} %get-tuple-element.32.early), channel_id=1, source_target_pairs={{16,0},{17,1},{18,2},{19,3},{20,4},{21,5},{22,6},{23,7},{24,8},{25... | collective-permute-start | bytes 1966088 | tf_op jit(solution)/shard_map/ppermute | solution.py:413
  33.0 22.7 %collective-permute-start.2 = (bf16[2,4,160,512]{3,2,1,0:T(8,128)(2,1)}, bf16[2,4,160,512]{3,2,1,0:T(8,128)(2,1)S(1)}, u32[]{:S(2)}, u32[]{:S(2)}) collective-permute-start(bf16[2,4,160,512]{3,2,1,0:T(8,128)(2,1)} %get-tuple-element.29), channel_id=1, source_target_pairs={{0,16},{1,17},{2,18},{3,19},{4,20},{5,21},{6,22},{7,23},{8,24},{9,... | collective-permute-start | bytes 3932168 | tf_op jit(solution)/shard_map/ppermute | solution.py:413
  45.3 23.7 %all-to-all-start.1 = ((f32[128,1,128]{2,1,0:T(1,128)}), f32[128,1,128]{2,1,0:T(1,128)S(1)}, u32[]{:S(2)}, u32[]{:S(2)}) async-start(f32[128,1,128]{2,1,0:T(1,128)} %bitcast.6), calls=%async_computation.1 | async-start | bytes 131072 | tf_op jit(solution)/shard_map/all_to_all | solution.py:504
  55.8 13.2 %copy-start = (bf16[2,2,160,512]{3,2,1,0:T(8,128)(2,1)S(1)}, bf16[2,2,160,512]{3,2,1,0:T(8,128)(2,1)}, u32[]{:S(2)}) copy-start(bf16[2,2,160,512]{3,2,1,0:T(8,128)(2,1)} %act.5) | copy-start | bytes 1966084

commit v6 on v5

--- a/solution.py
+++ b/solution.py
@@ -58,23 +58,23 @@
     return value.reshape(value.shape[0] // 8, 8, value.shape[1])
 
 
-def stats_kernel(act, cot, pay, up, down, act_sem, cot_sem):
-    frames, rows, cols, chans = act.shape
-    sides = ((0, down), (rows - 1, up))
-    loads = []
-    for t in range(frames):
-        for n, (h, side) in enumerate(sides):
-            loads.append(pltpu.make_async_copy(act.at[t, h], side.at[0, t], act_sem.at[t, n]))
-            loads[-1].start()
-    packs = [pltpu.make_async_copy(cot.at[:, h], side.at[1], cot_sem.at[n]) for n, (h, side) in enumerate(sides)]
+def pack_kernel(act, cot, up, down, sem):
+    packs = []
+    for n, source in enumerate((act, cot)):
+        for k, (h, side) in enumerate(((0, down), (act.shape[1] - 1, up))):
+            packs.append(pltpu.make_async_copy(source.at[:, h], side.at[n], sem.at[n, k]))
+            packs[-1].start()
     for pack in packs:
-        pack.start()
-    blocks = [(t, side) for t in range(frames) for _, side in sides]
-    entries = frames * rows * cols * (chans // GROUPS)
+        pack.wait()
+
+
+def stats_kernel(up, down, pay):
+    frames, cols, chans = up.shape[1:]
+    blocks = [(t, side) for t in range(frames) for side in (down, up)]
+    entries = len(blocks) * cols * (chans // GROUPS)
     none = jnp.zeros((8, chans), F32)
     total = none
-    for load, (t, side) in zip(loads, blocks):
-        load.wait()
+    for t, side in blocks:
         total = total + jnp.sum(eights(side[0, t].astype(F32)), axis=0)
     sums = to_groups(total, none)
     mean, _ = to_chans(sums / entries, sums, chans)
@@ -82,10 +82,7 @@
     for t, side in blocks:
         centered = eights(side[0, t].astype(F32)) - mean[None]
         spread = spread + jnp.sum(centered * centered, axis=0)
-    row = sums + to_groups(none, spread)
-    pay[...] = jnp.broadcast_to(row, pay.shape)
-    for pack in packs:
-        pack.wait()
+    pay[...] = jnp.broadcast_to(sums + to_groups(none, spread), pay.shape)
 
 
 def centre_kernel(up, down, weight, taps, early, own, block, acc, late, tap_sem, late_sem):
@@ -95,10 +92,10 @@
     order = [(2, 1), (1, 1), (0, 1), (0, 0), (0, 2), (1, 0), (1, 2)]
     fetches = [pltpu.make_async_copy(weight.at[a, b], taps.at[a, b], tap_sem.at[a, b]) for a, b in order]
     fetches[0].start()
-    fetches[1].start()
     for t in range(frames):
         block[t, 0] = down[1, t]
         block[t, 1] = up[1, t]
+    fetches[1].start()
     left = block[...].reshape(2 * half, chans)
     for n, a in enumerate((2, 1, 0)):
         fetches[n].wait()
@@ -327,30 +324,27 @@
         send.wait()
 
 
-def conv_kernel(acts, prior, weight, stats, gain, shift, out, raw, ext, near, far, near_taps, far_taps, acc, raw_sem, ext_sem, near_sem, far_sem):
+def conv_kernel(acts, prior, weight, stats, gain, shift, out, ext, near, far, near_taps, far_taps, acc, ext_sem, near_sem, far_sem):
     frames, rows, cols, chans = out.shape
     positions = frames * rows * cols
     order = (0, 2, 1)
     first = lax.axis_index("ta") == 0
-    load = pltpu.make_async_copy(prior, raw, raw_sem)
-    load.start()
     own = pltpu.make_async_copy(acts, ext.at[frames:], ext_sem)
     own.start()
     fetches = [pltpu.make_async_copy(weight.at[2, :, c], near_taps.at[c], near_sem.at[c]) for c in order]
     fetches += [pltpu.make_async_copy(weight.at[0:2, :, c], far_taps.at[c], far_sem.at[c]) for c in order]
     fetches[0].start()
-    fetches[1].start()
     activate = activation(stats[0], stats[1], gain, shift, ext)
-
-    load.wait()
 
     @pl.when(jnp.logical_not(first))
     def _():
         for t in range(frames):
             for i in range(rows + 2):
-                activate(raw[t, i], t, i)
+                activate(prior[t, i], t, i)
 
     own.wait()
+    fetches[1].start()
+    fetches[2].start()
 
     @pl.when(first)
     def _():
@@ -361,8 +355,14 @@
         near[:, :, :, b * chans : (b + 1) * chans] = ext[2 : 2 + frames, b : b + rows]
     left = near[...].reshape(positions, 3 * chans)
     for n, c in enumerate(order):
-        fetches[n].wait()
-        fetches[n + 2].start()
+        if n == 0:
+            fetches[0].wait()
+            fetches[3].start()
+        if n == 1:
+            fetches[1].wait()
+            fetches[2].wait()
+            fetches[4].start()
+            fetches[5].start()
         acc[c] = jnp.dot(left, near_taps[c].reshape(3 * chans, chans), preferred_element_type=F32)
     for a in range(2):
         for b in range(3):
@@ -370,30 +370,40 @@
             far[:, :, :, k : k + chans] = ext[a : a + frames, b : b + rows]
     left = far[...].reshape(positions, 6 * chans)
     for n, c in enumerate(order):
-        fetches[3 + n].wait()
         if n == 0:
-            fetches[5].start()
+            fetches[3].wait()
+        if n == 1:
+            fetches[4].wait()
+            fetches[5].wait()
         if c == 1:
             sides(acc, 0, 2, frames * rows)
         acc[c] += jnp.dot(left, far_taps[c].reshape(6 * chans, chans), preferred_element_type=F32)
     finish(acc, out, 0, None)
 
 
-def final_kernel(pre_grad, act, gathered, stats, gain, out, block, done, block_sem, done_sem):
+def final_kernel(pre_grad, act, gathered, stats, gain, out, block, raw, done, block_sem, raw_sem, done_sem):
     frames, rows, cols, chans = act.shape
     places = [(t, h) for t in range(frames) for h in range(rows)]
-    loads = [pltpu.make_async_copy(pre_grad.at[at], block.at[at], block_sem.at[at]) for at in places]
-    for load in loads:
-        load.start()
+    loads = [
+        (
+            pltpu.make_async_copy(act.at[at], raw.at[at], raw_sem.at[at]),
+            pltpu.make_async_copy(pre_grad.at[at], block.at[at], block_sem.at[at]),
+        )
+        for at in places
+    ]
+    for pair in loads:
+        for load in pair:
+            load.start()
     count = gathered.shape[0] * frames * rows * cols * (chans // GROUPS)
     sums = jnp.sum(gathered[...], axis=0, keepdims=True) / count
     first, second = to_chans(sums, second_part(sums), chans)
     mean, rstd = stats[0], stats[1]
     gains = jnp.broadcast_to(gain[...], (8, chans))
     sends = []
-    for at, load in zip(places, loads):
-        load.wait()
-        normed = (eights(act[at].astype(F32)) - mean[None]) * rstd[None]
+    for at, pair in zip(places, loads):
+        for load in pair:
+            load.wait()
+        normed = (eights(raw[at].astype(F32)) - mean[None]) * rstd[None]
         value = rstd[None] * (eights(block[at]) * gains[None] - first[None] - normed * second[None])
         done[at] = value.reshape(cols, chans).astype(BF16)
         sends.append(pltpu.make_async_copy(done.at[at], out.at[at], done_sem.at[at]))
@@ -432,14 +442,21 @@
     longer_shape = (frames, rows + 2, cols, chans)
     positions = frames * rows * cols
 
-    pay, up, down = pl.pallas_call(
-        stats_kernel,
+    up, down = pl.pallas_call(
+        pack_kernel,
         in_specs=[HBM, HBM],
-        out_specs=[WHOLE] * 3,
-        out_shape=[gathered_shape, edge, edge],
-        scratch_shapes=[DMA((frames, rows)), DMA((2,))],
+        out_specs=[WHOLE] * 2,
+        out_shape=[edge, edge],
+        scratch_shapes=[DMA((2, 2))],
         compiler_params=params(16),
     )(act, cot)
+    pay = pl.pallas_call(
+        stats_kernel,
+        in_specs=[WHOLE] * 2,
+        out_specs=WHOLE,
+        out_shape=gathered_shape,
+        compiler_params=params(16),
+    )(up, down)
     above = moved(up, 0, 1)
     below = moved(down, 0, -1)
     gathered = lax.all_to_all(pay, BOTH, 0, 0, tiled=True)
@@ -504,18 +521,16 @@
     gathered = lax.all_to_all(pay, BOTH, 0, 0, tiled=True)
     output = pl.pallas_call(
         conv_kernel,
-        in_specs=[HBM, ANY, HBM, WHOLE, WHOLE, WHOLE],
+        in_specs=[HBM, WHOLE, HBM, WHOLE, WHOLE, WHOLE],
         out_specs=WHOLE,
         out_shape=jax.ShapeDtypeStruct(shape, BF16),
         scratch_shapes=[
-            pltpu.VMEM(longer_shape, BF16),
             pltpu.VMEM((frames + 2, rows + 2, cols, chans), BF16),
             pltpu.VMEM((frames, rows, cols, 3 * chans), BF16),
             pltpu.VMEM((frames, rows, cols, 6 * chans), BF16),
             pltpu.VMEM((3, 3, chans, chans), BF16),
             pltpu.VMEM((3, 2, 3, chans, chans), BF16),
             pltpu.VMEM(sums, F32),
-            DMA,
             DMA,
             DMA((3,)),
             DMA((3,)),
@@ -525,17 +540,19 @@
     output, gathered = lax.optimization_barrier((output, gathered))
     input_grad = pl.pallas_call(
         final_kernel,
-        in_specs=[HBM] + [WHOLE] * 4,
+        in_specs=[HBM, HBM, WHOLE, WHOLE, WHOLE],
         out_specs=HBM,
         out_shape=pltpu.HBM(shape, BF16),
         scratch_shapes=[
             pltpu.VMEM(shape, F32),
             pltpu.VMEM(shape, BF16),
+            pltpu.VMEM(shape, BF16),
+            DMA((frames, rows)),
             DMA((frames, rows)),
             DMA((frames, rows)),
         ],
         compiler_params=params(16),
-    )(in_hbm(pre_grad), activations, gathered, stats, gain)
+    )(in_hbm(pre_grad), act, gathered, stats, gain)
     return (output, input_grad)
 
 

time: 71.6 us -> 70.4 us (0.983)
  starting transfers between devices: 33.6 us -> 32.1 us
    all_to_all x2, starting transfers between devices: 22.1 us -> 20.9 us  [on_device(): gathered = lax.all_to_all(pay, BOTH, 0, 0, tiled=True)]
    pallas_call x3 -> x4, Pallas kernels: 18 us -> 18.3 us  [the longest x1 13 us: on_device(): pl.pallas_call(conv_kernel, in_specs=[HBM, WHOLE, HBM, WHOLE, WHOLE, WHOL...]
  transfers between devices with their start and end apart: 6 -> 6, of which waited for: 1 -> 1; matrix products, arithmetic and copies ran while one was open for 0% -> 0% of each run, Pallas kernels for 44% -> 47%
where the time goes in v6:
time: 70.4 us; the launch traced here: 70 us
  Pallas kernels  36.3 us (52%)
  starting transfers between devices  32.1 us (46%)
  between operations  0.96 us (1%)
    all_to_all x2, starting transfers between devices, on_device(): gathered = lax.all_to_all(pay, BOTH, 0, 0, tiled=True)  20.9 us
    pallas_call x1, Pallas kernels, on_device(): pl.pallas_call(conv_kernel, in_specs=[HBM, WHOLE, HBM, WHOLE, WHOLE, WHOL...  13 us
    ppermute x4, starting transfers between devices, moved(): return lax.ppermute(value, BOTH, pairs)  11.3 us
    pallas_call x1, Pallas kernels, on_device(): pl.pallas_call(own_kernel, in_specs=[HBM, WHOLE, WHOLE, HBM, HBM, HBM, WH...  6.3 us
    pallas_call x1, Pallas kernels, on_device(): pl.pallas_call(centre_kernel, in_specs=[WHOLE, WHOLE, HBM], out_specs=[WH...  5.35 us
    pallas_call x1, Pallas kernels, on_device(): pl.pallas_call(early_kernel, in_specs=[WHOLE] * 6, out_specs=[WHOLE, HBM]...  3.5 us
    pallas_call x1, Pallas kernels, on_device(): pl.pallas_call(point_kernel, in_specs=[WHOLE] * 6 + [ANY], out_specs=[HBM...  2.94 us
    pallas_call x1, Pallas kernels, on_device(): pl.pallas_call(final_kernel, in_specs=[HBM, HBM, WHOLE, WHOLE, WHOLE], ou...  2.41 us
  transfers between devices with their start and end apart: 6, of which 1 were waited for; matrix products, arithmetic and copies ran while one was open for 0% of the time, Pallas kernels for 47%

profile of v6, /device:TPU:1, one launch (start us, length us, event | category | flops | bytes accessed | tf_op | source)
XLA Modules:
  0.0 70.0 jit_solution(15200020334202765305)
XLA Ops:
  0.6 1.3 %shard_map.68 = (bf16[2,2,160,512]{3,2,1,0:T(8,128)(2,1)S(1)}, bf16[2,2,160,512]{3,2,1,0:T(8,128)(2,1)S(1)}) custom-call(bf16[2,2,160,512]{3,2,1,0:T(8,128)(2,1)} %act.5, bf16[2,2,160,512]{3,2,1,0:T(8,128)(2,1)} %cot.3), custom_call_target="tpu_custom_call" | custom-call | tf_op jit(solution)/shard_map/pallas_call | solution.py:445
  1.9 4.4 %collective-permute-start = (bf16[2,2,160,512]{3,2,1,0:T(8,128)(2,1)S(1)}, bf16[2,2,160,512]{3,2,1,0:T(8,128)(2,1)S(1)}, u32[]{:S(2)}, u32[]{:S(2)}) collective-permute-start(bf16[2,2,160,512]{3,2,1,0:T(8,128)(2,1)S(1)} %get-tuple-element.19.up), channel_id=1, source_target_pairs={{0,1},{1,2},{2,3},{3,4},{4,5},{5,6},{6,7},{7,8},{8,9},{9,10},{10,1... | collective-permute-start | bytes 1966088 | tf_op jit(solution)/shard_map/ppermute | solution.py:423
  6.4 1.3 %collective-permute-start.1 = (bf16[2,2,160,512]{3,2,1,0:T(8,128)(2,1)S(1)}, bf16[2,2,160,512]{3,2,1,0:T(8,128)(2,1)S(1)}, u32[]{:S(2)}, u32[]{:S(2)}) collective-permute-start(bf16[2,2,160,512]{3,2,1,0:T(8,128)(2,1)S(1)} %get-tuple-element.20.down), channel_id=1, source_target_pairs={{1,0},{2,1},{3,2},{4,3},{5,4},{6,5},{7,6},{8,7},{9,8},{10,9},{11,1... | collective-permute-start | bytes 1966088 | tf_op jit(solution)/shard_map/ppermute | solution.py:423
  7.7 1.5 %shard_map.71 = f32[128,128]{1,0:T(8,128)} custom-call(bf16[2,2,160,512]{3,2,1,0:T(8,128)(2,1)S(1)} %get-tuple-element.19.up, bf16[2,2,160,512]{3,2,1,0:T(8,128)(2,1)S(1)} %get-tuple-element.20.down), custom_call_target="tpu_custom_call" | custom-call | tf_op jit(solution)/shard_map/pallas_call | solution.py:453
  9.2 11.6 %all-to-all-start = ((f32[128,1,128]{2,1,0:T(1,128)}), f32[128,1,128]{2,1,0:T(1,128)S(1)}, u32[]{:S(2)}, u32[]{:S(2)}) async-start(f32[128,1,128]{2,1,0:T(1,128)} %bitcast.1), calls=%async_computation | async-start | bytes 131072 | tf_op jit(solution)/shard_map/all_to_all | solution.py:462
  20.8 5.3 %shard_map.69 = (bf16[3,3,3,512,512]{4,3,2,1,0:T(8,128)(2,1)S(1)}, f32[2,2,160,512]{3,2,1,0:T(8,128)S(1)}, f32[2,2,160,512]{3,2,1,0:T(8,128)}) custom-call(bf16[2,2,160,512]{3,2,1,0:T(8,128)(2,1)S(1)} %get-tuple-element.19.up, bf16[2,2,160,512]{3,2,1,0:T(8,128)(2,1)S(1)} %get-tuple-element.20.down, bf16[3,3,3,512,512]{4,3,2,1,0:T(8,128)(2,1)} %weight.5), custom_call_target="tpu_custom_call" | custom-call | tf_op jit(solution)/shard_map/pallas_call | solution.py:466
  26.2 0.0 collective-permute-done.above
  26.2 0.0 collective-permute-done.1.below
  26.2 0.0 copy-start
  26.2 0.0 copy-start.1
  26.2 3.5 %shard_map.70 = (bf16[2,2,160,512]{3,2,1,0:T(8,128)(2,1)S(1)}, bf16[2,4,160,512]{3,2,1,0:T(8,128)(2,1)}) custom-call(bf16[2,2,160,512]{3,2,1,0:T(8,128)(2,1)S(1)} %get-tuple-element.19.up, bf16[2,2,160,512]{3,2,1,0:T(8,128)(2,1)S(1)} %get-tuple-element.20.down, bf16[2,2,160,512]{3,2,1,0:T(8,128)(2,1)S(1)} %collective-permute-done.above, ...), custom_call_target="tpu_custom_call" | custom-call | tf_op jit(solution)/shard_map/pallas_call | solution.py:481
  29.7 0.6 all-to-all-done
  30.3 2.9 %collective-permute-start.3 = (bf16[2,2,160,512]{3,2,1,0:T(8,128)(2,1)S(1)}, bf16[2,2,160,512]{3,2,1,0:T(8,128)(2,1)S(1)}, u32[]{:S(2)}, u32[]{:S(2)}) collective-permute-start(bf16[2,2,160,512]{3,2,1,0:T(8,128)(2,1)S(1)} %get-tuple-element.30.early), channel_id=1, source_target_pairs={{16,0},{17,1},{18,2},{19,3},{20,4},{21,5},{22,6},{23,7},{24,8},{25... | collective-permute-start | bytes 1966088 | tf_op jit(solution)/shard_map/ppermute | solution.py:423
  33.2 2.7 %collective-permute-start.2 = (bf16[2,4,160,512]{3,2,1,0:T(8,128)(2,1)}, bf16[2,4,160,512]{3,2,1,0:T(8,128)(2,1)S(1)}, u32[]{:S(2)}, u32[]{:S(2)}) collective-permute-start(bf16[2,4,160,512]{3,2,1,0:T(8,128)(2,1)} %get-tuple-element.27), channel_id=1, source_target_pairs={{0,16},{1,17},{2,18},{3,19},{4,20},{5,21},{6,22},{7,23},{8,24},{9,... | collective-permute-start | bytes 3932168 | tf_op jit(solution)/shard_map/ppermute | solution.py:423
  35.9 0.0 copy-done
  35.9 0.0 copy-done.1
  35.9 6.3 %shard_map.72 = (f32[2,2,160,512]{3,2,1,0:T(8,128)S(1)}, bf16[2,4,160,512]{3,2,1,0:T(8,128)(2,1)}, f32[2,8,512]{2,1,0:T(8,128)S(1)}, bf16[2,2,160,512]{3,2,1,0:T(8,128)(2,1)S(1)}) custom-call(bf16[2,2,160,512]{3,2,1,0:T(8,128)(2,1)} %cot.3, bf16[2,2,160,512]{3,2,1,0:T(8,128)(2,1)S(1)} %collective-permute-done.above, ...), custom_call_target="tpu_custom_call" | custom-call | tf_op jit(solution)/shard_map/pallas_call | solution.py:492
  42.2 0.0 collective-permute-done.3.incoming
  42.2 2.9 %shard_map.74 = (f32[2,2,160,512]{3,2,1,0:T(8,128)}, f32[128,128]{1,0:T(8,128)}) custom-call(f32[2,2,160,512]{3,2,1,0:T(8,128)S(1)} %get-tuple-element.29.own, bf16[2,2,160,512]{3,2,1,0:T(8,128)(2,1)S(1)} %collective-permute-done.3.incoming, bf16[2,2,160,512]{3,2,1,0:T(8,128)(2,1)S(1)} %get-tuple-element.31.act, f32[2,8,512]{2,1,0:T(8,128)S(1)} %get-tuple-element.28.stats, ...), custom_call_target="tpu_custom_call" | custom-call | flops 20000000000 | bytes 1000000 | tf_op jit(solution)/shard_map/pallas_call | solution.py:512
  45.2 9.2 %all-to-all-start.1 = ((f32[128,1,128]{2,1,0:T(1,128)}), f32[128,1,128]{2,1,0:T(1,128)S(1)}, u32[]{:S(2)}, u32[]{:S(2)}) async-start(f32[128,1,128]{2,1,0:T(1,128)} %bitcast.6), calls=%async_computation.1 | async-start | bytes 131072 | tf_op jit(solution)/shard_map/all_to_all | solution.py:521
  54.4 0.0 collective-permute-done.2.prior
  54.4 13.0 %shard_map.73 = bf16[2,2,160,512]{3,2,1,0:T(8,128)(2,1)} custom-call(bf16[2,4,160,512]{3,2,1,0:T(8,128)(2,1)} %get-tuple-element.26.acts, bf16[2,4,160,512]{3,2,1,0:T(8,128)(2,1)S(1)} %collective-permute-done.2.prior, bf16[3,3,3,512,512]{4,3,2,1,0:T(8,128)(2,1)} %weight.5, f32[2,8,512]{2,1,0:T(8,128)S(1)} %get-tuple-element.28.stats, f32[1,512]{1,0:T(1,128)S(1)} %bitcast.14, ...), custom_call_target="tpu_custom_call" | custom-call | tf_op jit(solution)/shard_map/pallas_call | solution.py:522
  67.5 0.0 all-to-all-done.1
  67.5 2.4 %shard_map.75 = bf16[2,2,160,512]{3,2,1,0:T(8,128)(2,1)} custom-call(f32[2,2,160,512]{3,2,1,0:T(8,128)} %get-tuple-element.34.pre_grad, bf16[2,2,160,512]{3,2,1,0:T(8,128)(2,1)} %act.5, f32[128,128]{1,0:T(8,128)S(1)} %bitcast.11, f32[2,8,512]{2,1,0:T(8,128)S(1)} %get-tuple-element.28.stats, f32[1,512]{1,0:T(1,128)S(1)} %bitcast.15), custom_call_target="tpu_custom_call" | custom-call | tf_op jit(solution)/shard_map/pallas_call | solution.py:541
Async XLA Ops:
  1.9 24.3 %collective-permute-start = (bf16[2,2,160,512]{3,2,1,0:T(8,128)(2,1)S(1)}, bf16[2,2,160,512]{3,2,1,0:T(8,128)(2,1)S(1)}, u32[]{:S(2)}, u32[]{:S(2)}) collective-permute-start(bf16[2,2,160,512]{3,2,1,0:T(8,128)(2,1)S(1)} %get-tuple-element.19.up), channel_id=1, source_target_pairs={{0,1},{1,2},{2,3},{3,4},{4,5},{5,6},{6,7},{7,8},{8,9},{9,10},{10,1... | collective-permute-start | bytes 1966088 | tf_op jit(solution)/shard_map/ppermute | solution.py:423
  6.4 19.8 %collective-permute-start.1 = (bf16[2,2,160,512]{3,2,1,0:T(8,128)(2,1)S(1)}, bf16[2,2,160,512]{3,2,1,0:T(8,128)(2,1)S(1)}, u32[]{:S(2)}, u32[]{:S(2)}) collective-permute-start(bf16[2,2,160,512]{3,2,1,0:T(8,128)(2,1)S(1)} %get-tuple-element.20.down), channel_id=1, source_target_pairs={{1,0},{2,1},{3,2},{4,3},{5,4},{6,5},{7,6},{8,7},{9,8},{10,9},{11,1... | collective-permute-start | bytes 1966088 | tf_op jit(solution)/shard_map/ppermute | solution.py:423
  9.2 21.1 %all-to-all-start = ((f32[128,1,128]{2,1,0:T(1,128)}), f32[128,1,128]{2,1,0:T(1,128)S(1)}, u32[]{:S(2)}, u32[]{:S(2)}) async-start(f32[128,1,128]{2,1,0:T(1,128)} %bitcast.1), calls=%async_computation | async-start | bytes 131072 | tf_op jit(solution)/shard_map/all_to_all | solution.py:462
  26.2 9.7 %copy-start = (f32[512]{0:T(512)S(1)}, f32[512]{0:T(512)}, u32[]{:S(2)}) copy-start(f32[512]{0:T(512)} %param.6) | copy-start | bytes 6148
  26.2 9.7 %copy-start.1 = (f32[512]{0:T(512)S(1)}, f32[512]{0:T(512)}, u32[]{:S(2)}) copy-start(f32[512]{0:T(512)} %param.7) | copy-start | bytes 6148
  30.3 11.9 %collective-permute-start.3 = (bf16[2,2,160,512]{3,2,1,0:T(8,128)(2,1)S(1)}, bf16[2,2,160,512]{3,2,1,0:T(8,128)(2,1)S(1)}, u32[]{:S(2)}, u32[]{:S(2)}) collective-permute-start(bf16[2,2,160,512]{3,2,1,0:T(8,128)(2,1)S(1)} %get-tuple-element.30.early), channel_id=1, source_target_pairs={{16,0},{17,1},{18,2},{19,3},{20,4},{21,5},{22,6},{23,7},{24,8},{25... | collective-permute-start | bytes 1966088 | tf_op jit(solution)/shard_map/ppermute | solution.py:423
  33.2 21.2 %collective-permute-start.2 = (bf16[2,4,160,512]{3,2,1,0:T(8,128)(2,1)}, bf16[2,4,160,512]{3,2,1,0:T(8,128)(2,1)S(1)}, u32[]{:S(2)}, u32[]{:S(2)}) collective-permute-start(bf16[2,4,160,512]{3,2,1,0:T(8,128)(2,1)} %get-tuple-element.27), channel_id=1, source_target_pairs={{0,16},{1,17},{2,18},{3,19},{4,20},{5,21},{6,22},{7,23},{8,24},{9,... | collective-permute-start | bytes 3932168 | tf_op jit(solution)/shard_map/ppermute | solution.py:423
  45.2 22.3 %all-to-all-start.1 = ((f32[128,1,128]{2,1,0:T(1,128)}), f32[128,1,128]{2,1,0:T(1,128)S(1)}, u32[]{:S(2)}, u32[]{:S(2)}) async-start(f32[128,1,128]{2,1,0:T(1,128)} %bitcast.6), calls=%async_computation.1 | async-start | bytes 131072 | tf_op jit(solution)/shard_map/all_to_all | solution.py:521

commit v7 on v6

--- a/solution.py
+++ b/solution.py
@@ -282,7 +282,7 @@
     return to_chans(mean, rstd, chans)
 
 
-def point_kernel(own, incoming, act, stats, gain, shift, early, pre_grad, pay, block, extra, block_sem, extra_sem):
+def point_kernel(own, incoming, act, stats, gain, shift, early, pre_grad, pay, block, extra, row_out, block_sem, extra_sem, row_sem):
     frames, rows, cols, chans = act.shape
     mean, rstd = stats[0], stats[1]
     first = lax.axis_index("ta") == 0
@@ -319,12 +319,14 @@
             sends.append(pltpu.make_async_copy(block.at[t, h], pre_grad.at[t, h], block_sem.at[t, h]))
             sends[-1].start()
     row = to_groups(gains * shift_sum, gains * gain_sum)
-    pay[...] = jnp.broadcast_to(row, pay.shape)
+    row_out[...] = jnp.broadcast_to(row, pay.shape)
+    sends.append(pltpu.make_async_copy(row_out, pay, row_sem))
+    sends[-1].start()
     for send in sends:
         send.wait()
 
 
-def conv_kernel(acts, prior, weight, stats, gain, shift, out, ext, near, far, near_taps, far_taps, acc, ext_sem, near_sem, far_sem):
+def conv_kernel(acts, prior, weight, stats, gain, shift, act, out, held, ext, near, far, near_taps, far_taps, acc, ext_sem, near_sem, far_sem, held_sem):
     frames, rows, cols, chans = out.shape
     positions = frames * rows * cols
     order = (0, 2, 1)
@@ -372,6 +374,8 @@
     for n, c in enumerate(order):
         if n == 0:
             fetches[3].wait()
+            hold = pltpu.make_async_copy(act, held, held_sem)
+            hold.start()
         if n == 1:
             fetches[4].wait()
             fetches[5].wait()
@@ -379,31 +383,24 @@
             sides(acc, 0, 2, frames * rows)
         acc[c] += jnp.dot(left, far_taps[c].reshape(6 * chans, chans), preferred_element_type=F32)
     finish(acc, out, 0, None)
-
-
-def final_kernel(pre_grad, act, gathered, stats, gain, out, block, raw, done, block_sem, raw_sem, done_sem):
+    hold.wait()
+
+
+def final_kernel(pre_grad, act, gathered, stats, gain, out, block, done, block_sem, done_sem):
     frames, rows, cols, chans = act.shape
     places = [(t, h) for t in range(frames) for h in range(rows)]
-    loads = [
-        (
-            pltpu.make_async_copy(act.at[at], raw.at[at], raw_sem.at[at]),
-            pltpu.make_async_copy(pre_grad.at[at], block.at[at], block_sem.at[at]),
-        )
-        for at in places
-    ]
-    for pair in loads:
-        for load in pair:
-            load.start()
+    loads = [pltpu.make_async_copy(pre_grad.at[at], block.at[at], block_sem.at[at]) for at in places]
+    for load in loads:
+        load.start()
     count = gathered.shape[0] * frames * rows * cols * (chans // GROUPS)
     sums = jnp.sum(gathered[...], axis=0, keepdims=True) / count
     first, second = to_chans(sums, second_part(sums), chans)
     mean, rstd = stats[0], stats[1]
     gains = jnp.broadcast_to(gain[...], (8, chans))
     sends = []
-    for at, pair in zip(places, loads):
-        for load in pair:
-            load.wait()
-        normed = (eights(raw[at].astype(F32)) - mean[None]) * rstd[None]
+    for at, load in zip(places, loads):
+        load.wait()
+        normed = (eights(act[at].astype(F32)) - mean[None]) * rstd[None]
         value = rstd[None] * (eights(block[at]) * gains[None] - first[None] - normed * second[None])
         done[at] = value.reshape(cols, chans).astype(BF16)
         sends.append(pltpu.make_async_copy(done.at[at], out.at[at], done_sem.at[at]))
@@ -512,18 +509,25 @@
     pre_grad, pay = pl.pallas_call(
         point_kernel,
         in_specs=[WHOLE] * 6 + [ANY],
-        out_specs=[HBM, WHOLE],
-        out_shape=[pltpu.HBM(shape, F32), gathered_shape],
-        scratch_shapes=[pltpu.VMEM(shape, F32), pltpu.VMEM(shape, BF16), DMA((frames, rows)), DMA],
+        out_specs=[HBM, HBM],
+        out_shape=[pltpu.HBM(shape, F32), pltpu.HBM(gathered_shape.shape, F32)],
+        scratch_shapes=[
+            pltpu.VMEM(shape, F32),
+            pltpu.VMEM(shape, BF16),
+            pltpu.VMEM(gathered_shape.shape, F32),
+            DMA((frames, rows)),
+            DMA,
+            DMA,
+        ],
         cost_estimate=pl.CostEstimate(flops=2 * 10**10, bytes_accessed=10**6, transcendentals=0),
         compiler_params=params(16),
     )(own, incoming, act_held, stats, gain, shift, early)
     gathered = lax.all_to_all(pay, BOTH, 0, 0, tiled=True)
-    output = pl.pallas_call(
+    output, act_late = pl.pallas_call(
         conv_kernel,
-        in_specs=[HBM, WHOLE, HBM, WHOLE, WHOLE, WHOLE],
-        out_specs=WHOLE,
-        out_shape=jax.ShapeDtypeStruct(shape, BF16),
+        in_specs=[HBM, WHOLE, HBM, WHOLE, WHOLE, WHOLE, HBM],
+        out_specs=[WHOLE] * 2,
+        out_shape=[jax.ShapeDtypeStruct(shape, BF16)] * 2,
         scratch_shapes=[
             pltpu.VMEM((frames + 2, rows + 2, cols, chans), BF16),
             pltpu.VMEM((frames, rows, cols, 3 * chans), BF16),
@@ -534,25 +538,24 @@
             DMA,
             DMA((3,)),
             DMA((3,)),
+            DMA,
         ],
         compiler_params=params(36),
-    )(in_hbm(acts), prior, taps, stats, gain, shift)
+    )(in_hbm(acts), prior, taps, stats, gain, shift, act)
     output, gathered = lax.optimization_barrier((output, gathered))
     input_grad = pl.pallas_call(
         final_kernel,
-        in_specs=[HBM, HBM, WHOLE, WHOLE, WHOLE],
+        in_specs=[HBM] + [WHOLE] * 4,
         out_specs=HBM,
         out_shape=pltpu.HBM(shape, BF16),
         scratch_shapes=[
             pltpu.VMEM(shape, F32),
             pltpu.VMEM(shape, BF16),
-            pltpu.VMEM(shape, BF16),
-            DMA((frames, rows)),
             DMA((frames, rows)),
             DMA((frames, rows)),
         ],
         compiler_params=params(16),
-    )(in_hbm(pre_grad), act, gathered, stats, gain)
+    )(in_hbm(pre_grad), act_late, gathered, stats, gain)
     return (output, input_grad)
 
 

time: 70.4 us -> 69.3 us (0.984)
  Pallas kernels: 36.3 us -> 35.2 us
  transfers between devices with their start and end apart: 6 -> 6, of which waited for: 1 -> 1; matrix products, arithmetic and copies ran while one was open for 0% -> 0% of each run, Pallas kernels for 47% -> 46%
where the time goes in v7:
time: 69.3 us; the launch traced here: 69 us
  Pallas kernels  35.2 us (51%)
  starting transfers between devices  32 us (46%)
  between operations  0.95 us (1%)
  waiting for transfers between devices  0.75 us (1%)
    all_to_all x2, starting transfers between devices, on_device(): gathered = lax.all_to_all(pay, BOTH, 0, 0, tiled=True)  20.8 us
    pallas_call x1, Pallas kernels, on_device(): pl.pallas_call(conv_kernel, in_specs=[HBM, WHOLE, HBM, WHOLE, WHOLE, WHOL...  13 us
    ppermute x4, starting transfers between devices, moved(): return lax.ppermute(value, BOTH, pairs)  11.3 us
    pallas_call x1, Pallas kernels, on_device(): pl.pallas_call(own_kernel, in_specs=[HBM, WHOLE, WHOLE, HBM, HBM, HBM, WH...  6.27 us
    pallas_call x1, Pallas kernels, on_device(): pl.pallas_call(centre_kernel, in_specs=[WHOLE, WHOLE, HBM], out_specs=[WH...  5.31 us
    pallas_call x1, Pallas kernels, on_device(): pl.pallas_call(early_kernel, in_specs=[WHOLE] * 6, out_specs=[WHOLE, HBM]...  3.42 us
    pallas_call x1, Pallas kernels, on_device(): pl.pallas_call(point_kernel, in_specs=[WHOLE] * 6 + [ANY], out_specs=[HBM...  2.26 us
    pallas_call x1, Pallas kernels, on_device(): pl.pallas_call(final_kernel, in_specs=[HBM] + [WHOLE] * 4, out_specs=HBM,...  2.1 us
  transfers between devices with their start and end apart: 6, of which 1 were waited for; matrix products, arithmetic and copies ran while one was open for 0% of the time, Pallas kernels for 46%

profile of v7, /device:TPU:1, one launch (start us, length us, event | category | flops | bytes accessed | tf_op | source)
XLA Modules:
  0.0 69.0 jit_solution(180342199806885457)
XLA Ops:
  0.6 1.3 %shard_map.68 = (bf16[2,2,160,512]{3,2,1,0:T(8,128)(2,1)S(1)}, bf16[2,2,160,512]{3,2,1,0:T(8,128)(2,1)S(1)}) custom-call(bf16[2,2,160,512]{3,2,1,0:T(8,128)(2,1)} %act.5, bf16[2,2,160,512]{3,2,1,0:T(8,128)(2,1)} %cot.3), custom_call_target="tpu_custom_call" | custom-call | tf_op jit(solution)/shard_map/pallas_call | solution.py:442
  1.9 4.4 %collective-permute-start = (bf16[2,2,160,512]{3,2,1,0:T(8,128)(2,1)S(1)}, bf16[2,2,160,512]{3,2,1,0:T(8,128)(2,1)S(1)}, u32[]{:S(2)}, u32[]{:S(2)}) collective-permute-start(bf16[2,2,160,512]{3,2,1,0:T(8,128)(2,1)S(1)} %get-tuple-element.21.up), channel_id=1, source_target_pairs={{0,1},{1,2},{2,3},{3,4},{4,5},{5,6},{6,7},{7,8},{8,9},{9,10},{10,1... | collective-permute-start | bytes 1966088 | tf_op jit(solution)/shard_map/ppermute | solution.py:420
  6.4 1.3 %collective-permute-start.1 = (bf16[2,2,160,512]{3,2,1,0:T(8,128)(2,1)S(1)}, bf16[2,2,160,512]{3,2,1,0:T(8,128)(2,1)S(1)}, u32[]{:S(2)}, u32[]{:S(2)}) collective-permute-start(bf16[2,2,160,512]{3,2,1,0:T(8,128)(2,1)S(1)} %get-tuple-element.22.down), channel_id=1, source_target_pairs={{1,0},{2,1},{3,2},{4,3},{5,4},{6,5},{7,6},{8,7},{9,8},{10,9},{11,1... | collective-permute-start | bytes 1966088 | tf_op jit(solution)/shard_map/ppermute | solution.py:420
  7.7 1.5 %shard_map.71 = f32[128,128]{1,0:T(8,128)} custom-call(bf16[2,2,160,512]{3,2,1,0:T(8,128)(2,1)S(1)} %get-tuple-element.21.up, bf16[2,2,160,512]{3,2,1,0:T(8,128)(2,1)S(1)} %get-tuple-element.22.down), custom_call_target="tpu_custom_call" | custom-call | tf_op jit(solution)/shard_map/pallas_call | solution.py:450
  9.2 11.6 %all-to-all-start = ((f32[128,1,128]{2,1,0:T(1,128)}), f32[128,1,128]{2,1,0:T(1,128)S(1)}, u32[]{:S(2)}, u32[]{:S(2)}) async-start(f32[128,1,128]{2,1,0:T(1,128)} %bitcast.1), calls=%async_computation | async-start | bytes 131072 | tf_op jit(solution)/shard_map/all_to_all | solution.py:459
  20.8 5.3 %shard_map.69 = (bf16[3,3,3,512,512]{4,3,2,1,0:T(8,128)(2,1)S(1)}, f32[2,2,160,512]{3,2,1,0:T(8,128)S(1)}, f32[2,2,160,512]{3,2,1,0:T(8,128)}) custom-call(bf16[2,2,160,512]{3,2,1,0:T(8,128)(2,1)S(1)} %get-tuple-element.21.up, bf16[2,2,160,512]{3,2,1,0:T(8,128)(2,1)S(1)} %get-tuple-element.22.down, bf16[3,3,3,512,512]{4,3,2,1,0:T(8,128)(2,1)} %weight.5), custom_call_target="tpu_custom_call" | custom-call | tf_op jit(solution)/shard_map/pallas_call | solution.py:463
  26.2 0.0 collective-permute-done.above
  26.2 0.0 collective-permute-done.1.below
  26.2 0.0 copy-start
  26.2 0.0 copy-start.1
  26.2 3.4 %shard_map.70 = (bf16[2,2,160,512]{3,2,1,0:T(8,128)(2,1)S(1)}, bf16[2,4,160,512]{3,2,1,0:T(8,128)(2,1)}) custom-call(bf16[2,2,160,512]{3,2,1,0:T(8,128)(2,1)S(1)} %get-tuple-element.21.up, bf16[2,2,160,512]{3,2,1,0:T(8,128)(2,1)S(1)} %get-tuple-element.22.down, bf16[2,2,160,512]{3,2,1,0:T(8,128)(2,1)S(1)} %collective-permute-done.above, ...), custom_call_target="tpu_custom_call" | custom-call | tf_op jit(solution)/shard_map/pallas_call | solution.py:478
  29.6 0.7 %all-to-all-done = f32[128,1,128]{2,1,0:T(1,128)S(1)} async-done(((f32[128,1,128]{2,1,0:T(1,128)}), f32[128,1,128]{2,1,0:T(1,128)S(1)}, u32[]{:S(2)}, u32[]{:S(2)}) %all-to-all-start) | async-done | bytes 65568 | tf_op jit(solution)/shard_map/all_to_all | solution.py:459
  30.3 2.9 %collective-permute-start.3 = (bf16[2,2,160,512]{3,2,1,0:T(8,128)(2,1)S(1)}, bf16[2,2,160,512]{3,2,1,0:T(8,128)(2,1)S(1)}, u32[]{:S(2)}, u32[]{:S(2)}) collective-permute-start(bf16[2,2,160,512]{3,2,1,0:T(8,128)(2,1)S(1)} %get-tuple-element.33.early), channel_id=1, source_target_pairs={{16,0},{17,1},{18,2},{19,3},{20,4},{21,5},{22,6},{23,7},{24,8},{25... | collective-permute-start | bytes 1966088 | tf_op jit(solution)/shard_map/ppermute | solution.py:420
  33.2 2.7 %collective-permute-start.2 = (bf16[2,4,160,512]{3,2,1,0:T(8,128)(2,1)}, bf16[2,4,160,512]{3,2,1,0:T(8,128)(2,1)S(1)}, u32[]{:S(2)}, u32[]{:S(2)}) collective-permute-start(bf16[2,4,160,512]{3,2,1,0:T(8,128)(2,1)} %get-tuple-element.29), channel_id=1, source_target_pairs={{0,16},{1,17},{2,18},{3,19},{4,20},{5,21},{6,22},{7,23},{8,24},{9,... | collective-permute-start | bytes 3932168 | tf_op jit(solution)/shard_map/ppermute | solution.py:420
  35.9 0.0 copy-done
  35.9 0.0 copy-done.1
  35.9 6.3 %shard_map.72 = (f32[2,2,160,512]{3,2,1,0:T(8,128)S(1)}, bf16[2,4,160,512]{3,2,1,0:T(8,128)(2,1)}, f32[2,8,512]{2,1,0:T(8,128)S(1)}, bf16[2,2,160,512]{3,2,1,0:T(8,128)(2,1)S(1)}) custom-call(bf16[2,2,160,512]{3,2,1,0:T(8,128)(2,1)} %cot.3, bf16[2,2,160,512]{3,2,1,0:T(8,128)(2,1)S(1)} %collective-permute-done.above, ...), custom_call_target="tpu_custom_call" | custom-call | tf_op jit(solution)/shard_map/pallas_call | solution.py:489
  42.2 0.0 collective-permute-done.3.incoming
  42.2 2.3 %shard_map.74 = (f32[2,2,160,512]{3,2,1,0:T(8,128)}, f32[128,128]{1,0:T(8,128)}) custom-call(f32[2,2,160,512]{3,2,1,0:T(8,128)S(1)} %get-tuple-element.32.own, bf16[2,2,160,512]{3,2,1,0:T(8,128)(2,1)S(1)} %collective-permute-done.3.incoming, bf16[2,2,160,512]{3,2,1,0:T(8,128)(2,1)S(1)} %get-tuple-element.34.act, f32[2,8,512]{2,1,0:T(8,128)S(1)} %get-tuple-element.30.stats, ...), custom_call_target="tpu_custom_call" | custom-call | flops 20000000000 | bytes 1000000 | tf_op jit(solution)/shard_map/pallas_call | solution.py:509
  44.5 9.1 %all-to-all-start.1 = ((f32[128,1,128]{2,1,0:T(1,128)}), f32[128,1,128]{2,1,0:T(1,128)S(1)}, u32[]{:S(2)}, u32[]{:S(2)}) async-start(f32[128,1,128]{2,1,0:T(1,128)} %bitcast.19), calls=%async_computation.1 | async-start | bytes 131072 | tf_op jit(solution)/shard_map/all_to_all | solution.py:525
  53.7 0.0 collective-permute-done.2.prior
  53.7 13.0 %shard_map.73 = (bf16[2,2,160,512]{3,2,1,0:T(8,128)(2,1)}, bf16[2,2,160,512]{3,2,1,0:T(8,128)(2,1)S(1)}) custom-call(bf16[2,4,160,512]{3,2,1,0:T(8,128)(2,1)} %get-tuple-element.28.acts, bf16[2,4,160,512]{3,2,1,0:T(8,128)(2,1)S(1)} %collective-permute-done.2.prior, bf16[3,3,3,512,512]{4,3,2,1,0:T(8,128)(2,1)} %weight.5, ...), custom_call_target="tpu_custom_call" | custom-call | tf_op jit(solution)/shard_map/pallas_call | solution.py:526
  66.7 0.0 all-to-all-done.1
  66.7 2.1 %shard_map.75 = bf16[2,2,160,512]{3,2,1,0:T(8,128)(2,1)} custom-call(f32[2,2,160,512]{3,2,1,0:T(8,128)} %get-tuple-element.37.pre_grad, bf16[2,2,160,512]{3,2,1,0:T(8,128)(2,1)S(1)} %get-tuple-element.38.act, f32[128,128]{1,0:T(8,128)S(1)} %bitcast.11, f32[2,8,512]{2,1,0:T(8,128)S(1)} %get-tuple-element.30.stats, f32[1,512]{1,0:T(1,128)S(1)} %bitcast.15), custom_call_target="tpu_custom_call" | custom-call | tf_op jit(solution)/shard_map/pallas_call | solution.py:546
Async XLA Ops:
  1.9 24.2 %collective-permute-start = (bf16[2,2,160,512]{3,2,1,0:T(8,128)(2,1)S(1)}, bf16[2,2,160,512]{3,2,1,0:T(8,128)(2,1)S(1)}, u32[]{:S(2)}, u32[]{:S(2)}) collective-permute-start(bf16[2,2,160,512]{3,2,1,0:T(8,128)(2,1)S(1)} %get-tuple-element.21.up), channel_id=1, source_target_pairs={{0,1},{1,2},{2,3},{3,4},{4,5},{5,6},{6,7},{7,8},{8,9},{9,10},{10,1... | collective-permute-start | bytes 1966088 | tf_op jit(solution)/shard_map/ppermute | solution.py:420
  6.4 19.8 %collective-permute-start.1 = (bf16[2,2,160,512]{3,2,1,0:T(8,128)(2,1)S(1)}, bf16[2,2,160,512]{3,2,1,0:T(8,128)(2,1)S(1)}, u32[]{:S(2)}, u32[]{:S(2)}) collective-permute-start(bf16[2,2,160,512]{3,2,1,0:T(8,128)(2,1)S(1)} %get-tuple-element.22.down), channel_id=1, source_target_pairs={{1,0},{2,1},{3,2},{4,3},{5,4},{6,5},{7,6},{8,7},{9,8},{10,9},{11,1... | collective-permute-start | bytes 1966088 | tf_op jit(solution)/shard_map/ppermute | solution.py:420
  9.2 21.1 %all-to-all-start = ((f32[128,1,128]{2,1,0:T(1,128)}), f32[128,1,128]{2,1,0:T(1,128)S(1)}, u32[]{:S(2)}, u32[]{:S(2)}) async-start(f32[128,1,128]{2,1,0:T(1,128)} %bitcast.1), calls=%async_computation | async-start | bytes 131072 | tf_op jit(solution)/shard_map/all_to_all | solution.py:459
  26.2 9.7 %copy-start = (f32[512]{0:T(512)S(1)}, f32[512]{0:T(512)}, u32[]{:S(2)}) copy-start(f32[512]{0:T(512)} %param.6) | copy-start | bytes 6148
  26.2 9.7 %copy-start.1 = (f32[512]{0:T(512)S(1)}, f32[512]{0:T(512)}, u32[]{:S(2)}) copy-start(f32[512]{0:T(512)} %param.7) | copy-start | bytes 6148
  30.3 11.9 %collective-permute-start.3 = (bf16[2,2,160,512]{3,2,1,0:T(8,128)(2,1)S(1)}, bf16[2,2,160,512]{3,2,1,0:T(8,128)(2,1)S(1)}, u32[]{:S(2)}, u32[]{:S(2)}) collective-permute-start(bf16[2,2,160,512]{3,2,1,0:T(8,128)(2,1)S(1)} %get-tuple-element.33.early), channel_id=1, source_target_pairs={{16,0},{17,1},{18,2},{19,3},{20,4},{21,5},{22,6},{23,7},{24,8},{25... | collective-permute-start | bytes 1966088 | tf_op jit(solution)/shard_map/ppermute | solution.py:420
  33.2 20.4 %collective-permute-start.2 = (bf16[2,4,160,512]{3,2,1,0:T(8,128)(2,1)}, bf16[2,4,160,512]{3,2,1,0:T(8,128)(2,1)S(1)}, u32[]{:S(2)}, u32[]{:S(2)}) collective-permute-start(bf16[2,4,160,512]{3,2,1,0:T(8,128)(2,1)} %get-tuple-element.29), channel_id=1, source_target_pairs={{0,16},{1,17},{2,18},{3,19},{4,20},{5,21},{6,22},{7,23},{8,24},{9,... | collective-permute-start | bytes 3932168 | tf_op jit(solution)/shard_map/ppermute | solution.py:420
  44.5 22.2 %all-to-all-start.1 = ((f32[128,1,128]{2,1,0:T(1,128)}), f32[128,1,128]{2,1,0:T(1,128)S(1)}, u32[]{:S(2)}, u32[]{:S(2)}) async-start(f32[128,1,128]{2,1,0:T(1,128)} %bitcast.19), calls=%async_computation.1 | async-start | bytes 131072 | tf_op jit(solution)/shard_map/all_to_all | solution.py:525

commit v8 on v7

--- a/solution.py
+++ b/solution.py
@@ -218,6 +218,8 @@
         activate(above[0, t], t, 0)
         activate(below[0, t], t, rows + 1)
     load_act.wait()
+    for fetch in fetches[1]:
+        fetch.start()
     sends = [pltpu.make_async_copy(acts.at[t], longer.at[t], acts_sem.at[t]) for t in range(frames)]
     for load in load_cot:
         load.wait()
@@ -227,8 +229,6 @@
         for fetch in fetches[n]:
             fetch.wait()
         if n == 0:
-            for fetch in fetches[1]:
-                fetch.start()
             load_more.start()
         else:
             for send in sends:

time: 69.3 us -> 69.3 us (level)
  no operation moved by 1% of the time
where the time goes in v8:
time: 69.3 us; the launch traced here: 69 us
  Pallas kernels  35.2 us (51%)
  starting transfers between devices  32 us (46%)
  between operations  0.95 us (1%)
  waiting for transfers between devices  0.75 us (1%)
    all_to_all x2, starting transfers between devices, on_device(): gathered = lax.all_to_all(pay, BOTH, 0, 0, tiled=True)  20.8 us
    pallas_call x1, Pallas kernels, on_device(): pl.pallas_call(conv_kernel, in_specs=[HBM, WHOLE, HBM, WHOLE, WHOLE, WHOL...  13 us
    ppermute x4, starting transfers between devices, moved(): return lax.ppermute(value, BOTH, pairs)  11.3 us
    pallas_call x1, Pallas kernels, on_device(): pl.pallas_call(own_kernel, in_specs=[HBM, WHOLE, WHOLE, HBM, HBM, HBM, WH...  6.27 us
    pallas_call x1, Pallas kernels, on_device(): pl.pallas_call(centre_kernel, in_specs=[WHOLE, WHOLE, HBM], out_specs=[WH...  5.31 us
    pallas_call x1, Pallas kernels, on_device(): pl.pallas_call(early_kernel, in_specs=[WHOLE] * 6, out_specs=[WHOLE, HBM]...  3.42 us
    pallas_call x1, Pallas kernels, on_device(): pl.pallas_call(point_kernel, in_specs=[WHOLE] * 6 + [ANY], out_specs=[HBM...  2.26 us
    pallas_call x1, Pallas kernels, on_device(): pl.pallas_call(final_kernel, in_specs=[HBM] + [WHOLE] * 4, out_specs=HBM,...  2.1 us
  transfers between devices with their start and end apart: 6, of which 1 were waited for; matrix products, arithmetic and copies ran while one was open for 0% of the time, Pallas kernels for 46%

profile of v8, /device:TPU:1, one launch (start us, length us, event | category | flops | bytes accessed | tf_op | source)
XLA Modules:
  0.0 69.0 jit_solution(6016775544630863905)
XLA Ops:
  0.6 1.3 %shard_map.68 = (bf16[2,2,160,512]{3,2,1,0:T(8,128)(2,1)S(1)}, bf16[2,2,160,512]{3,2,1,0:T(8,128)(2,1)S(1)}) custom-call(bf16[2,2,160,512]{3,2,1,0:T(8,128)(2,1)} %act.5, bf16[2,2,160,512]{3,2,1,0:T(8,128)(2,1)} %cot.3), custom_call_target="tpu_custom_call" | custom-call | tf_op jit(solution)/shard_map/pallas_call | solution.py:442
  1.9 4.4 %collective-permute-start = (bf16[2,2,160,512]{3,2,1,0:T(8,128)(2,1)S(1)}, bf16[2,2,160,512]{3,2,1,0:T(8,128)(2,1)S(1)}, u32[]{:S(2)}, u32[]{:S(2)}) collective-permute-start(bf16[2,2,160,512]{3,2,1,0:T(8,128)(2,1)S(1)} %get-tuple-element.21.up), channel_id=1, source_target_pairs={{0,1},{1,2},{2,3},{3,4},{4,5},{5,6},{6,7},{7,8},{8,9},{9,10},{10,1... | collective-permute-start | bytes 1966088 | tf_op jit(solution)/shard_map/ppermute | solution.py:420
  6.4 1.3 %collective-permute-start.1 = (bf16[2,2,160,512]{3,2,1,0:T(8,128)(2,1)S(1)}, bf16[2,2,160,512]{3,2,1,0:T(8,128)(2,1)S(1)}, u32[]{:S(2)}, u32[]{:S(2)}) collective-permute-start(bf16[2,2,160,512]{3,2,1,0:T(8,128)(2,1)S(1)} %get-tuple-element.22.down), channel_id=1, source_target_pairs={{1,0},{2,1},{3,2},{4,3},{5,4},{6,5},{7,6},{8,7},{9,8},{10,9},{11,1... | collective-permute-start | bytes 1966088 | tf_op jit(solution)/shard_map/ppermute | solution.py:420
  7.7 1.5 %shard_map.71 = f32[128,128]{1,0:T(8,128)} custom-call(bf16[2,2,160,512]{3,2,1,0:T(8,128)(2,1)S(1)} %get-tuple-element.21.up, bf16[2,2,160,512]{3,2,1,0:T(8,128)(2,1)S(1)} %get-tuple-element.22.down), custom_call_target="tpu_custom_call" | custom-call | tf_op jit(solution)/shard_map/pallas_call | solution.py:450
  9.2 11.6 %all-to-all-start = ((f32[128,1,128]{2,1,0:T(1,128)}), f32[128,1,128]{2,1,0:T(1,128)S(1)}, u32[]{:S(2)}, u32[]{:S(2)}) async-start(f32[128,1,128]{2,1,0:T(1,128)} %bitcast.1), calls=%async_computation | async-start | bytes 131072 | tf_op jit(solution)/shard_map/all_to_all | solution.py:459
  20.8 5.3 %shard_map.69 = (bf16[3,3,3,512,512]{4,3,2,1,0:T(8,128)(2,1)S(1)}, f32[2,2,160,512]{3,2,1,0:T(8,128)S(1)}, f32[2,2,160,512]{3,2,1,0:T(8,128)}) custom-call(bf16[2,2,160,512]{3,2,1,0:T(8,128)(2,1)S(1)} %get-tuple-element.21.up, bf16[2,2,160,512]{3,2,1,0:T(8,128)(2,1)S(1)} %get-tuple-element.22.down, bf16[3,3,3,512,512]{4,3,2,1,0:T(8,128)(2,1)} %weight.5), custom_call_target="tpu_custom_call" | custom-call | tf_op jit(solution)/shard_map/pallas_call | solution.py:463
  26.2 0.0 collective-permute-done.above
  26.2 0.0 collective-permute-done.1.below
  26.2 0.0 copy-start
  26.2 0.0 copy-start.1
  26.2 3.4 %shard_map.70 = (bf16[2,2,160,512]{3,2,1,0:T(8,128)(2,1)S(1)}, bf16[2,4,160,512]{3,2,1,0:T(8,128)(2,1)}) custom-call(bf16[2,2,160,512]{3,2,1,0:T(8,128)(2,1)S(1)} %get-tuple-element.21.up, bf16[2,2,160,512]{3,2,1,0:T(8,128)(2,1)S(1)} %get-tuple-element.22.down, bf16[2,2,160,512]{3,2,1,0:T(8,128)(2,1)S(1)} %collective-permute-done.above, ...), custom_call_target="tpu_custom_call" | custom-call | tf_op jit(solution)/shard_map/pallas_call | solution.py:478
  29.6 0.7 %all-to-all-done = f32[128,1,128]{2,1,0:T(1,128)S(1)} async-done(((f32[128,1,128]{2,1,0:T(1,128)}), f32[128,1,128]{2,1,0:T(1,128)S(1)}, u32[]{:S(2)}, u32[]{:S(2)}) %all-to-all-start) | async-done | bytes 65568 | tf_op jit(solution)/shard_map/all_to_all | solution.py:459
  30.3 2.9 %collective-permute-start.3 = (bf16[2,2,160,512]{3,2,1,0:T(8,128)(2,1)S(1)}, bf16[2,2,160,512]{3,2,1,0:T(8,128)(2,1)S(1)}, u32[]{:S(2)}, u32[]{:S(2)}) collective-permute-start(bf16[2,2,160,512]{3,2,1,0:T(8,128)(2,1)S(1)} %get-tuple-element.33.early), channel_id=1, source_target_pairs={{16,0},{17,1},{18,2},{19,3},{20,4},{21,5},{22,6},{23,7},{24,8},{25... | collective-permute-start | bytes 1966088 | tf_op jit(solution)/shard_map/ppermute | solution.py:420
  33.2 2.7 %collective-permute-start.2 = (bf16[2,4,160,512]{3,2,1,0:T(8,128)(2,1)}, bf16[2,4,160,512]{3,2,1,0:T(8,128)(2,1)S(1)}, u32[]{:S(2)}, u32[]{:S(2)}) collective-permute-start(bf16[2,4,160,512]{3,2,1,0:T(8,128)(2,1)} %get-tuple-element.29), channel_id=1, source_target_pairs={{0,16},{1,17},{2,18},{3,19},{4,20},{5,21},{6,22},{7,23},{8,24},{9,... | collective-permute-start | bytes 3932168 | tf_op jit(solution)/shard_map/ppermute | solution.py:420
  35.9 0.0 copy-done
  35.9 0.0 copy-done.1
  35.9 6.3 %shard_map.72 = (f32[2,2,160,512]{3,2,1,0:T(8,128)S(1)}, bf16[2,4,160,512]{3,2,1,0:T(8,128)(2,1)}, f32[2,8,512]{2,1,0:T(8,128)S(1)}, bf16[2,2,160,512]{3,2,1,0:T(8,128)(2,1)S(1)}) custom-call(bf16[2,2,160,512]{3,2,1,0:T(8,128)(2,1)} %cot.3, bf16[2,2,160,512]{3,2,1,0:T(8,128)(2,1)S(1)} %collective-permute-done.above, ...), custom_call_target="tpu_custom_call" | custom-call | tf_op jit(solution)/shard_map/pallas_call | solution.py:489
  42.2 0.0 collective-permute-done.3.incoming
  42.2 2.3 %shard_map.74 = (f32[2,2,160,512]{3,2,1,0:T(8,128)}, f32[128,128]{1,0:T(8,128)}) custom-call(f32[2,2,160,512]{3,2,1,0:T(8,128)S(1)} %get-tuple-element.32.own, bf16[2,2,160,512]{3,2,1,0:T(8,128)(2,1)S(1)} %collective-permute-done.3.incoming, bf16[2,2,160,512]{3,2,1,0:T(8,128)(2,1)S(1)} %get-tuple-element.34.act, f32[2,8,512]{2,1,0:T(8,128)S(1)} %get-tuple-element.30.stats, ...), custom_call_target="tpu_custom_call" | custom-call | flops 20000000000 | bytes 1000000 | tf_op jit(solution)/shard_map/pallas_call | solution.py:509
  44.5 9.1 %all-to-all-start.1 = ((f32[128,1,128]{2,1,0:T(1,128)}), f32[128,1,128]{2,1,0:T(1,128)S(1)}, u32[]{:S(2)}, u32[]{:S(2)}) async-start(f32[128,1,128]{2,1,0:T(1,128)} %bitcast.19), calls=%async_computation.1 | async-start | bytes 131072 | tf_op jit(solution)/shard_map/all_to_all | solution.py:525
  53.7 0.0 collective-permute-done.2.prior
  53.7 13.0 %shard_map.73 = (bf16[2,2,160,512]{3,2,1,0:T(8,128)(2,1)}, bf16[2,2,160,512]{3,2,1,0:T(8,128)(2,1)S(1)}) custom-call(bf16[2,4,160,512]{3,2,1,0:T(8,128)(2,1)} %get-tuple-element.28.acts, bf16[2,4,160,512]{3,2,1,0:T(8,128)(2,1)S(1)} %collective-permute-done.2.prior, bf16[3,3,3,512,512]{4,3,2,1,0:T(8,128)(2,1)} %weight.5, ...), custom_call_target="tpu_custom_call" | custom-call | tf_op jit(solution)/shard_map/pallas_call | solution.py:526
  66.7 0.0 all-to-all-done.1
  66.7 2.1 %shard_map.75 = bf16[2,2,160,512]{3,2,1,0:T(8,128)(2,1)} custom-call(f32[2,2,160,512]{3,2,1,0:T(8,128)} %get-tuple-element.37.pre_grad, bf16[2,2,160,512]{3,2,1,0:T(8,128)(2,1)S(1)} %get-tuple-element.38.act, f32[128,128]{1,0:T(8,128)S(1)} %bitcast.11, f32[2,8,512]{2,1,0:T(8,128)S(1)} %get-tuple-element.30.stats, f32[1,512]{1,0:T(1,128)S(1)} %bitcast.15), custom_call_target="tpu_custom_call" | custom-call | tf_op jit(solution)/shard_map/pallas_call | solution.py:546
Async XLA Ops:
  1.9 24.2 %collective-permute-start = (bf16[2,2,160,512]{3,2,1,0:T(8,128)(2,1)S(1)}, bf16[2,2,160,512]{3,2,1,0:T(8,128)(2,1)S(1)}, u32[]{:S(2)}, u32[]{:S(2)}) collective-permute-start(bf16[2,2,160,512]{3,2,1,0:T(8,128)(2,1)S(1)} %get-tuple-element.21.up), channel_id=1, source_target_pairs={{0,1},{1,2},{2,3},{3,4},{4,5},{5,6},{6,7},{7,8},{8,9},{9,10},{10,1... | collective-permute-start | bytes 1966088 | tf_op jit(solution)/shard_map/ppermute | solution.py:420
  6.4 19.8 %collective-permute-start.1 = (bf16[2,2,160,512]{3,2,1,0:T(8,128)(2,1)S(1)}, bf16[2,2,160,512]{3,2,1,0:T(8,128)(2,1)S(1)}, u32[]{:S(2)}, u32[]{:S(2)}) collective-permute-start(bf16[2,2,160,512]{3,2,1,0:T(8,128)(2,1)S(1)} %get-tuple-element.22.down), channel_id=1, source_target_pairs={{1,0},{2,1},{3,2},{4,3},{5,4},{6,5},{7,6},{8,7},{9,8},{10,9},{11,1... | collective-permute-start | bytes 1966088 | tf_op jit(solution)/shard_map/ppermute | solution.py:420
  9.2 21.1 %all-to-all-start = ((f32[128,1,128]{2,1,0:T(1,128)}), f32[128,1,128]{2,1,0:T(1,128)S(1)}, u32[]{:S(2)}, u32[]{:S(2)}) async-start(f32[128,1,128]{2,1,0:T(1,128)} %bitcast.1), calls=%async_computation | async-start | bytes 131072 | tf_op jit(solution)/shard_map/all_to_all | solution.py:459
  26.2 9.7 %copy-start = (f32[512]{0:T(512)S(1)}, f32[512]{0:T(512)}, u32[]{:S(2)}) copy-start(f32[512]{0:T(512)} %param.6) | copy-start | bytes 6148
  26.2 9.7 %copy-start.1 = (f32[512]{0:T(512)S(1)}, f32[512]{0:T(512)}, u32[]{:S(2)}) copy-start(f32[512]{0:T(512)} %param.7) | copy-start | bytes 6148
  30.3 11.9 %collective-permute-start.3 = (bf16[2,2,160,512]{3,2,1,0:T(8,128)(2,1)S(1)}, bf16[2,2,160,512]{3,2,1,0:T(8,128)(2,1)S(1)}, u32[]{:S(2)}, u32[]{:S(2)}) collective-permute-start(bf16[2,2,160,512]{3,2,1,0:T(8,128)(2,1)S(1)} %get-tuple-element.33.early), channel_id=1, source_target_pairs={{16,0},{17,1},{18,2},{19,3},{20,4},{21,5},{22,6},{23,7},{24,8},{25... | collective-permute-start | bytes 1966088 | tf_op jit(solution)/shard_map/ppermute | solution.py:420
  33.2 20.4 %collective-permute-start.2 = (bf16[2,4,160,512]{3,2,1,0:T(8,128)(2,1)}, bf16[2,4,160,512]{3,2,1,0:T(8,128)(2,1)S(1)}, u32[]{:S(2)}, u32[]{:S(2)}) collective-permute-start(bf16[2,4,160,512]{3,2,1,0:T(8,128)(2,1)} %get-tuple-element.29), channel_id=1, source_target_pairs={{0,16},{1,17},{2,18},{3,19},{4,20},{5,21},{6,22},{7,23},{8,24},{9,... | collective-permute-start | bytes 3932168 | tf_op jit(solution)/shard_map/ppermute | solution.py:420
  44.5 22.2 %all-to-all-start.1 = ((f32[128,1,128]{2,1,0:T(1,128)}), f32[128,1,128]{2,1,0:T(1,128)S(1)}, u32[]{:S(2)}, u32[]{:S(2)}) async-start(f32[128,1,128]{2,1,0:T(1,128)} %bitcast.19), calls=%async_computation.1 | async-start | bytes 131072 | tf_op jit(solution)/shard_map/all_to_all | solution.py:525
